TPU v7x, 32 devices: a whole 2x2x4 slice. The times are simulated.
32 devices in a mesh: fsdp: 4 (over z), context: 2 (over y), tensor: 4 (over x, core).
Axes of the slice: x: 2, y: 2, z: 4, core: 2. Of those that a mesh axis runs over, the one named last changes fastest.
Arguments:
- patches: bfloat16 [10240, 768], P(('fsdp', 'context')), may hold values from -6 to 6
- out_grad: bfloat16 [10240, 768], P(('fsdp', 'context')), may hold values from -6 to 6
- block_order: int32 [4, 20], P('fsdp'), may hold values from 0 to 19, as said below
- first_gain: float32 [768], replicated, may hold values from 0.25 to 1.75
- first_shift: float32 [768], replicated, may hold values from -2 to 2
- attn_proj: bfloat16 [3, 768, 768], P(None, 'fsdp', 'tensor'), may hold values from -0.21875 to 0.21875
- attn_bias: float32 [2, 768], P(None, 'tensor'), may hold values from -3 to 3
- out_proj: bfloat16 [768, 768], P('tensor', 'fsdp'), may hold values from -0.875 to 0.875
- out_bias: float32 [768], replicated, may hold values from -2 to 2
- second_gain: float32 [768], replicated, may hold values from 0.25 to 1.75
- second_shift: float32 [768], replicated, may hold values from -2 to 2
- up_proj: bfloat16 [768, 3072], P('fsdp', 'tensor'), may hold values from -0.21875 to 0.21875
- up_bias: float32 [3072], P('tensor'), may hold values from -3 to 3
- down_proj: bfloat16 [3072, 768], P('tensor', 'fsdp'), may hold values from -0.109375 to 0.109375
- down_bias: float32 [768], replicated, may hold values from -2 to 2
Outputs:
- result: bfloat16 [10240, 768], P(('fsdp', 'context'))
- patch_grad: float32 [10240, 768], P(('fsdp', 'context'))
- grad_first_gain: float32 [768], replicated
- grad_first_shift: float32 [768], replicated
- grad_attn_proj: float32 [3, 768, 768], P(None, 'fsdp', 'tensor')
- grad_attn_bias: float32 [2, 768], P(None, 'tensor')
- grad_out_proj: float32 [768, 768], P('tensor', 'fsdp')
- grad_out_bias: float32 [768], replicated
- grad_second_gain: float32 [768], replicated
- grad_second_shift: float32 [768], replicated
- grad_up_proj: float32 [768, 3072], P('fsdp', 'tensor')
- grad_up_bias: float32 [3072], P('tensor')
- grad_down_proj: float32 [3072, 768], P('tensor', 'fsdp')
- grad_down_bias: float32 [768], replicated
Inputs may be any that keep to these rules, and one draw needn't show every extreme that they name: `block_order`: each row lists every block number of its group once. In every group, each device of context holds 20 // 2 blocks of every tree, or one more.
All inputs are finite; a program needn't handle non-finite values.
Results may differ from a plain program's by a relative error of at most 0.0098.
Values may be sent and summed in bfloat16 or wider, within the bound.
A program may use at most 128 MiB of HBM per device.

v0:
```python
from functools import partial

import jax
import jax.numpy as jnp
from jax import lax
from jax.sharding import PartitionSpec as P

HEAD_DIM = 64
BLOCK = 128
TRUNK_BLK = 8
BRANCHES = 4
LEAVES = 2
TREE_BLK = 20


epsilon = 1e-05
far_below = -1e30


def layer_norm(values, norm_gain, norm_shift):
    center = values - jnp.mean(values, axis=1, keepdims=True)
    inverse = lax.rsqrt(jnp.mean(center * center, axis=1, keepdims=True) + epsilon)
    normed = center * inverse
    return (normed * norm_gain + norm_shift, normed, inverse)


def norm_back(gradient, normed, inverse, norm_gain):
    scaled = gradient * norm_gain
    return inverse * (
        scaled
        - jnp.mean(scaled, axis=1, keepdims=True)
        - normed * jnp.mean(scaled * normed, axis=1, keepdims=True)
    )


def slot_labels(order_row):
    position = order_row % TREE_BLK
    return (order_row // TREE_BLK, jnp.where(position < TRUNK_BLK, 0, position - TRUNK_BLK + 1))


def spread_rows(values):
    return jnp.broadcast_to(values[:, None], (values.shape[0], BLOCK)).reshape(-1)


def row_labels(labels, first_slot, slot_count):
    return tuple(
        (
            spread_rows(lax.dynamic_slice_in_dim(label_table, first_slot, slot_count))
            for label_table in labels
        )
    )


def visible(query_labels, key_labels):
    query_tree, query_seg = query_labels
    key_tree, key_seg = key_labels
    parent = jnp.where(query_seg > BRANCHES, 1 + (query_seg - BRANCHES - 1) // LEAVES, 0)
    reaches = (
        (key_seg[None, :] == 0)
        | (key_seg[None, :] == query_seg[:, None])
        | (key_seg[None, :] == parent[:, None])
    )
    return (query_tree[:, None] == key_tree[None, :]) & reaches


def head_view(matrix):
    return matrix.reshape(matrix.shape[0], matrix.shape[1] // HEAD_DIM, HEAD_DIM)


def scores_of(query_heads, key_heads):
    return jnp.einsum(
        "qhd,khd->hqk", query_heads, key_heads, preferred_element_type=jnp.float32
    ) * HEAD_DIM ** (-0.5)


def weights_of(scores, log_total, allowed):
    return jnp.where(allowed[None], jnp.exp(scores - log_total[:, :, None]), 0.0)


def score_grads(query_heads, grad_heads, key_heads, value_heads, log_total, row_delta, allowed):
    weights = weights_of(scores_of(query_heads, key_heads), log_total, allowed)
    prob_grad = jnp.einsum(
        "qhd,khd->hqk", grad_heads, value_heads, preferred_element_type=jnp.float32
    )
    return (
        (weights * (prob_grad - row_delta[:, :, None])).astype(jnp.bfloat16),
        weights.astype(jnp.bfloat16),
    )


def shards(
    patches,
    out_grad,
    block_order,
    first_gain,
    first_shift,
    attn_proj,
    attn_bias,
    out_proj,
    out_bias,
    second_gain,
    second_shift,
    up_proj,
    up_bias,
    down_proj,
    down_bias,
):
    attn_full, out_full, up_full, down_full = (
        lax.all_gather(attn_proj, "fsdp", axis=1, tiled=True),
        lax.all_gather(out_proj, "fsdp", axis=1, tiled=True),
        lax.all_gather(up_proj, "fsdp", axis=0, tiled=True),
        lax.all_gather(down_proj, "fsdp", axis=1, tiled=True),
    )
    labels = slot_labels(block_order[0])
    row_count = patches.shape[0]
    own_slots = row_count // BLOCK
    query_labels = row_labels(labels, lax.axis_index("context") * own_slots, own_slots)
    head_width = attn_full.shape[2]
    head_count = head_width // HEAD_DIM
    key_block = 4 * BLOCK
    block_slots = key_block // BLOCK
    score_scale = HEAD_DIM ** (-0.5)
    inputs = patches.astype(jnp.float32)
    first_norm, first_normed, first_inverse = layer_norm(inputs, first_gain, first_shift)
    first_low = first_norm.astype(jnp.bfloat16)
    projected = jnp.einsum("rd,cde->cre", first_low, attn_full, preferred_element_type=jnp.float32)
    queries = (projected[0] + attn_bias[0]).astype(jnp.bfloat16)
    keys_low = projected[1].astype(jnp.bfloat16)
    values_low = (projected[2] + attn_bias[1]).astype(jnp.bfloat16)
    keys_all = lax.all_gather(
        jnp.concatenate([keys_low, values_low], axis=1), "context", axis=0, tiled=True
    )
    block_count = keys_all.shape[0] // key_block
    query_heads = head_view(queries)

    def key_piece(step_index):
        key_slab = lax.dynamic_slice_in_dim(keys_all, step_index * key_block, key_block, 0)
        allowed = visible(query_labels, row_labels(labels, step_index * block_slots, block_slots))
        return (head_view(key_slab[:, :head_width]), head_view(key_slab[:, head_width:]), allowed)

    def total_step(step_index, carried):
        running_top, running_sum = carried
        key_heads, value_heads, allowed = key_piece(step_index)
        masked = jnp.where(allowed[None], scores_of(query_heads, key_heads), far_below)
        new_top = jnp.maximum(running_top, jnp.max(masked, axis=2))
        kept_exp = jnp.where(allowed[None], jnp.exp(masked - new_top[:, :, None]), 0.0)
        return (new_top, running_sum * jnp.exp(running_top - new_top) + jnp.sum(kept_exp, axis=2))

    start_top = jnp.full((head_count, row_count), far_below, jnp.float32)
    running_top, running_sum = lax.fori_loop(
        0, block_count, total_step, (start_top, jnp.zeros((head_count, row_count), jnp.float32))
    )
    log_total = running_top + jnp.log(running_sum)

    def mix_step(step_index, mixed):
        key_heads, value_heads, allowed = key_piece(step_index)
        weights = weights_of(scores_of(query_heads, key_heads), log_total, allowed).astype(
            jnp.bfloat16
        )
        return mixed + jnp.einsum(
            "hqk,khd->qhd", weights, value_heads, preferred_element_type=jnp.float32
        )

    attended = lax.fori_loop(
        0, block_count, mix_step, jnp.zeros((row_count, head_count, HEAD_DIM), jnp.float32)
    )
    attended_low = attended.reshape(row_count, head_width).astype(jnp.bfloat16)
    attn_part = jnp.dot(attended_low, out_full, preferred_element_type=jnp.float32)
    middle = inputs + (lax.psum(attn_part, "tensor") + out_bias)
    second_norm, second_normed, second_inverse = layer_norm(middle, second_gain, second_shift)
    second_low = second_norm.astype(jnp.bfloat16)
    pre_act = jnp.dot(second_low, up_full, preferred_element_type=jnp.float32) + up_bias
    hidden, gelu_back = jax.vjp(partial(jax.nn.gelu, approximate=False), pre_act)
    hidden_low = hidden.astype(jnp.bfloat16)
    mlp_part = jnp.dot(hidden_low, down_full, preferred_element_type=jnp.float32)
    result = (
        middle + (lax.psum(mlp_part.astype(jnp.bfloat16), "tensor").astype(jnp.float32) + down_bias)
    ).astype(jnp.bfloat16)
    top_grad = out_grad.astype(jnp.float32)
    grad_down_bias = jnp.sum(top_grad, axis=0)
    grad_down = jnp.einsum("rf,rd->fd", hidden_low, out_grad, preferred_element_type=jnp.float32)
    hidden_grad = jnp.einsum("rd,fd->rf", out_grad, down_full, preferred_element_type=jnp.float32)
    pre_grad = gelu_back(hidden_grad)[0].astype(jnp.bfloat16)
    grad_up_bias = jnp.sum(pre_grad.astype(jnp.float32), axis=0)
    grad_up = jnp.einsum("rd,rf->df", second_low, pre_grad, preferred_element_type=jnp.float32)
    second_part = jnp.einsum("rf,df->rd", pre_grad, up_full, preferred_element_type=jnp.float32)
    second_grad = lax.psum(second_part, "tensor")
    grad_second_gain = jnp.sum(second_grad * second_normed, axis=0)
    grad_second_shift = jnp.sum(second_grad, axis=0)
    middle_grad = top_grad + norm_back(second_grad, second_normed, second_inverse, second_gain)
    branch_grad = middle_grad.astype(jnp.bfloat16)
    grad_out_bias = jnp.sum(branch_grad.astype(jnp.float32), axis=0)
    grad_out = jnp.einsum(
        "re,rd->ed", attended_low, branch_grad, preferred_element_type=jnp.float32
    )
    attended_grad = jnp.einsum(
        "rd,ed->re", branch_grad, out_full, preferred_element_type=jnp.float32
    ).astype(jnp.bfloat16)
    grad_heads = head_view(attended_grad)

    def delta_step(step_index, row_delta):
        key_heads, value_heads, allowed = key_piece(step_index)
        weights = weights_of(scores_of(query_heads, key_heads), log_total, allowed)
        prob_grad = jnp.einsum(
            "qhd,khd->hqk", grad_heads, value_heads, preferred_element_type=jnp.float32
        )
        return row_delta + jnp.sum(weights * prob_grad, axis=2)

    row_delta = lax.fori_loop(
        0, block_count, delta_step, jnp.zeros((head_count, row_count), jnp.float32)
    )
    query_start = jnp.zeros((row_count, head_count, HEAD_DIM), jnp.float32)

    def back_step(step_index, carried):
        query_acc, key_acc = carried
        key_heads, value_heads, allowed = key_piece(step_index)
        score_low, weights_low = score_grads(
            query_heads, grad_heads, key_heads, value_heads, log_total, row_delta, allowed
        )
        query_acc = query_acc + jnp.einsum(
            "hqk,khd->qhd", score_low, key_heads, preferred_element_type=jnp.float32
        )
        key_part = jnp.einsum(
            "hqk,qhd->khd", score_low, query_heads, preferred_element_type=jnp.float32
        )
        value_part = jnp.einsum(
            "hqk,qhd->khd", weights_low, grad_heads, preferred_element_type=jnp.float32
        )
        joined = jnp.concatenate(
            [key_part.reshape(key_block, head_width), value_part.reshape(key_block, head_width)],
            axis=1,
        )
        return (
            query_acc,
            lax.dynamic_update_slice_in_dim(key_acc, joined, step_index * key_block, 0),
        )

    key_start = jnp.zeros((keys_all.shape[0], 2 * head_width), jnp.float32)
    query_acc, key_acc = lax.fori_loop(0, block_count, back_step, (query_start, key_start))
    key_value_grad = lax.psum_scatter(key_acc, "context", scatter_dimension=0, tiled=True)
    query_grad = (query_acc.reshape(row_count, head_width) * score_scale).astype(jnp.bfloat16)
    key_grad = (key_value_grad[:, :head_width] * score_scale).astype(jnp.bfloat16)
    value_grad = key_value_grad[:, head_width:].astype(jnp.bfloat16)
    stacked = jnp.stack([query_grad, key_grad, value_grad])
    grad_attn_bias = jnp.stack(
        [
            jnp.sum(query_grad.astype(jnp.float32), axis=0),
            jnp.sum(value_grad.astype(jnp.float32), axis=0),
        ]
    )
    grad_attn = jnp.einsum("rd,cre->cde", first_low, stacked, preferred_element_type=jnp.float32)
    first_grad = lax.psum(
        jnp.einsum("cre,cde->rd", stacked, attn_full, preferred_element_type=jnp.float32), "tensor"
    )
    grad_first_gain = jnp.sum(first_grad * first_normed, axis=0)
    grad_first_shift = jnp.sum(first_grad, axis=0)
    patch_grad = middle_grad + norm_back(first_grad, first_normed, first_inverse, first_gain)
    wide_attn, wide_out, wide_up, wide_down = (
        lax.psum_scatter(grad_attn, ("fsdp", "context"), scatter_dimension=1, tiled=True),
        lax.psum_scatter(grad_out, ("fsdp", "context"), scatter_dimension=1, tiled=True),
        lax.psum_scatter(grad_up, ("fsdp", "context"), scatter_dimension=0, tiled=True),
        lax.psum_scatter(grad_down, ("fsdp", "context"), scatter_dimension=1, tiled=True),
    )
    grad_attn, grad_out, grad_up, grad_down = (
        lax.all_gather(wide_attn, "context", axis=1, tiled=True),
        lax.all_gather(wide_out, "context", axis=1, tiled=True),
        lax.all_gather(wide_up, "context", axis=0, tiled=True),
        lax.all_gather(wide_down, "context", axis=1, tiled=True),
    )
    small_grads = lax.psum(
        (
            grad_first_gain,
            grad_first_shift,
            grad_attn_bias,
            grad_out_bias,
            grad_second_gain,
            grad_second_shift,
            grad_up_bias,
            grad_down_bias,
        ),
        ("fsdp", "context"),
    )
    return (
        result,
        patch_grad,
        small_grads[0],
        small_grads[1],
        grad_attn,
        small_grads[2],
        grad_out,
        small_grads[3],
        small_grads[4],
        small_grads[5],
        grad_up,
        small_grads[6],
        grad_down,
        small_grads[7],
    )


def solution(mesh):
    return jax.shard_map(
        shards,
        mesh=mesh,
        in_specs=(
            P(("fsdp", "context"), None),
            P(("fsdp", "context"), None),
            P("fsdp", None),
            P(),
            P(),
            P(None, "fsdp", "tensor"),
            P(None, "tensor"),
            P("tensor", "fsdp"),
            P(),
            P(),
            P(),
            P("fsdp", "tensor"),
            P("tensor"),
            P("tensor", "fsdp"),
            P(),
        ),
        out_specs=(
            P(("fsdp", "context"), None),
            P(("fsdp", "context"), None),
            P(),
            P(),
            P(None, "fsdp", "tensor"),
            P(None, "tensor"),
            P("tensor", "fsdp"),
            P(),
            P(),
            P(),
            P("fsdp", "tensor"),
            P("tensor"),
            P("tensor", "fsdp"),
            P(),
        ),
        check_vma=False,
    )
```

profile of v0, /device:TPU:0, one launch (start us, length us, event | category | flops | bytes accessed | tf_op | source)
XLA Modules:
  0.0 950.1 jit_solution(17451952683291024522)
XLA Ops:
  13.5 31.5 %all_gather.27 = bf16[3,768,192]{2,0,1:T(4,128)(2,1)} all-gather(bf16[3,192,192]{2,0,1:T(4,128)(2,1)S(1)} %copy.39), channel_id=1, replica_groups=mesh['fsdp'=4,'context'=2,'tensor'=4] {'fsdp'}, dimensions={1}, use_global_device_ids=true | all-gather | bytes 1105920 | tf_op jit(solution)/shard_map/all_gather | solution.py:109
  56.9 16.8 %all_gather.29 = bf16[192,768]{0,1:T(8,128)(2,1)} all-gather(bf16[192,192]{0,1:T(8,128)(2,1)} %copy.42), channel_id=1, replica_groups=mesh['fsdp'=4,'context'=2,'tensor'=4] {'fsdp'}, dimensions={1}, use_global_device_ids=true | all-gather | bytes 368640 | tf_op jit(solution)/shard_map/all_gather | solution.py:110
  73.8 11.5 %all-gather.4.cloned.1.call-done = bf16[2560,384]{0,1:T(8,128)(2,1)} async-done(((bf16[1280,384]{0,1:T(8,128)(2,1)}), bf16[2560,384]{0,1:T(8,128)(2,1)}) %all-gather.4.cloned.1.call-update) | async-done | bytes 1966096 | tf_op jit(solution)/shard_map/all_gather | solution.py:130
  85.2 31.9 %while.88 = (s32[]{:T(128)}, f32[3,1280]{1,0:T(4,128)S(1)}, f32[3,1280]{1,0:T(4,128)S(1)}, s32[20]{0:T(128)S(1)}, s32[20]{0:T(128)S(1)}, /*index=5*/bf16[2560,38...) while((s32[]{:T(128)}, f32[3,1280]{1,0:T(4,128)S(1)}, ...), condition=%wide.region_5.6_spmd.clone.clone.clone, body=%wide.region_2.5_spmd.clone.clone.clone.sunk | while | flops 271363072 | bytes 19016176 | solution.py:150
  117.2 40.3 %while.89 = (s32[]{:T(128)}, f32[1280,3,64]{0,2,1:T(8,128)}, bf16[2560,384]{0,1:T(8,128)(2,1)}, s32[20]{0:T(128)S(1)}, s32[20]{0:T(128)S(1)}, /*index=5*/bf16[12...) while((s32[]{:T(128)}, f32[1280,3,64]{0,2,1:T(8,128)}, ...), condition=%wide.region_7.8_spmd.clone.clone.clone, body=%wide.region_6.7_spmd.clone.clone.clone.sunk | while | flops 515629312 | bytes 5003783 | solution.py:164
  164.6 79.9 %all-reduce.6.cloned.1.call-done = f32[1280,768]{1,0:T(8,128)} async-done(((f32[1280,768]{1,0:T(8,128)}), f32[1280,768]{1,0:T(8,128)}) %all-reduce.6.cloned.1.call-update) | async-done | bytes 3932176 | tf_op jit(solution)/shard_map/psum | solution.py:169
  249.9 6.5 convolution_add_fusion
  256.4 13.5 %convert_reduce_fusion.2 = (f32[768]{0:T(1024)}, bf16[1280,768]{1,0:T(8,128)(2,1)S(1)}, f32[1280,768]{1,0:T(8,128)}) fusion(f32[1280,768]{1,0:T(8,128)} %convolution_add_fusion, bf16[1280,768]{1,0:T(8,128)(2,1)S(1)} %copy-done.10, bf16[768,768]{0,1:T(8,128)(2,1)} %all-gather.8.cloned.1.call-done), kind=kOutput, calls=%fused_computation.149 | convolution fusion | flops 1582693632 | bytes 12979200 | tf_op jit(solution)/shard_map/rd,fd->rf/dot_general | solution.py:182
  283.4 73.0 %all-reduce.10.cloned.1.call-done = f32[1280,768]{1,0:T(8,128)} async-done(((f32[1280,768]{1,0:T(8,128)}), f32[1280,768]{1,0:T(8,128)}) %all-reduce.10.cloned.1.call-update) | async-done | bytes 3932176 | tf_op jit(solution)/shard_map/psum | solution.py:187
  361.6 47.0 %all-reduce.8.cloned.1.call-done = bf16[1280,768]{1,0:T(8,128)(2,1)} async-done(((bf16[1280,768]{1,0:T(8,128)(2,1)}), bf16[1280,768]{1,0:T(8,128)(2,1)}) %all-reduce.8.cloned.1.call-update) | async-done | bytes 1966096 | tf_op jit(solution)/shard_map/psum | solution.py:177
  408.7 5.9 convert_reduce_fusion.3
  417.3 33.9 %while.90 = (s32[]{:T(128)}, f32[3,1280]{1,0:T(4,128)S(1)}, s32[20]{0:T(128)S(1)}, s32[20]{0:T(128)S(1)}, bf16[2560,384]{0,1:T(8,128)(2,1)}, /*index=5*/bf16[128...) while((s32[]{:T(128)}, f32[3,1280]{1,0:T(4,128)S(1)}, ...), condition=%wide.region_17.18_spmd.clone.clone.clone, body=%wide.region_15.17_spmd.clone.clone.clone.sunk | while | flops 517107712 | bytes 19319308 | solution.py:209
  453.5 59.0 %while.91 = (s32[]{:T(128)}, f32[1280,3,64]{0,2,1:T(8,128)S(1)}, f32[2560,384]{0,1:T(8,128)}, bf16[2560,384]{0,1:T(8,128)(2,1)}, s32[20]{0:T(128)S(1)}, /*index=...) while((s32[]{:T(128)}, f32[1280,3,64]{0,2,1:T(8,128)S(1)}, ...), condition=%wide.region_19.20_spmd.clone.clone.clone, body=%wide.region_18.19_spmd.clone.clone.clone.sunk | while | flops 1282597120 | bytes 45109792 | solution.py:239
  522.7 6.4 fusion.116
  529.3 35.4 %reduce-scatter.10.cloned.1.call-done = f32[1280,384]{0,1:T(8,128)} async-done(((f32[2560,384]{0,1:T(8,128)}), f32[1280,384]{0,1:T(8,128)}) %reduce-scatter.10.cloned.1.call-update) | async-done | bytes 1966096 | tf_op jit(solution)/shard_map/reduce_scatter | solution.py:240
  584.6 46.2 %reduce-scatter.18.cloned.1.call-done = f32[96,192]{1,0:T(8,128)} async-done(((f32[768,192]{1,0:T(8,128)}), f32[96,192]{1,0:T(8,128)}) %reduce-scatter.18.cloned.1.call-update) | async-done | bytes 73744
  637.1 65.3 %reduce-scatter.14.cloned.1.call-done = f32[768,96]{0,1:T(8,128)} async-done(((f32[768,768]{0,1:T(8,128)}), f32[768,96]{0,1:T(8,128)}) %reduce-scatter.14.cloned.1.call-update) | async-done | bytes 294928 | tf_op jit(solution)/shard_map/reduce_scatter | solution.py:262
  702.4 8.6 all_gather.35
  711.0 63.1 %reduce-scatter.12.cloned.1.call-done = f32[96,768]{1,0:T(8,128)} async-done(((f32[768,768]{1,0:T(8,128)}), f32[96,768]{1,0:T(8,128)}) %reduce-scatter.12.cloned.1.call-update) | async-done | bytes 294928 | tf_op jit(solution)/shard_map/reduce_scatter | solution.py:261
  774.1 9.6 %all_gather.34 = f32[192,768]{1,0:T(8,128)} all-gather(f32[96,768]{1,0:T(8,128)} %reduce-scatter.12.cloned.1.call-done), channel_id=1, replica_groups=mesh['fsdp'=4,'context'=2,'tensor'=4] {'context'}, dimensions={0}, use_global_device_ids=true | all-gather | bytes 884736 | tf_op jit(solution)/shard_map/all_gather | solution.py:267
  783.8 73.6 %all-reduce.12.cloned.1.call-done = f32[1280,768]{1,0:T(8,128)} async-done(((f32[1280,768]{1,0:T(8,128)}), f32[1280,768]{1,0:T(8,128)}) %all-reduce.12.cloned.1.call-update) | async-done | bytes 3932176 | tf_op jit(solution)/shard_map/psum | solution.py:252
  860.9 38.0 %all-reduce = (f32[768]{0:T(1024)}, f32[768]{0:T(1024)}, f32[2,192]{1,0:T(2,128)}, f32[768]{0:T(1024)}, f32[768]{0:T(1024)}, /*index=5*/f32[768]{0:T(1024)}, f32[768]{0:T(1024)}, f32[768]{0:T(1024)}) all-reduce(f32[768]{0:T(1024)S(1)} %get-tuple-element.1970, ...), channel_id=1, replica_groups=mesh['fsdp'=4,'context'=2,'tensor'=4] {'fsdp','context'}, use_global_device_ids=true, to_apply=%region_25.26 | all-reduce | flops 5760 | bytes 46080 | tf_op jit(solution)/shard_map/psum | solution.py:270
  904.3 23.6 %reduce-scatter.16.cloned.1.call-done = f32[96,576]{1,0:T(8,128)} async-done(((f32[768,576]{1,0:T(8,128)}), f32[96,576]{1,0:T(8,128)}) %reduce-scatter.16.cloned.1.call-update) | async-done | bytes 221200
  929.0 9.8 %all_gather.32 = f32[3,192,192]{2,0,1:T(4,128)S(1)} all-gather(f32[3,96,192]{2,0,1:T(4,128)S(1)} %bitcast.417), channel_id=1, replica_groups=mesh['fsdp'=4,'context'=2,'tensor'=4] {'context'}, dimensions={1}, use_global_device_ids=true | all-gather | bytes 663552 | tf_op jit(solution)/shard_map/all_gather | solution.py:265
  (390 shorter events, 267.3 us)
Async XLA Ops:
  8.0 77.2 %all-gather.4.cloned.1.call-start = ((), (), s32[]{:S(2)}) async-start(), calls=%async_computation.5 | async-start | bytes 2949120 | tf_op jit(solution)/shard_map/all_gather | solution.py:130
  10.7 36.9 %copy-start.2 = (bf16[1280,768]{1,0:T(8,128)(2,1)S(1)}, bf16[1280,768]{1,0:T(8,128)(2,1)}, u32[]{:S(2)}) copy-start(bf16[1280,768]{1,0:T(8,128)(2,1)} %param.23) | copy-start | bytes 5898244
  10.7 36.9 %copy-start.18 = (f32[768]{0:T(1024)S(1)}, f32[768]{0:T(1024)}, u32[]{:S(2)}) copy-start(f32[768]{0:T(1024)} %param.26) | copy-start | bytes 9220
  10.7 36.9 %copy-start.31 = (f32[768]{0:T(1024)S(1)}, f32[768]{0:T(1024)}, u32[]{:S(2)}) copy-start(f32[768]{0:T(1024)} %param.27) | copy-start | bytes 9220
  10.8 38.4 %copy-start.14 = (f32[1280]{0:T(1024)}, f32[1280]{0:T(1024)S(1)}, u32[]{:S(2)}) copy-start(f32[1280]{0:T(1024)S(1)} %broadcast_multiply_fusion.5) | copy-start | bytes 15364
  13.2 36.0 %copy-start.16 = (f32[1280]{0:T(1024)}, f32[1280]{0:T(1024)S(1)}, u32[]{:S(2)}) copy-start(f32[1280]{0:T(1024)S(1)} %add_rsqrt_fusion.1) | copy-start | bytes 15364
  52.0 192.6 %all-reduce.6.cloned.1.call-start = ((), (), s32[]{:S(2)}) async-start(), calls=%async_computation.6 | async-start | bytes 7864320 | tf_op jit(solution)/shard_map/psum | solution.py:169
  159.5 85.1 %copy-start.23 = (f32[768]{0:T(1024)S(1)}, f32[768]{0:T(1024)}, u32[]{:S(2)}) copy-start(f32[768]{0:T(1024)} %param.31) | copy-start | bytes 9220
  163.2 86.7 %all-gather.6.cloned.1.call-start = ((), (), s32[]{:S(2)}) async-start(), calls=%async_computation.7 | async-start | bytes 1474560 | tf_op jit(solution)/shard_map/all_gather | solution.py:111
  163.8 92.7 %all-gather.8.cloned.1.call-start = ((), (), s32[]{:S(2)}) async-start(), calls=%async_computation.8 | async-start | bytes 1474560 | tf_op jit(solution)/shard_map/all_gather | solution.py:112
  164.4 192.1 %all-reduce.10.cloned.1.call-start = ((), (), s32[]{:S(2)}) async-start(), calls=%async_computation.10 | async-start | bytes 7864320 | tf_op jit(solution)/shard_map/psum | solution.py:187
  256.4 14.8 %copy-start.27 = (bf16[768,768]{1,0:T(8,128)(2,1)S(1)}, bf16[768,768]{1,0:T(8,128)(2,1)}, u32[]{:S(2)}) copy-start(bf16[768,768]{1,0:T(8,128)(2,1)} %all-gather.6.cloned.1.call-done) | copy-start | bytes 3538948
  274.9 133.8 %all-reduce.8.cloned.1.call-start = ((), (), s32[]{:S(2)}) async-start(), calls=%async_computation.9 | async-start | bytes 3932160 | tf_op jit(solution)/shard_map/psum | solution.py:177
  283.3 281.4 %reduce-scatter.10.cloned.1.call-start = ((), (), s32[]{:S(2)}) async-start(), calls=%async_computation.11 | async-start | bytes 5898240 | tf_op jit(solution)/shard_map/reduce_scatter | solution.py:240
  283.4 125.3 %copy-start.24 = (f32[768]{0:T(1024)S(1)}, f32[768]{0:T(1024)}, u32[]{:S(2)}) copy-start(f32[768]{0:T(1024)} %param.37) | copy-start | bytes 9220
  512.5 118.2 %reduce-scatter.18.cloned.1.call-start = ((), (), s32[]{:S(2)}) async-start(), calls=%async_computation.16 | async-start | bytes 884736
  517.5 184.9 %reduce-scatter.14.cloned.1.call-start = ((), (), s32[]{:S(2)}) async-start(), calls=%async_computation.14 | async-start | bytes 2654208 | tf_op jit(solution)/shard_map/reduce_scatter | solution.py:262
  522.7 251.5 %reduce-scatter.12.cloned.1.call-start = ((), (), s32[]{:S(2)}) async-start(), calls=%async_computation.13 | async-start | bytes 2654208 | tf_op jit(solution)/shard_map/reduce_scatter | solution.py:261
  529.1 38.5 %copy-start.12 = (bf16[3,768,192]{1,2,0:T(8,128)(2,1)S(1)}, bf16[3,768,192]{1,2,0:T(8,128)(2,1)}, u32[]{:S(2)}) copy-start(bf16[3,768,192]{1,2,0:T(8,128)(2,1)} %copy-done.11) | copy-start | bytes 2654212
  529.1 328.2 %all-reduce.12.cloned.1.call-start = ((), (), s32[]{:S(2)}) async-start(), calls=%async_computation.12 | async-start | bytes 7864320 | tf_op jit(solution)/shard_map/psum | solution.py:252
  571.3 356.5 %reduce-scatter.16.cloned.1.call-start = ((), (), s32[]{:S(2)}) async-start(), calls=%async_computation.15 | async-start | bytes 2211840
  637.1 223.8 %copy-start.21 = (f32[768]{0:T(1024)S(1)}, f32[768]{0:T(1024)}, u32[]{:S(2)}) copy-start(f32[768]{0:T(1024)} %get-tuple-element.1968) | copy-start | bytes 9220
  637.1 223.8 %copy-start.22 = (f32[768]{0:T(1024)S(1)}, f32[768]{0:T(1024)}, u32[]{:S(2)}) copy-start(f32[768]{0:T(1024)} %get-tuple-element.1974) | copy-start | bytes 9220
  637.1 223.9 %copy-start.25 = (f32[768]{0:T(1024)S(1)}, f32[768]{0:T(1024)}, u32[]{:S(2)}) copy-start(f32[768]{0:T(1024)} %get-tuple-element.2064) | copy-start | bytes 9220
  (23 other events, 66.2 us)
Sparse Core Ops, SparseCore 0:
  52.1 33.0 all-gather.3
  163.3 81.2 all-reduce.5
  275.0 81.3 all-reduce.9
  359.3 49.3 all-reduce.7
  512.7 52.0 reduce-scatter.9
  568.3 62.4 reduce-scatter.17
  634.3 68.0 reduce-scatter.13
  705.9 68.1 reduce-scatter.11
  777.1 80.2 all-reduce.11
  860.7 67.1 reduce-scatter.15
Sparse Core Ops, SparseCore 1:
  165.2 30.2 all-gather.5
  196.9 29.4 all-gather.7
where the time goes:
time: 960 us; the launch traced here: 950 us
  waiting for transfers between devices  520 us (54%)
  matrix products  149 us (16%)
  blocking collectives  120 us (12%)
  other arithmetic  79.7 us (8%)
  local copies, waits for them, and re-layouts  63.8 us (7%)
  between operations  16.4 us (2%)
    psum x1, waiting for transfers between devices, shards(): middle = inputs + (lax.psum(attn_part, 'tensor') + out_bias)  79.9 us
    psum x1, waiting for transfers between devices, shards(): lax.psum(jnp.einsum('cre,cde->rd', stacked, attn_full, preferred_element_...  73.6 us
    psum x1, waiting for transfers between devices, shards(): second_grad = lax.psum(second_part, 'tensor')  73 us
    unnamed x14, waiting for transfers between devices  70.9 us
    reduce_scatter x1, waiting for transfers between devices, shards(): lax.psum_scatter(grad_down, ('fsdp', 'context'), scatter_dimension=1, til...  65.3 us
    reduce_scatter x1, waiting for transfers between devices, shards(): lax.psum_scatter(grad_up, ('fsdp', 'context'), scatter_dimension=0, tiled...  63.1 us
    psum x1, waiting for transfers between devices, shards(): lax.psum(mlp_part.astype(jnp.bfloat16), 'tensor').astype(jnp.float32)  47 us
    psum x1, blocking collectives, shards(): lax.psum((grad_first_gain, grad_first_shift, grad_attn_bias, grad_out_bia...  38 us
  transfers between devices with their start and end apart: 12, of which 10 were waited for; matrix products, arithmetic and copies ran while one was open for 7% of the time, Pallas kernels for 0%

commit v1 on v0

--- a/solution.py
+++ b/solution.py
@@ -3,6 +3,8 @@
 import jax
 import jax.numpy as jnp
 from jax import lax
+from jax.experimental import pallas as pl
+from jax.experimental.pallas import tpu as pltpu
 from jax.sharding import PartitionSpec as P
 
 HEAD_DIM = 64
@@ -298,9 +300,845 @@
     )
 
 
+bf16 = jnp.bfloat16
+f32 = jnp.float32
+VMEM = pl.BlockSpec(memory_space=pltpu.VMEM)
+SMEM = pl.BlockSpec(memory_space=pltpu.SMEM)
+ANY = pl.BlockSpec(memory_space=pl.ANY)
+MESH = pl.DeviceIdType.MESH
+LIMIT = 60 * 1024 * 1024
+
+
+def dot_nn(a, b):
+    return lax.dot_general(a, b, (((1,), (0,)), ((), ())), preferred_element_type=f32)
+
+
+def dot_nt(a, b):
+    return lax.dot_general(a, b, (((1,), (1,)), ((), ())), preferred_element_type=f32)
+
+
+def dot_tn(a, b):
+    return lax.dot_general(a, b, (((0,), (0,)), ((), ())), preferred_element_type=f32)
+
+
+class Here:
+    def __init__(self, fsdp_count):
+        self.f = lax.axis_index("fsdp")
+        self.c = lax.axis_index("context")
+        self.t = lax.axis_index("tensor")
+        self.x = self.t // 2
+        self.k = self.t % 2
+        self.core = (self.f, self.c, 2 * self.x + 1 - self.k)
+        self.xp = (self.f, self.c, 2 * (1 - self.x) + self.k)
+        self.yp = (self.f, 1 - self.c, self.t)
+        self.z = [((self.f + i) % fsdp_count, self.c, self.t) for i in range(1, fsdp_count)]
+        self.back = [(self.f + fsdp_count - i) % fsdp_count for i in range(1, fsdp_count)]
+
+
+def greet(devices):
+    barrier = pltpu.get_barrier_semaphore()
+    for device in devices:
+        pl.semaphore_signal(barrier, inc=1, device_id=device, device_id_type=MESH)
+    pl.semaphore_wait(barrier, len(devices))
+
+
+class Post:
+    def __init__(self, send_sem, recv_sem):
+        self.send_sem, self.recv_sem = send_sem, recv_sem
+        self.sent, self.open = [], []
+
+    def send(self, src, dst, device):
+        index = len(self.sent)
+        copy = pltpu.make_async_remote_copy(
+            src_ref=src,
+            dst_ref=dst,
+            send_sem=self.send_sem.at[index],
+            recv_sem=self.recv_sem.at[index],
+            device_id=device,
+            device_id_type=MESH,
+        )
+        copy.start()
+        self.sent.append(copy)
+        self.open.append(copy)
+        return copy
+
+    def got(self, copy):
+        copy.wait_recv()
+        self.open = [other for other in self.open if other is not copy]
+
+    def close(self):
+        for copy in self.open:
+            copy.wait_recv()
+        for copy in self.sent:
+            copy.wait_send()
+
+
+def ds(start, size, step=16):
+    return pl.ds(pl.multiple_of(start, step), size)
+
+
+def gather_kernel(
+    fsdp_count, patches, grads, wa, wu, wd, bias, rows_all, grads_all, wa_all, wu_all, wd_all, bias_all, local, ss, rs
+):
+    me = Here(fsdp_count)
+    f, c, t, k = me.f, me.c, me.t, me.k
+    rows = patches.shape[0]
+    part = rows // 4
+    deep = wa.shape[0]
+    half = deep // 2
+    greet([me.core, me.xp, me.yp] + me.z)
+    post = Post(ss, rs)
+    keep = [
+        (patches, rows_all.at[ds(rows * c, rows)]),
+        (grads, grads_all.at[ds(rows * c, rows)]),
+        (wa, wa_all.at[k, ds(deep * f, deep)]),
+        (wu, wu_all.at[k, ds(deep * f, deep)]),
+        (wd, wd_all.at[k, ds(deep * f, deep)]),
+        (bias, bias_all.at[k]),
+    ]
+    own = []
+    for index, (src, dst) in enumerate(keep):
+        copy = pltpu.make_async_copy(src, dst, local.at[index])
+        copy.start()
+        own.append(copy)
+    from_y = []
+    for src, dst in ((patches, rows_all), (grads, grads_all)):
+        from_y.append(post.send(src.at[ds(part * t, part)], dst.at[ds(rows * c + part * t, part)], me.yp))
+    from_z = []
+    for device in me.z:
+        from_z.append(post.send(wa, wa_all.at[k, ds(deep * f, deep)], device))
+    strips = []
+    for device in me.z:
+        for src, dst in ((wu, wu_all), (wd, wd_all)):
+            strips.append(
+                post.send(src.at[ds(half * c, half)], dst.at[k, ds(deep * f + half * c, half)], device)
+            )
+    for src, dst in keep[2:]:
+        post.send(src, dst, me.core)
+    from_x = []
+    there = rows * (1 - c)
+    for copy, dst in zip(from_y, (rows_all, grads_all)):
+        post.got(copy)
+        piece = dst.at[ds(there + part * t, part)]
+        from_x.append(post.send(piece, piece, me.xp))
+        post.send(piece, piece, me.core)
+    for copy, source in zip(from_z, me.back):
+        post.got(copy)
+        piece = wa_all.at[k, ds(deep * source, deep)]
+        post.send(piece, piece, me.core)
+    passed = []
+    for index, source in enumerate(me.back):
+        for copy, dst in zip(strips[2 * index : 2 * index + 2], (wu_all, wd_all)):
+            post.got(copy)
+            piece = dst.at[k, ds(deep * source + half * c, half)]
+            passed.append(post.send(piece, piece, me.yp))
+            post.send(piece, piece, me.core)
+    other = (t + 2) % 4
+    for copy, dst in zip(from_x, (rows_all, grads_all)):
+        post.got(copy)
+        piece = dst.at[ds(there + part * other, part)]
+        post.send(piece, piece, me.core)
+    for index, source in enumerate(me.back):
+        for copy, dst in zip(passed[2 * index : 2 * index + 2], (wu_all, wd_all)):
+            post.got(copy)
+            piece = dst.at[k, ds(deep * source + half * (1 - c), half)]
+            post.send(piece, piece, me.core)
+    post.close()
+    for copy in own:
+        copy.wait()
+
+
+def gather(fsdp_count, patches, grads, wa, wu, wd, bias):
+    rows, width = patches.shape
+    deep = wa.shape[0]
+    whole = jax.ShapeDtypeStruct((2 * rows, width), bf16)
+    weight = lambda w: jax.ShapeDtypeStruct((2, deep * fsdp_count, w.shape[1]), bf16)
+    return pl.pallas_call(
+        partial(gather_kernel, fsdp_count),
+        out_shape=(whole, whole, weight(wa), weight(wu), weight(wd), jax.ShapeDtypeStruct((2,) + bias.shape, f32)),
+        in_specs=[ANY] * 6,
+        out_specs=(ANY,) * 6,
+        scratch_shapes=[pltpu.SemaphoreType.DMA((6,)), pltpu.SemaphoreType.DMA((64,)), pltpu.SemaphoreType.DMA((64,))],
+        compiler_params=pltpu.CompilerParams(collective_id=0, has_side_effects=True, vmem_limit_bytes=LIMIT),
+        name="gather",
+    )(patches, grads, wa, wu, wd, bias)
+
+
+TRUNK = TRUNK_BLK * BLOCK
+SUB = (1 + LEAVES) * BLOCK
+KEYS = TRUNK + SUB
+OWN = 2 * BLOCK + SUB
+PIECES = (
+    (2 * BLOCK, TRUNK, 2 * BLOCK),
+    (3 * BLOCK, TRUNK + BLOCK, BLOCK),
+    (4 * BLOCK, TRUNK + BLOCK, 2 * BLOCK),
+)
+
+
+def own_places(s):
+    return [2 * s, 2 * s + 1, 12 + 2 * s, 8 + s, 13 + 2 * s]
+
+
+def row_norm(values):
+    center = values - jnp.mean(values, axis=1, keepdims=True)
+    inverse = lax.rsqrt(jnp.mean(center * center, axis=1, keepdims=True) + epsilon)
+    return center * inverse, inverse
+
+
+def front_kernel(
+    where, rows_all, grads_all, wa, bias, gain, shift,
+    x_own, g_own, low_own, q_out, k_out, v_out, kt_out, attended, lse_out, wh,
+    low, vt, att_t, st, pt,
+):
+    c, t = lax.axis_index("context"), lax.axis_index("tensor")
+    s = 2 * c + t % 2
+    places = [*range(TRUNK_BLK)] + own_places(s)[2:]
+    gain_row, shift_row = gain[...], shift[...]
+
+    def norm_block(place, dst, dst_row):
+        values = rows_all[ds(where[place] * BLOCK, BLOCK), :]
+        normed, _ = row_norm(values.astype(f32))
+        dst[ds(dst_row, BLOCK), :] = (normed * gain_row + shift_row).astype(bf16)
+
+    def trunk_step(j, carried):
+        norm_block(j, low, j * BLOCK)
+        return carried
+
+    lax.fori_loop(0, TRUNK_BLK, trunk_step, 0)
+    for j in range(TRUNK_BLK, len(places)):
+        norm_block(places[j], low, j * BLOCK)
+    for j, place in enumerate(own_places(s)):
+        x_own[pl.ds(j * BLOCK, BLOCK), :] = rows_all[ds(where[place] * BLOCK, BLOCK), :]
+        g_own[pl.ds(j * BLOCK, BLOCK), :] = grads_all[ds(where[place] * BLOCK, BLOCK), :]
+    low_own[0 : 2 * BLOCK, :] = low[ds(2 * BLOCK * s, 2 * BLOCK), :]
+    low_own[2 * BLOCK :, :] = low[TRUNK:, :]
+    for i, slab in enumerate((0, 1, 2, 5)):
+        wh[i, :, 0:128] = wa[0, :, 128 * slab : 128 * slab + 128]
+        wh[i, :, 128:256] = wa[1, :, 128 * slab : 128 * slab + 128]
+        start = 384 + 64 * i
+        wh[i, :, 256:384] = jnp.concatenate(
+            [wa[0, :, start : start + 64], wa[1, :, start : start + 64]], axis=1
+        )
+
+    def heads_row(row):
+        a, b = bias[0, row : row + 1, :], bias[1, row : row + 1, :]
+        return jnp.concatenate([a[:, 0:128], b[:, 0:128], a[:, 128:192], b[:, 128:192]], axis=1)
+
+    q_out[...] = ((dot_nn(low_own[...], wh[0]) + heads_row(1)).astype(bf16) * HEAD_DIM ** (-0.5)).astype(bf16)
+    value_bias = heads_row(2)
+
+    def project(j, carried):
+        rows = ds(j * (KEYS // 2), KEYS // 2)
+        k_out[rows, :] = dot_nn(low[rows, :], wh[1]).astype(bf16)
+        v_out[rows, :] = (dot_nn(low[rows, :], wh[2]) + value_bias).astype(bf16)
+        return carried
+
+    lax.fori_loop(0, 2, project, 0)
+    kt_out[...] = k_out[...].T
+    vt[...] = v_out[...].T
+    lane = lax.broadcasted_iota(jnp.int32, (OWN, 128), 1) // HEAD_DIM
+
+    def head(h, carried):
+        slab, part = h // 2, h % 2
+        lanes = pl.ds(pl.multiple_of(slab * 128, 128), 128)
+        own_q = q_out[:, lanes]
+        q_part = jnp.where(lane == part, own_q, jnp.zeros_like(own_q))
+        st[0:TRUNK, :] = dot_nt(k_out[0:TRUNK, lanes], q_part)
+        for q_row, k_row, count in PIECES:
+            st[TRUNK : TRUNK + count, q_row : q_row + BLOCK] = dot_nt(
+                k_out[k_row : k_row + count, lanes], q_part[q_row : q_row + BLOCK]
+            )
+        tops, totals = [], []
+        for j in range(OWN // BLOCK):
+            cols = slice(j * BLOCK, (j + 1) * BLOCK)
+            count = TRUNK + (0 if j < 2 else PIECES[j - 2][2])
+            top = jnp.full((8, BLOCK), far_below, f32)
+            for r in range(0, count, BLOCK):
+                piece = st[r : r + BLOCK, cols].reshape(BLOCK // 8, 8, BLOCK)
+                top = jnp.maximum(top, jnp.max(piece, axis=0))
+            top = jnp.max(top, axis=0, keepdims=True)
+            total = jnp.zeros((8, BLOCK), f32)
+            for r in range(0, count, BLOCK):
+                weight = jnp.exp(st[r : r + BLOCK, cols] - top)
+                total = total + jnp.sum(weight.reshape(BLOCK // 8, 8, BLOCK), axis=0)
+                pt[r : r + BLOCK, cols] = weight.astype(bf16)
+            tops.append(top)
+            totals.append(jnp.sum(total, axis=0, keepdims=True))
+        total = jnp.concatenate(totals, axis=1)
+        head_rows = ds(h * HEAD_DIM, HEAD_DIM)
+        att_t[head_rows, :] = dot_nn(vt[head_rows, 0:TRUNK], pt[0:TRUNK, :])
+        for q_row, k_row, count in PIECES:
+            cols = slice(q_row, q_row + BLOCK)
+            att_t[head_rows, cols] += dot_nn(
+                vt[head_rows, k_row : k_row + count], pt[TRUNK : TRUNK + count, cols]
+            )
+        att_t[head_rows, :] = att_t[head_rows, :] / total
+        lse_out[pl.ds(h, 1), :] = jnp.concatenate(tops, axis=1) + jnp.log(total)
+        return carried
+
+    lax.fori_loop(0, 6, head, 0)
+    attended[...] = att_t[...].T.astype(bf16)
+
+
+def front(where, rows_all, grads_all, wa, bias, gain, shift):
+    width = rows_all.shape[1]
+    shape = jax.ShapeDtypeStruct
+    return pl.pallas_call(
+        front_kernel,
+        out_shape=(
+            shape((OWN, width), bf16),
+            shape((OWN, width), bf16),
+            shape((OWN, width), bf16),
+            shape((OWN, 384), bf16),
+            shape((KEYS, 384), bf16),
+            shape((KEYS, 384), bf16),
+            shape((384, KEYS), bf16),
+            shape((OWN, 384), bf16),
+            shape((8, OWN), f32),
+            shape((4, width, 384), bf16),
+        ),
+        in_specs=[SMEM] + [VMEM] * 6,
+        out_specs=(VMEM,) * 10,
+        scratch_shapes=[
+            pltpu.VMEM((KEYS, width), bf16),
+            pltpu.VMEM((384, KEYS), bf16),
+            pltpu.VMEM((384, OWN), f32),
+            pltpu.VMEM((TRUNK + 2 * BLOCK, OWN), f32),
+            pltpu.VMEM((TRUNK + 2 * BLOCK, OWN), bf16),
+        ],
+        compiler_params=pltpu.CompilerParams(vmem_limit_bytes=LIMIT),
+        name="front",
+    )(where, rows_all, grads_all, wa, bias, gain, shift)
+
+
+HALF = OWN // 2
+
+
+def middle_kernel(
+    fsdp_count, attended, wo, x_own, g_own, wu_in, wd_in, bias, gain, shift, out_bias, down_bias,
+    result_half, middle_grad, da, g_up, g_down, g_out, stats, up_stats,
+    wu, wd, att_x, wo_x, middle, normed, inverse, low, hidden, pre_grad, second, second_send, second_x,
+    mlp_send, mlp_x, da_send, g_out_send, g_out_x, local, ss, rs,
+):
+    me = Here(fsdp_count)
+    x, k = me.x, me.k
+    width = x_own.shape[1]
+    mine, far = HALF * x, HALF * (1 - x)
+    here_rows, far_rows = ds(mine, HALF), ds(far, HALF)
+    copies = [pltpu.make_async_copy(wu_in, wu, local.at[0]), pltpu.make_async_copy(wd_in, wd, local.at[1])]
+    for copy in copies:
+        copy.start()
+    greet([me.core, me.xp])
+    post = Post(ss, rs)
+    att_copy = post.send(attended.at[far_rows], att_x, me.xp)
+    part = ds(width // 2 * k, width // 2)
+    wo_copy = post.send(wo.at[part], wo_x.at[part], me.xp)
+    middle[...] = (
+        x_own[here_rows, :].astype(f32) + out_bias[...] + dot_nt(attended[here_rows, :], wo[...])
+    )
+    post.got(wo_copy)
+    wo_core = post.send(wo_x.at[part], wo_x.at[part], me.core)
+    post.got(wo_core)
+    post.got(att_copy)
+    middle[...] += dot_nt(att_x[...], wo_x[...])
+    n2, s2 = row_norm(middle[...])
+    normed[...] = n2
+    inverse[...] = s2
+    low[here_rows, :] = (n2 * gain[...] + shift[...]).astype(bf16)
+    low_copy = post.send(low.at[here_rows], low.at[here_rows], me.xp)
+    for copy in copies:
+        copy.wait()
+    tile = 256
+
+    def feed(rows):
+        second[rows, :] = jnp.zeros((HALF, width), f32)
+
+        def step(j, carried):
+            shard, lanes = j // 3, pl.ds(pl.multiple_of(j % 3 * tile, 128), tile)
+            out = pl.ds(pl.multiple_of(j * tile, 128), tile)
+            pre = dot_nn(low[rows, :], wu[shard, :, lanes]) + bias[shard, 0:1, lanes]
+            below = 0.5 * (1.0 + lax.erf(pre * (2.0**-0.5)))
+            density = jnp.exp(-0.5 * pre * pre) * (2.0 * jnp.pi) ** -0.5
+            hidden[rows, out] = (pre * below).astype(bf16)
+            back = dot_nn(g_own[rows, :], wd[shard, :, lanes])
+            low_back = (back * (below + pre * density)).astype(bf16)
+            pre_grad[rows, out] = low_back
+            second[rows, :] += dot_nt(low_back, wu[shard, :, lanes])
+            return carried
+
+        lax.fori_loop(0, 6, step, 0)
+
+    def mlp(rows):
+        return dot_nt(hidden[rows, 0:width], wd[0]) + dot_nt(hidden[rows, width:], wd[1])
+
+    feed(here_rows)
+    post.got(low_copy)
+    feed(far_rows)
+    second_send[...] = second[far_rows, :].astype(bf16)
+    second_copy = post.send(second_send, second_x, me.xp)
+    mlp_send[...] = mlp(far_rows).astype(bf16)
+    mlp_copy = post.send(mlp_send, mlp_x, me.xp)
+
+    def weight_step(j, carried):
+        lanes = pl.ds(pl.multiple_of(j * tile, 128), tile)
+        g_up[:, lanes] = dot_tn(low[...], pre_grad[:, lanes]).astype(bf16)
+        g_down[:, lanes] = dot_tn(g_own[...], hidden[:, lanes]).astype(bf16)
+        return carried
+
+    lax.fori_loop(0, 6, weight_step, 0)
+    up_stats[0:1, :] = jnp.sum(pre_grad[:, 0:width].astype(f32), axis=0, keepdims=True)
+    up_stats[1:2, :] = jnp.sum(pre_grad[:, width:].astype(f32), axis=0, keepdims=True)
+    own_result = middle[...] + mlp(here_rows) + down_bias[...]
+    middle[...] = own_result
+    post.got(second_copy)
+    second_grad = second[here_rows, :] + second_x[...].astype(f32)
+    n2 = normed[...]
+    dy = g_own[here_rows, :].astype(f32)
+    stats[0:1, :] = jnp.sum(second_grad * n2, axis=0, keepdims=True)
+    stats[1:2, :] = jnp.sum(second_grad, axis=0, keepdims=True)
+    stats[2:3, :] = jnp.sum(dy, axis=0, keepdims=True)
+    grad = dy + norm_back(second_grad, n2, inverse[...], gain[...])
+    middle_grad[...] = grad
+    branch = grad.astype(bf16)
+    stats[3:4, :] = jnp.sum(branch.astype(f32), axis=0, keepdims=True)
+    da_send[...] = dot_nn(branch, wo_x[...]).astype(bf16)
+    da_copy = post.send(da_send, da.at[here_rows], me.xp)
+    da[here_rows, :] = dot_nn(branch, wo[...]).astype(bf16)
+    g_out_send[...] = dot_tn(branch, att_x[...]).astype(bf16)
+    g_out_copy = post.send(g_out_send, g_out_x, me.xp)
+    g_out_own = dot_tn(branch, attended[here_rows, :])
+    post.got(mlp_copy)
+    result_half[...] = (middle[...] + mlp_x[...].astype(f32)).astype(bf16)
+    post.got(g_out_copy)
+    g_out[...] = (g_out_own + g_out_x[...].astype(f32)).astype(bf16)
+    post.close()
+
+
+def middle_layer(fsdp_count, attended, wo, x_own, g_own, wu, wd, bias, gain, shift, out_bias, down_bias):
+    width = x_own.shape[1]
+    shape = jax.ShapeDtypeStruct
+    units = 2 * wu.shape[2]
+    return pl.pallas_call(
+        partial(middle_kernel, fsdp_count),
+        out_shape=(
+            shape((HALF, width), bf16),
+            shape((HALF, width), f32),
+            shape((OWN, 384), bf16),
+            shape((width, units), bf16),
+            shape((width, units), bf16),
+            shape((width, 384), bf16),
+            shape((4, width), f32),
+            shape((2, width), f32),
+        ),
+        in_specs=[VMEM] * 4 + [ANY] * 2 + [VMEM] * 5,
+        out_specs=(VMEM,) * 8,
+        scratch_shapes=[
+            pltpu.VMEM(wu.shape, bf16),
+            pltpu.VMEM(wd.shape, bf16),
+            pltpu.VMEM((HALF, 384), bf16),
+            pltpu.VMEM((width, 384), bf16),
+            pltpu.VMEM((HALF, width), f32),
+            pltpu.VMEM((HALF, width), f32),
+            pltpu.VMEM((HALF, 1), f32),
+            pltpu.VMEM((OWN, width), bf16),
+            pltpu.VMEM((OWN, units), bf16),
+            pltpu.VMEM((OWN, units), bf16),
+            pltpu.VMEM((OWN, width), f32),
+            pltpu.VMEM((HALF, width), bf16),
+            pltpu.VMEM((HALF, width), bf16),
+            pltpu.VMEM((HALF, width), bf16),
+            pltpu.VMEM((HALF, width), bf16),
+            pltpu.VMEM((HALF, 384), bf16),
+            pltpu.VMEM((width, 384), bf16),
+            pltpu.VMEM((width, 384), bf16),
+            pltpu.SemaphoreType.DMA((2,)),
+            pltpu.SemaphoreType.DMA((8,)),
+            pltpu.SemaphoreType.DMA((8,)),
+        ],
+        compiler_params=pltpu.CompilerParams(collective_id=1, has_side_effects=True, vmem_limit_bytes=LIMIT),
+        name="middle",
+    )(attended, wo, x_own, g_own, wu, wd, bias, gain, shift, out_bias, down_bias)
+
+
+def back_kernel(da, attended, q, k, v, kt, lse, dq, dkv, delta, st, dpt, pt, dst, dk_acc, dv_acc, dq_t):
+    product = (da[...].astype(f32) * attended[...].astype(f32)).T
+    for h in range(6):
+        delta[h : h + 1, :] = jnp.sum(product[h * HEAD_DIM : (h + 1) * HEAD_DIM], axis=0, keepdims=True)
+    dk_acc[...] = jnp.zeros_like(dk_acc)
+    dv_acc[...] = jnp.zeros_like(dv_acc)
+    lane = lax.broadcasted_iota(jnp.int32, (OWN, 128), 1) // HEAD_DIM
+
+    def head(h, carried):
+        slab, part = h // 2, h % 2
+        lanes = pl.ds(pl.multiple_of(slab * 128, 128), 128)
+        q_slab, da_slab = q[:, lanes], da[:, lanes]
+        q_part = jnp.where(lane == part, q_slab, jnp.zeros_like(q_slab))
+        da_part = jnp.where(lane == part, da_slab, jnp.zeros_like(da_slab))
+        st[0:TRUNK, :] = dot_nt(k[0:TRUNK, lanes], q_part)
+        dpt[0:TRUNK, :] = dot_nt(v[0:TRUNK, lanes], da_part)
+        for q_row, k_row, count in PIECES:
+            cols, rows = slice(q_row, q_row + BLOCK), slice(TRUNK, TRUNK + count)
+            st[rows, cols] = dot_nt(k[k_row : k_row + count, lanes], q_part[q_row : q_row + BLOCK])
+            dpt[rows, cols] = dot_nt(v[k_row : k_row + count, lanes], da_part[q_row : q_row + BLOCK])
+        log_total, row_delta = lse[pl.ds(h, 1), :], delta[pl.ds(h, 1), :]
+        for j in range(OWN // BLOCK):
+            cols = slice(j * BLOCK, (j + 1) * BLOCK)
+            count = TRUNK + (0 if j < 2 else PIECES[j - 2][2])
+            for r in range(0, count, BLOCK):
+                weight = jnp.exp(st[r : r + BLOCK, cols] - log_total[:, cols])
+                pt[r : r + BLOCK, cols] = weight.astype(bf16)
+                dst[r : r + BLOCK, cols] = (
+                    weight * (dpt[r : r + BLOCK, cols] - row_delta[:, cols])
+                ).astype(bf16)
+        dk_acc[0:TRUNK, lanes] += dot_nn(dst[0:TRUNK, :], q_part)
+        dv_acc[0:TRUNK, lanes] += dot_nn(pt[0:TRUNK, :], da_part)
+        head_rows = ds(h * HEAD_DIM, HEAD_DIM)
+        dq_t[head_rows, :] = dot_nn(kt[head_rows, 0:TRUNK], dst[0:TRUNK, :])
+        for q_row, k_row, count in PIECES:
+            cols, rows = slice(q_row, q_row + BLOCK), slice(TRUNK, TRUNK + count)
+            own = slice(k_row, k_row + count)
+            dk_acc[own, lanes] += dot_nn(dst[rows, cols], q_part[q_row : q_row + BLOCK])
+            dv_acc[own, lanes] += dot_nn(pt[rows, cols], da_part[q_row : q_row + BLOCK])
+            dq_t[head_rows, cols] += dot_nn(kt[head_rows, own], dst[rows, cols])
+        return carried
+
+    lax.fori_loop(0, 6, head, 0)
+    dq[...] = (dq_t[...].T * HEAD_DIM ** (-0.5)).astype(bf16)
+    dkv[:, 0:384] = dk_acc[...].astype(bf16)
+    dkv[:, 384:768] = dv_acc[...].astype(bf16)
+
+
+def back(da, attended, q, k, v, kt, lse):
+    shape = jax.ShapeDtypeStruct
+    tall = TRUNK + 2 * BLOCK
+    return pl.pallas_call(
+        back_kernel,
+        out_shape=(shape((OWN, 384), bf16), shape((KEYS, 768), bf16)),
+        in_specs=[VMEM] * 7,
+        out_specs=(VMEM, VMEM),
+        scratch_shapes=[
+            pltpu.VMEM((8, OWN), f32),
+            pltpu.VMEM((tall, OWN), f32),
+            pltpu.VMEM((tall, OWN), f32),
+            pltpu.VMEM((tall, OWN), bf16),
+            pltpu.VMEM((tall, OWN), bf16),
+            pltpu.VMEM((KEYS, 384), f32),
+            pltpu.VMEM((KEYS, 384), f32),
+            pltpu.VMEM((384, OWN), f32),
+        ],
+        compiler_params=pltpu.CompilerParams(vmem_limit_bytes=LIMIT),
+        name="back",
+    )(da, attended, q, k, v, kt, lse)
+
+
+UNIT = 32
+
+
+def finish_kernel(
+    fsdp_count, where, dq, dkv, wh, low_own, x_own, middle_grad, result_half, gain,
+    result, patch_grad, g_attn, stats, attn_stats,
+    trunk_core, trunk_far, trunk_send, trunk_y, dkv_own, first_send, first_x, all_rows, local, ss, rs,
+):
+    me = Here(fsdp_count)
+    c, x, k = me.c, me.x, me.k
+    s = 2 * c + k
+    pair = 2 * BLOCK
+    units = HALF // UNIT
+    mine, far = HALF * x, HALF * (1 - x)
+    here_rows, far_rows = ds(mine, HALF), ds(far, HALF)
+    greet([me.core, me.xp, me.yp])
+    post = Post(ss, rs)
+
+    all_rows[0, pl.ds(units * (2 * s + x), units)] = result_half[...].reshape(units, UNIT, -1)
+    far_core = post.send(dkv.at[ds(pair * (2 * (1 - c) + 1 - k), pair)], trunk_far, me.core)
+    own_core = post.send(dkv.at[ds(pair * (2 * c + 1 - k), pair)], trunk_core, me.core)
+    post.got(far_core)
+    trunk_send[...] = (
+        dkv[ds(pair * (2 * (1 - c) + k), pair), :].astype(f32) + trunk_far[...].astype(f32)
+    ).astype(bf16)
+    y_copy = post.send(trunk_send, trunk_y, me.yp)
+    dkv_own[pair:, :] = dkv[TRUNK:, :]
+    post.got(own_core)
+    post.got(y_copy)
+    dkv_own[0:pair, :] = (
+        dkv[ds(pair * s, pair), :].astype(f32) + trunk_core[...].astype(f32) + trunk_y[...].astype(f32)
+    ).astype(bf16)
+
+    def first(rows):
+        return (
+            dot_nt(dq[rows, :], wh[0])
+            + dot_nt(dkv_own[rows, 0:384], wh[1])
+            + dot_nt(dkv_own[rows, 384:768], wh[2])
+        )
+
+    first_send[...] = first(far_rows).astype(bf16)
+    first_copy = post.send(first_send, first_x, me.xp)
+    own_first = first(here_rows)
+    g_attn[0] = dot_tn(low_own[...], dq[...]).astype(bf16)
+    g_attn[1] = dot_tn(low_own[...], dkv_own[:, 0:384]).astype(bf16)
+    g_attn[2] = dot_tn(low_own[...], dkv_own[:, 384:768]).astype(bf16)
+    attn_stats[0:1, 0:384] = jnp.sum(dq[...].astype(f32), axis=0, keepdims=True)
+    attn_stats[0:1, 384:768] = jnp.sum(dkv_own[:, 384:768].astype(f32), axis=0, keepdims=True)
+    post.got(first_copy)
+    first_grad = own_first + first_x[...].astype(f32)
+    n1, s1 = row_norm(x_own[here_rows, :].astype(f32))
+    stats[0:1, :] = jnp.sum(first_grad * n1, axis=0, keepdims=True)
+    stats[1:2, :] = jnp.sum(first_grad, axis=0, keepdims=True)
+    grad = middle_grad[...] + norm_back(first_grad, n1, s1, gain[...])
+    all_rows[1, pl.ds(units * (2 * s + x), units)] = grad.astype(bf16).reshape(units, UNIT, -1)
+    there = (2 * s + 1 - x, 2 * (2 * (1 - c) + k) + x)
+    for index in (1, 0):
+        own = all_rows.at[index, pl.ds(units * (2 * s + x), units)]
+        from_x = post.send(own, own, me.xp)
+        from_y = post.send(own, own, me.yp)
+        post.send(own, own, me.core)
+        post.got(from_x)
+        quarter = units // 2
+        beside = all_rows.at[index, pl.ds(units * there[0], units)]
+        first_part = all_rows.at[index, pl.ds(units * there[0], quarter)]
+        diagonal = [post.send(first_part, first_part, me.yp)]
+        post.send(beside, beside, me.core)
+        post.got(from_y)
+        beyond = all_rows.at[index, pl.ds(units * there[1], units)]
+        last_part = all_rows.at[index, pl.ds(units * there[1] + quarter, units - quarter)]
+        diagonal.append(post.send(last_part, last_part, me.xp))
+        post.send(beyond, beyond, me.core)
+        for copy in diagonal:
+            post.got(copy)
+        corner = all_rows.at[index, pl.ds(units * (2 * (2 * (1 - c) + k) + 1 - x), units)]
+        post.send(corner, corner, me.core)
+    post.close()
+    for j in range(result.shape[0] // BLOCK):
+        first_unit = where[j]
+        to = slice(j * BLOCK, (j + 1) * BLOCK)
+        result[to, :] = all_rows[0, pl.ds(first_unit, BLOCK // UNIT)].reshape(BLOCK, -1)
+        patch_grad[to, :] = all_rows[1, pl.ds(first_unit, BLOCK // UNIT)].reshape(BLOCK, -1).astype(f32)
+
+
+def finish(fsdp_count, where, dq, dkv, wh, low_own, x_own, middle_grad, result_half, gain):
+    width = x_own.shape[1]
+    shape = jax.ShapeDtypeStruct
+    rows = where.shape[0] * BLOCK
+    pair = 2 * BLOCK
+    return pl.pallas_call(
+        partial(finish_kernel, fsdp_count),
+        out_shape=(
+            shape((rows, width), bf16),
+            shape((rows, width), f32),
+            shape((3, width, 384), bf16),
+            shape((2, width), f32),
+            shape((1, width), f32),
+        ),
+        in_specs=[SMEM] + [VMEM] * 8,
+        out_specs=(VMEM,) * 5,
+        scratch_shapes=[
+            pltpu.VMEM((pair, 768), bf16),
+            pltpu.VMEM((pair, 768), bf16),
+            pltpu.VMEM((pair, 768), bf16),
+            pltpu.VMEM((pair, 768), bf16),
+            pltpu.VMEM((OWN, 768), bf16),
+            pltpu.VMEM((HALF, width), bf16),
+            pltpu.VMEM((HALF, width), bf16),
+            pltpu.VMEM((2, 2 * rows // UNIT, UNIT, width), bf16),
+            pltpu.SemaphoreType.DMA((2,)),
+            pltpu.SemaphoreType.DMA((24,)),
+            pltpu.SemaphoreType.DMA((24,)),
+        ],
+        compiler_params=pltpu.CompilerParams(collective_id=2, has_side_effects=True, vmem_limit_bytes=LIMIT),
+        name="finish",
+    )(where, dq, dkv, wh, low_own, x_own, middle_grad, result_half, gain)
+
+
+def total_kernel(
+    fsdp_count, g_up, g_down, g_attn, g_out, all_stats, part_stats,
+    final, all_total, part_total,
+    packed, from_core, summed, from_y, strips, from_z, final_f32, stat_buf, stat_in, stat_z, ss, rs,
+):
+    me = Here(fsdp_count)
+    f, c, x, k = me.f, me.c, me.x, me.k
+    width = g_up.shape[0]
+    deep = width // fsdp_count
+    half = deep // 2
+    greet([me.core, me.xp, me.yp] + me.z)
+    post = Post(ss, rs)
+    for j in (0, 1):
+        packed[j, :, 0:768] = g_up[:, 768 * j : 768 * j + 768]
+        packed[j, :, 768:1536] = g_down[:, 768 * j : 768 * j + 768]
+        parts = [g_attn[0], g_attn[1], g_attn[2], g_out[...]]
+        lanes = slice(128 * j, 128 * j + 128)
+        tails = [p[:, 256 + 64 * j : 320 + 64 * j] for p in parts]
+        for i, p in enumerate(parts):
+            packed[j, :, 1536 + 128 * i : 1664 + 128 * i] = p[:, lanes]
+        packed[j, :, 2048:2176] = jnp.concatenate(tails[0:2], axis=1)
+        packed[j, :, 2176:2304] = jnp.concatenate(tails[2:4], axis=1)
+    core_copy = post.send(packed.at[1 - k], from_core, me.core)
+    rows_all, rows_part = all_stats.shape[0], part_stats.shape[0]
+    stat_buf[0:rows_all, :] = all_stats[...]
+    stat_buf[8 : 8 + rows_part, :] = part_stats[...]
+    stat_copy = post.send(stat_buf.at[pl.ds(0, 16)], stat_in.at[0], me.core)
+    post.got(stat_copy)
+    post.got(core_copy)
+
+    def add_core(j, carried):
+        rows = ds(j * half, half)
+        summed[rows, :] = (packed[k, rows, :].astype(f32) + from_core[rows, :].astype(f32)).astype(bf16)
+        return carried
+
+    lax.fori_loop(0, 2 * fsdp_count, add_core, 0)
+    y_copies = []
+    for g in range(fsdp_count):
+        y_copies.append(post.send(summed.at[ds(deep * g + half * (1 - c), half)], from_y.at[g], me.yp))
+    stat_buf[16:32, :] = stat_buf[0:16, :] + stat_in[0]
+    stat_copy = post.send(stat_buf.at[pl.ds(16, 16)], stat_in.at[1], me.yp)
+    for copy in y_copies:
+        post.got(copy)
+
+    def add_y(g, carried):
+        rows = ds(deep * g + half * c, half)
+        strips[g] = (summed[rows, :].astype(f32) + from_y[g].astype(f32)).astype(bf16)
+        return carried
+
+    lax.fori_loop(0, fsdp_count, add_y, 0)
+    z_copies = []
+    for i, device in enumerate(me.z):
+        z_copies.append(post.send(strips.at[(f + i + 1) % fsdp_count], from_z.at[i], device))
+    post.got(stat_copy)
+    stat_buf[32:48, :] = stat_buf[16:32, :] + stat_in[1]
+    stat_copy = post.send(stat_buf.at[pl.ds(32, 16)], stat_in.at[2], me.xp)
+    post.got(stat_copy)
+    stat_buf[48:56, :] = stat_buf[32:40, :] + stat_in[2, 0:8]
+    stat_buf[56:64, :] = stat_buf[40:48, :]
+    stat_z[f] = stat_buf[48:64, :]
+    stat_copies = []
+    for device in me.z:
+        stat_copies.append(post.send(stat_buf.at[pl.ds(48, 16)], stat_z.at[f], device))
+    for copy in z_copies:
+        post.got(copy)
+    final_f32[...] = strips[f].astype(f32)
+    for i in range(len(me.z)):
+        final_f32[...] += from_z[i].astype(f32)
+    final[c] = final_f32[...].astype(bf16)
+    post.send(final.at[c], final.at[c], me.yp)
+    for copy in stat_copies:
+        post.got(copy)
+    total = stat_z[0]
+    for g in range(1, fsdp_count):
+        total = total + stat_z[g]
+    all_total[...] = total[0:rows_all]
+    part_total[...] = total[8 : 8 + rows_part]
+    post.close()
+
+
+def totals(fsdp_count, g_up, g_down, g_attn, g_out, all_stats, part_stats):
+    width = g_up.shape[0]
+    wide = 2304
+    half = width // fsdp_count // 2
+    shape = jax.ShapeDtypeStruct
+    return pl.pallas_call(
+        partial(total_kernel, fsdp_count),
+        out_shape=(shape((2, half, wide), bf16), shape(all_stats.shape, f32), shape(part_stats.shape, f32)),
+        in_specs=[VMEM] * 6,
+        out_specs=(VMEM,) * 3,
+        scratch_shapes=[
+            pltpu.VMEM((2, width, wide), bf16),
+            pltpu.VMEM((width, wide), bf16),
+            pltpu.VMEM((width, wide), bf16),
+            pltpu.VMEM((fsdp_count, half, wide), bf16),
+            pltpu.VMEM((fsdp_count, half, wide), bf16),
+            pltpu.VMEM((fsdp_count - 1, half, wide), bf16),
+            pltpu.VMEM((half, wide), f32),
+            pltpu.VMEM((64, width), f32),
+            pltpu.VMEM((3, 16, width), f32),
+            pltpu.VMEM((fsdp_count, 16, width), f32),
+            pltpu.SemaphoreType.DMA((24,)),
+            pltpu.SemaphoreType.DMA((24,)),
+        ],
+        compiler_params=pltpu.CompilerParams(collective_id=3, has_side_effects=True, vmem_limit_bytes=LIMIT),
+        name="totals",
+    )(g_up, g_down, g_attn, g_out, all_stats, part_stats)
+
+
+def tree_shards(
+    fsdp_count, patches, out_grad, block_order, first_gain, first_shift, attn_proj, attn_bias, out_proj, out_bias,
+    second_gain, second_shift, up_proj, up_bias, down_proj, down_bias,
+):
+    row = lambda vector: vector.reshape(1, -1)
+    order = block_order[0]
+    slots = jnp.arange(order.shape[0], dtype=jnp.int32)
+    where = jnp.sum(jnp.where(order[None, :] == slots[:, None], slots[None, :], 0), axis=1, dtype=jnp.int32)
+    q, k, v = attn_proj[0], attn_proj[1], attn_proj[2]
+    out_t = out_proj.T
+    wa = jnp.concatenate(
+        [q[:, :128], k[:, :128], v[:, :128], q[:, 128:], k[:, 128:], v[:, 128:], out_t[:, 128:], out_t[:, :128]],
+        axis=1,
+    )
+    head_width = attn_bias.shape[1]
+    bias = jnp.zeros((8, up_bias.shape[0]), f32)
+    bias = bias.at[0].set(up_bias).at[1:3, :head_width].set(attn_bias)
+    rows_all, grads_all, wa, wu, wd, bias = gather(
+        fsdp_count, patches, out_grad, wa, up_proj, down_proj.T, bias
+    )
+    x_own, g_own, low_own, q, k, v, kt, attended, lse, wh = front(
+        where, rows_all, grads_all, wa, bias, row(first_gain), row(first_shift)
+    )
+    result_half, middle_grad, da, g_up, g_down, g_out, stats, up_stats = middle_layer(
+        fsdp_count, attended, wh[3], x_own, g_own, wu, wd, bias,
+        row(second_gain), row(second_shift), row(out_bias), row(down_bias),
+    )
+    dq, dkv = back(da, attended, q, k, v, kt, lse)
+    trunk, branch, leaf = order, order - TRUNK_BLK, order - TRUNK_BLK - BRANCHES
+    gathered = jnp.where(
+        order < TRUNK_BLK,
+        5 * (trunk // 2) + trunk % 2,
+        jnp.where(branch < BRANCHES, 5 * branch + 3, 5 * (leaf // 2) + 2 + 2 * (leaf % 2)),
+    )
+    own = patches.shape[0] // BLOCK
+    gathered = lax.dynamic_slice_in_dim(gathered, lax.axis_index("context") * own, own)
+    result, patch_grad, g_attn, first_stats, attn_stats = finish(
+        fsdp_count, gathered * (BLOCK // UNIT), dq, dkv, wh, low_own, x_own, middle_grad, result_half, row(first_gain)
+    )
+    final, all_total, part_total = totals(
+        fsdp_count, g_up, g_down, g_attn, g_out,
+        jnp.concatenate([first_stats, stats], axis=0), jnp.concatenate([up_stats, attn_stats], axis=0),
+    )
+    final = final.reshape(-1, final.shape[2]).astype(f32)
+    slab = lambda i: final[:, 1536 + 128 * i : 1664 + 128 * i]
+    half_slab = lambda i: final[:, 2048 + 64 * i : 2112 + 64 * i]
+    joined = [jnp.concatenate([slab(i), half_slab(i)], axis=1) for i in range(4)]
+    core = lax.axis_index("tensor") % 2
+    part_total = part_total.reshape(-1)
+    up_total = lax.dynamic_slice_in_dim(part_total, core * 768, 768)
+    attn_total = part_total[1536:].reshape(2, 384)
+    attn_total = jnp.concatenate(
+        [
+            lax.dynamic_slice_in_dim(attn_total, core * 128, 128, 1),
+            lax.dynamic_slice_in_dim(attn_total, 256 + core * 64, 64, 1),
+        ],
+        axis=1,
+    )
+    return (
+        result,
+        patch_grad,
+        all_total[0],
+        all_total[1],
+        jnp.stack(joined[0:3]),
+        attn_total,
+        joined[3].T,
+        all_total[5],
+        all_total[2],
+        all_total[3],
+        final[:, 0:768],
+        up_total,
+        final[:, 768:1536].T,
+        all_total[4],
+    )
+
+
 def solution(mesh):
+    fits = mesh.shape["context"] * 2 == BRANCHES and mesh.shape["tensor"] == 4 and mesh.shape["fsdp"] == 4
+    body = partial(tree_shards, mesh.shape["fsdp"]) if fits else shards
     return jax.shard_map(
-        shards,
+        body,
         mesh=mesh,
         in_specs=(
             P(("fsdp", "context"), None),

time: 960 us -> 474 us (0.49)
  waiting for transfers between devices: 520 us -> 0 us
  Pallas kernels: 0 us -> 441 us
  matrix products: 149 us -> 0 us
  blocking collectives: 120 us -> 0 us
  other arithmetic: 79.7 us -> 6.62 us
  local copies, waits for them, and re-layouts: 63.8 us -> 17.8 us
  between operations: 16.4 us -> 0.89 us
    pallas_call x0 -> x6, Pallas kernels: none -> 441 us  [the longest x1 154 us: gather(): pl.pallas_call(partial(gather_kernel, fsdp_count), out_shape=(whole, whol...]
    psum x4 -> x0, waiting for transfers between devices: 274 us -> none  [the longest x1 79.9 us: shards(): middle = inputs + (lax.psum(attn_part, 'tensor') + out_bias)]
    reduce_scatter x3 -> x0, waiting for transfers between devices: 164 us -> none  [the longest x1 65.3 us: shards(): lax.psum_scatter(grad_down, ('fsdp', 'context'), scatter_dimension=1, til...]
    dot_general x55 -> x0, matrix products: 143 us -> none  [the longest x15 27.9 us: scores_of(): jnp.einsum('qhd,khd->hqk', query_heads, key_heads, preferred_element_type...]
    all_gather x6 -> x0, blocking collectives: 81.9 us -> none  [the longest x1 31.5 us: shards(): lax.all_gather(attn_proj, 'fsdp', axis=1, tiled=True)]
    unnamed x14 -> x0, waiting for transfers between devices: 70.9 us -> none
    psum x1 -> x0, blocking collectives: 38 us -> none  [shards(): lax.psum((grad_first_gain, grad_first_shift, grad_attn_bias, grad_out_bia...]
    reduce_sum x14 -> x1, other arithmetic: 34 us -> 0.63 us  [tree_shards(): jnp.sum(jnp.where(order[None, :] == slots[:, None], slots[None, :], 0), a...]
  transfers between devices with their start and end apart: 12 -> 0, of which waited for: 10 -> 0; matrix products, arithmetic and copies ran while one was open for 7% -> 0% of each run, Pallas kernels for 0% -> 0%
where the time goes in v1:
time: 474 us; the launch traced here: 467 us
  Pallas kernels  441 us (93%)
  local copies, waits for them, and re-layouts  17.8 us (4%)
  other arithmetic  6.62 us (1%)
    pallas_call x1, Pallas kernels, gather(): pl.pallas_call(partial(gather_kernel, fsdp_count), out_shape=(whole, whol...  154 us
    pallas_call x1, Pallas kernels, totals(): pl.pallas_call(partial(total_kernel, fsdp_count), out_shape=(shape((2, ha...  97.5 us
    pallas_call x1, Pallas kernels, middle_layer(): pl.pallas_call(partial(middle_kernel, fsdp_count), out_shape=(shape((HALF...  79.5 us
    pallas_call x1, Pallas kernels, finish(): pl.pallas_call(partial(finish_kernel, fsdp_count), out_shape=(shape((rows...  71.4 us
    pallas_call x1, Pallas kernels, front(): pl.pallas_call(front_kernel, out_shape=(shape((OWN, width), bf16), shape(...  21.4 us
    pallas_call x1, Pallas kernels, back(): pl.pallas_call(back_kernel, out_shape=(shape((OWN, 384), bf16), shape((KE...  17.6 us

profile of v1, /device:TPU:0, one launch (start us, length us, event | category | flops | bytes accessed | tf_op | source)
XLA Modules:
  0.0 466.7 jit_solution(4812217832508856744)
XLA Ops:
  0.7 1.0 slice_bitcast_fusion.2
  1.8 1.0 copy.31
  2.8 0.8 concatenate.28.wa
  4.1 0.6 copy-done.1
  4.7 154.0 %gather.1 = (bf16[2560,768]{1,0:T(8,128)(2,1)}, bf16[2560,768]{1,0:T(8,128)(2,1)}, bf16[2,768,768]{2,1,0:T(8,128)(2,1)}, bf16[2,768,768]{2,1,0:T(8,128)(2,1)}, b...) custom-call(bf16[1280,768]{1,0:T(8,128)(2,1)} %patches.1, bf16[1280,768]{1,0:T(8,128)(2,1)} %grads.1, ...), custom_call_target="tpu_custom_call" | custom-call | tf_op jit(solution)/shard_map/gather/pallas_call | solution.py:456
  159.9 0.6 select_reduce_fusion.where
  160.5 21.4 %front.1 = (bf16[640,768]{1,0:T(8,128)(2,1)}, bf16[640,768]{1,0:T(8,128)(2,1)}, bf16[640,768]{1,0:T(8,128)(2,1)}, bf16[640,384]{1,0:T(8,128)(2,1)}, bf16[1408,38...) custom-call(s32[20]{0:T(128)} %select_reduce_fusion.where, ...), custom_call_target="tpu_custom_call" | custom-call | tf_op jit(solution)/shard_map/front/pallas_call | solution.py:586
  181.9 1.9 slice_bitcast_fusion.1.wo
  186.2 79.5 %middle.1 = (bf16[320,768]{1,0:T(8,128)(2,1)}, f32[320,768]{1,0:T(8,128)}, bf16[640,384]{1,0:T(8,128)(2,1)}, bf16[768,1536]{1,0:T(8,128)(2,1)}, bf16[768,1536]{1...) custom-call(bf16[640,384]{1,0:T(8,128)(2,1)} %get-tuple-element.76.attended, ...), custom_call_target="tpu_custom_call" | custom-call | tf_op jit(solution)/shard_map/middle/pallas_call | solution.py:721
  265.7 17.6 %back.1 = (bf16[640,384]{1,0:T(8,128)(2,1)}, bf16[1408,768]{1,0:T(8,128)(2,1)}) custom-call(bf16[640,384]{1,0:T(8,128)(2,1)} %get-tuple-element.82.da, bf16[640,384]{1,0:T(8,128)(2,1)} %get-tuple-element.76.attended, bf16[640,384]{1,0:T(8,128)(2,1)} %get-tuple-element.83.q, bf16[1408,384]{1,0:T(8,128)(2,1)} %get-tuple-element.84.k, ...), custom_call_target="tpu_custom_call" | custom-call | tf_op jit(solution)/shard_map/back/pallas_call | solution.py:814
  283.2 0.6 dynamic-slice_multiply_fusion.where
  283.8 71.4 %finish.1 = (bf16[1280,768]{1,0:T(8,128)(2,1)}, f32[1280,768]{1,0:T(8,128)}, bf16[3,768,384]{2,1,0:T(8,128)(2,1)}, f32[2,768]{1,0:T(2,128)}, f32[1,768]{1,0:T(1,128)}) custom-call(s32[10]{0:T(128)} %dynamic-slice_multiply_fusion.where, bf16[640,384]{1,0:T(8,128)(2,1)} %get-tuple-element.88.dq, bf16[1408,768]{1,0:T(8,128)(2,1)} %get-tuple-element.89.dkv, ...), custom_call_target="tpu_custom_call" | custom-call | tf_op jit(solution)/shard_map/finish/pallas_call | solution.py:923
  355.3 1.3 pad_maximum_fusion.2.part_stats
  356.5 1.3 pad_maximum_fusion.1.all_stats
  357.9 97.5 %totals.1 = (bf16[2,96,2304]{2,1,0:T(8,128)(2,1)}, f32[6,768]{1,0:T(8,128)}, f32[3,768]{1,0:T(4,128)}) custom-call(bf16[768,1536]{1,0:T(8,128)(2,1)} %get-tuple-element.95.g_up, bf16[768,1536]{1,0:T(8,128)(2,1)} %get-tuple-element.96.g_down, bf16[3,768,384]{2,1,0:T(8,128)(2,1)} %get-tuple-element.97.g_attn, bf16[768,384]{1,0:T(8,128)(2,1)} %get-tuple-element.98.g_out, ...), custom_call_target="tpu_custom_call" | custom-call | tf_op jit(solution)/shard_map/totals/pallas_call | solution.py:1037
  455.4 1.3 bitcast_convert_fusion
  456.9 0.8 copy.32
  457.7 0.6 slice_reduce_fusion
  458.4 0.6 pad_maximum_fusion.3
  459.1 0.9 pad_maximum_fusion
  459.9 1.1 slice_bitcast_fusion
  461.0 0.7 dynamic_slice.15
  461.7 3.1 copy.36
  464.8 1.9 copy.37
  (56 shorter events, 4.3 us)
Async XLA Ops:
  0.6 3.0 copy-start.6
  0.7 3.0 copy-start.13
  4.1 0.6 copy-start.1
  4.7 154.0 %copy-start.7 = (f32[768]{0:T(1024)S(1)}, f32[768]{0:T(1024)}, u32[]{:S(2)}) copy-start(f32[768]{0:T(1024)} %param.22) | copy-start | bytes 9220
  4.7 154.6 %copy-start.8 = (f32[768]{0:T(1024)S(1)}, f32[768]{0:T(1024)}, u32[]{:S(2)}) copy-start(f32[768]{0:T(1024)} %param.23) | copy-start | bytes 9220
  4.7 155.2 %copy-start.14 = (s32[1,20]{1,0:T(1,128)S(1)}, s32[1,20]{1,0:T(1,128)}, u32[]{:S(2)}) copy-start(s32[1,20]{1,0:T(1,128)} %param.21) | copy-start | bytes 244
  160.5 23.4 %copy-start.9 = (f32[768]{0:T(1024)S(1)}, f32[768]{0:T(1024)}, u32[]{:S(2)}) copy-start(f32[768]{0:T(1024)} %param.28) | copy-start | bytes 9220
  160.5 23.9 %copy-start.10 = (f32[768]{0:T(1024)S(1)}, f32[768]{0:T(1024)}, u32[]{:S(2)}) copy-start(f32[768]{0:T(1024)} %param.29) | copy-start | bytes 9220
  160.5 24.5 %copy-start.11 = (f32[768]{0:T(1024)S(1)}, f32[768]{0:T(1024)}, u32[]{:S(2)}) copy-start(f32[768]{0:T(1024)} %param.27) | copy-start | bytes 9220
  160.5 25.1 %copy-start.12 = (f32[768]{0:T(1024)S(1)}, f32[768]{0:T(1024)}, u32[]{:S(2)}) copy-start(f32[768]{0:T(1024)} %param.33) | copy-start | bytes 9220
  283.8 71.4 %copy-start.5 = (f32[2,768]{1,0:T(2,128)S(1)}, f32[2,768]{1,0:T(2,128)}, u32[]{:S(2)}) copy-start(f32[2,768]{1,0:T(2,128)} %get-tuple-element.101) | copy-start | bytes 18436
  283.8 72.7 %copy-start.4 = (f32[4,768]{1,0:T(4,128)S(1)}, f32[4,768]{1,0:T(4,128)}, u32[]{:S(2)}) copy-start(f32[4,768]{1,0:T(4,128)} %get-tuple-element.100) | copy-start | bytes 36868
  455.4 2.3 copy-start.2
  455.4 2.3 copy-start.3
  461.7 3.1 copy-start

commit v2 on v0

--- a/solution.py
+++ b/solution.py
@@ -3,6 +3,8 @@
 import jax
 import jax.numpy as jnp
 from jax import lax
+from jax.experimental import pallas as pl
+from jax.experimental.pallas import tpu as pltpu
 from jax.sharding import PartitionSpec as P
 
 HEAD_DIM = 64
@@ -298,9 +300,1011 @@
     )
 
 
+bf16 = jnp.bfloat16
+f32 = jnp.float32
+VMEM = pl.BlockSpec(memory_space=pltpu.VMEM)
+SMEM = pl.BlockSpec(memory_space=pltpu.SMEM)
+ANY = pl.BlockSpec(memory_space=pl.ANY)
+MESH = pl.DeviceIdType.MESH
+LIMIT = 60 * 1024 * 1024
+
+
+def dot_nn(a, b):
+    return lax.dot_general(a, b, (((1,), (0,)), ((), ())), preferred_element_type=f32)
+
+
+def dot_nt(a, b):
+    return lax.dot_general(a, b, (((1,), (1,)), ((), ())), preferred_element_type=f32)
+
+
+def dot_tn(a, b):
+    return lax.dot_general(a, b, (((0,), (0,)), ((), ())), preferred_element_type=f32)
+
+
+class Here:
+    def __init__(self, fsdp_count):
+        self.f = lax.axis_index("fsdp")
+        self.c = lax.axis_index("context")
+        self.t = lax.axis_index("tensor")
+        self.x = self.t // 2
+        self.k = self.t % 2
+        self.core = (self.f, self.c, 2 * self.x + 1 - self.k)
+        self.xp = (self.f, self.c, 2 * (1 - self.x) + self.k)
+        self.yp = (self.f, 1 - self.c, self.t)
+        self.z = [((self.f + i) % fsdp_count, self.c, self.t) for i in range(1, fsdp_count)]
+        self.back = [(self.f + fsdp_count - i) % fsdp_count for i in range(1, fsdp_count)]
+
+
+def greet(devices):
+    barrier = pltpu.get_barrier_semaphore()
+    for device in devices:
+        pl.semaphore_signal(barrier, inc=1, device_id=device, device_id_type=MESH)
+    pl.semaphore_wait(barrier, len(devices))
+
+
+class Post:
+    def __init__(self, send_sem, recv_sem):
+        self.send_sem, self.recv_sem = send_sem, recv_sem
+        self.sent, self.open = [], []
+
+    def send(self, src, dst, device):
+        index = len(self.sent)
+        copy = pltpu.make_async_remote_copy(
+            src_ref=src,
+            dst_ref=dst,
+            send_sem=self.send_sem.at[index],
+            recv_sem=self.recv_sem.at[index],
+            device_id=device,
+            device_id_type=MESH,
+        )
+        copy.start()
+        self.sent.append(copy)
+        self.open.append((copy, device))
+        return copy
+
+    def got(self, copy):
+        copy.wait_recv()
+        self.open = [entry for entry in self.open if entry[0] is not copy]
+
+    def got_from(self, device):
+        for copy, to in self.open:
+            if to is device:
+                self.got(copy)
+
+    def close(self):
+        for copy, _ in self.open:
+            copy.wait_recv()
+        for copy in self.sent:
+            copy.wait_send()
+
+
+def ds(start, size, step=16):
+    return pl.ds(pl.multiple_of(start, step), size)
+
+
+TRUNK = TRUNK_BLK * BLOCK
+SUB = (1 + LEAVES) * BLOCK
+KEYS = TRUNK + SUB
+OWN = 2 * BLOCK + SUB
+PIECES = (
+    (2 * BLOCK, TRUNK, 2 * BLOCK),
+    (3 * BLOCK, TRUNK + BLOCK, BLOCK),
+    (4 * BLOCK, TRUNK + BLOCK, 2 * BLOCK),
+)
+
+
+def own_places(s):
+    return [2 * s, 2 * s + 1, 12 + 2 * s, 8 + s, 13 + 2 * s]
+
+
+def row_norm(values):
+    center = values - jnp.mean(values, axis=1, keepdims=True)
+    inverse = lax.rsqrt(jnp.mean(center * center, axis=1, keepdims=True) + epsilon)
+    return center * inverse, inverse
+
+HALF = OWN // 2
+UNIT = 32
+
+
+def first_kernel(
+    fsdp_count, where, patches, grads, attn_proj, out_proj, up, down, bias, gain1, shift1, gain2, shift2, out_bias, down_bias,
+    q_out, k_out, v_out, kt_out, att_out, low_out, x_out, wh_out, g_up_out, g_down_out,
+    lse, da, middle_grad, mlp_own, mlp_send, g_out_own, g_out_send, stats, up_stats,
+    a_own, d_own, rows_all, grads_all, wa, wh, wo_x, wu, wd, bias_all,
+    low, low_own, x_own, g_own, q, k, v, kt, vt, attended, att_t, att_x, st, pt,
+    middle, normed, inverse, low2, hidden, pre_grad, second, second_send, second_x, da_send, g_up, g_down,
+    local, ss, rs,
+):
+    me = Here(fsdp_count)
+    f, c, x, core, t = me.f, me.c, me.x, me.k, me.t
+    s = 2 * c + core
+    units = patches.shape[0]
+    part = units // 4
+    width = patches.shape[2]
+    deep = up.shape[0]
+    half = deep // 2
+    head_width = attn_proj.shape[2]
+    early = 640
+    own_copies = []
+
+    def keep(src, dst):
+        copy = pltpu.make_async_copy(src, dst, local.at[len(own_copies)])
+        copy.start()
+        own_copies.append(copy)
+
+    keep(patches, rows_all.at[pl.ds(units * c, units)])
+    keep(grads, grads_all.at[pl.ds(units * c, units)])
+    keep(up, wu.at[core, ds(deep * f, deep)])
+    a_own[:, 0:128] = attn_proj[0, :, 0:128]
+    a_own[:, 128:256] = attn_proj[1, :, 0:128]
+    a_own[:, 256:384] = attn_proj[2, :, 0:128]
+    out_t = out_proj[...].T
+    a_own[:, 384:512] = jnp.concatenate([attn_proj[0, :, 128:head_width], attn_proj[1, :, 128:head_width]], axis=1)
+    a_own[:, 512:640] = jnp.concatenate([attn_proj[2, :, 128:head_width], out_t[:, 128:head_width]], axis=1)
+    a_own[:, 640:768] = out_t[:, 0:128]
+    greet([me.core, me.xp, me.yp] + me.z)
+    post = Post(ss, rs)
+    there = units * (1 - c)
+    strip, other_strip = half * c, half * (1 - c)
+
+    def quarter(array, index, piece, count=2):
+        size = part // count
+        return array.at[pl.ds(there + part * index + size * piece, size)]
+
+    def to_y(src, dst, piece, count=2):
+        size = part // count
+        return post.send(
+            src.at[pl.ds(part * t + size * piece, size)],
+            dst.at[pl.ds(units * c + part * t + size * piece, size)],
+            me.yp,
+        )
+
+    def relay(piece, device):
+        return post.send(piece, piece, device)
+
+    a_dst = lambda shard, row, lanes: wa.at[shard, ds(row, half), lanes]
+    lo, hi = pl.ds(0, early), pl.ds(early, width - early)
+    patches_y = [to_y(patches, rows_all, i) for i in range(2)]
+    a1_z = [
+        post.send(a_own.at[ds(strip, half), lo], a_dst(core, deep * f + strip, lo), device) for device in me.z
+    ]
+    a_core = post.send(a_own, wa.at[core, ds(deep * f, deep)], me.core)
+    bias_core = post.send(bias, bias_all.at[core], me.core)
+    u_core = post.send(up, wu.at[core, ds(deep * f, deep)], me.core)
+    wa[core, ds(deep * f, deep), :] = a_own[...]
+    bias_all[core] = bias[...]
+    d_own[...] = down[...].T
+    wd[core, ds(deep * f, deep), :] = d_own[...]
+    d_core = post.send(d_own, wd.at[core, ds(deep * f, deep)], me.core)
+    patches_x = []
+    for i in range(2):
+        post.got(patches_y[i])
+        patches_x.append(relay(quarter(rows_all, t, i), me.xp))
+        relay(quarter(rows_all, t, i), me.core)
+    a1_y = []
+    for copy, source in zip(a1_z, me.back):
+        post.got(copy)
+        piece = a_dst(core, deep * source + strip, lo)
+        a1_y.append(relay(piece, me.yp))
+        relay(piece, me.core)
+    a2_z = [
+        post.send(a_own.at[ds(strip, half), hi], a_dst(core, deep * f + strip, hi), device) for device in me.z
+    ]
+    u_z = [
+        post.send(up.at[ds(strip, half)], wu.at[core, ds(deep * f + strip, half)], device) for device in me.z
+    ]
+    over = (t + 2) % 4
+    for i in range(2):
+        post.got(patches_x[i])
+        relay(quarter(rows_all, over, i), me.core)
+    post.got_from(me.core)
+    own_copies[0].wait()
+
+    gain_row, shift_row = gain1[...], shift1[...]
+
+    def block_of(array, place):
+        return array[pl.ds(where[place], BLOCK // UNIT)].reshape(BLOCK, width)
+
+    def norm_block(place, row):
+        normed_rows, _ = row_norm(block_of(rows_all, place).astype(f32))
+        low[ds(row, BLOCK), :] = (normed_rows * gain_row + shift_row).astype(bf16)
+
+    def trunk_step(j, carried):
+        norm_block(j, j * BLOCK)
+        return carried
+
+    lax.fori_loop(0, TRUNK_BLK, trunk_step, 0)
+    places = own_places(s)
+    for j in range(2, 5):
+        norm_block(places[j], TRUNK + (j - 2) * BLOCK)
+    for j, place in enumerate(places):
+        x_own[pl.ds(j * BLOCK, BLOCK), :] = block_of(rows_all, place)
+    low_own[0 : 2 * BLOCK, :] = low[ds(2 * BLOCK * s, 2 * BLOCK), :]
+    low_own[2 * BLOCK :, :] = low[TRUNK:, :]
+    for copy, source in zip(a1_y, me.back):
+        post.got(copy)
+        relay(a_dst(core, deep * source + other_strip, lo), me.core)
+    grads_y = [to_y(grads, grads_all, i) for i in range(2)]
+    post.got_from(me.core)
+
+    def assemble(i):
+        slab = (0, 1, 2, 5)[i]
+        wh[i, :, 0:128] = wa[0, :, 128 * slab : 128 * slab + 128]
+        wh[i, :, 128:256] = wa[1, :, 128 * slab : 128 * slab + 128]
+        start = 384 + 64 * i
+        wh[i, :, 256:384] = jnp.concatenate(
+            [wa[0, :, start : start + 64], wa[1, :, start : start + 64]], axis=1
+        )
+
+    for i in range(3):
+        assemble(i)
+
+    def heads_row(row):
+        a, b = bias_all[0, row : row + 1, :], bias_all[1, row : row + 1, :]
+        return jnp.concatenate([a[:, 0:128], b[:, 0:128], a[:, 128:192], b[:, 128:192]], axis=1)
+
+    q[...] = ((dot_nn(low_own[...], wh[0]) + heads_row(1)).astype(bf16) * HEAD_DIM ** (-0.5)).astype(bf16)
+    value_bias = heads_row(2)
+
+    def project(j, carried):
+        rows = ds(j * (KEYS // 2), KEYS // 2)
+        k[rows, :] = dot_nn(low[rows, :], wh[1]).astype(bf16)
+        v[rows, :] = (dot_nn(low[rows, :], wh[2]) + value_bias).astype(bf16)
+        return carried
+
+    lax.fori_loop(0, 2, project, 0)
+    kt[...] = k[...].T
+    vt[...] = v[...].T
+    for src, dst in ((q, q_out), (k, k_out), (v, v_out), (kt, kt_out), (low_own, low_out), (x_own, x_out)):
+        keep(src, dst)
+    lane = lax.broadcasted_iota(jnp.int32, (OWN, 128), 1) // HEAD_DIM
+
+    def head(h, carried):
+        slab, side = h // 2, h % 2
+        lanes = pl.ds(pl.multiple_of(slab * 128, 128), 128)
+        own_q = q[:, lanes]
+        q_part = jnp.where(lane == side, own_q, jnp.zeros_like(own_q))
+        st[0:TRUNK, :] = dot_nt(k[0:TRUNK, lanes], q_part)
+        for q_row, k_row, count in PIECES:
+            st[TRUNK : TRUNK + count, q_row : q_row + BLOCK] = dot_nt(
+                k[k_row : k_row + count, lanes], q_part[q_row : q_row + BLOCK]
+            )
+        tops, sums = [], []
+        for j in range(OWN // BLOCK):
+            cols = slice(j * BLOCK, (j + 1) * BLOCK)
+            count = TRUNK + (0 if j < 2 else PIECES[j - 2][2])
+            top = jnp.full((8, BLOCK), far_below, f32)
+            for r in range(0, count, BLOCK):
+                piece = st[r : r + BLOCK, cols].reshape(BLOCK // 8, 8, BLOCK)
+                top = jnp.maximum(top, jnp.max(piece, axis=0))
+            top = jnp.max(top, axis=0, keepdims=True)
+            total = jnp.zeros((8, BLOCK), f32)
+            for r in range(0, count, BLOCK):
+                weight = jnp.exp(st[r : r + BLOCK, cols] - top)
+                total = total + jnp.sum(weight.reshape(BLOCK // 8, 8, BLOCK), axis=0)
+                pt[r : r + BLOCK, cols] = weight.astype(bf16)
+            tops.append(top)
+            sums.append(jnp.sum(total, axis=0, keepdims=True))
+        total = jnp.concatenate(sums, axis=1)
+        head_rows = ds(h * HEAD_DIM, HEAD_DIM)
+        att_t[head_rows, :] = dot_nn(vt[head_rows, 0:TRUNK], pt[0:TRUNK, :])
+        for q_row, k_row, count in PIECES:
+            cols = slice(q_row, q_row + BLOCK)
+            att_t[head_rows, cols] += dot_nn(
+                vt[head_rows, k_row : k_row + count], pt[TRUNK : TRUNK + count, cols]
+            )
+        att_t[head_rows, :] = att_t[head_rows, :] / total
+        lse[pl.ds(h, 1), :] = jnp.concatenate(tops, axis=1) + jnp.log(total)
+        return carried
+
+    lax.fori_loop(0, 2, head, 0)
+    a2_y, u_y, grads_x = [], [], []
+    for copy, source in zip(a2_z, me.back):
+        post.got(copy)
+        piece = a_dst(core, deep * source + strip, hi)
+        a2_y.append(relay(piece, me.yp))
+        relay(piece, me.core)
+    post.got(grads_y[0])
+    grads_x.append(relay(quarter(grads_all, t, 0), me.xp))
+    relay(quarter(grads_all, t, 0), me.core)
+    for copy, source in zip(u_z, me.back):
+        post.got(copy)
+        piece = wu.at[core, ds(deep * source + strip, half)]
+        u_y.append(relay(piece, me.yp))
+        relay(piece, me.core)
+    d_z = [
+        post.send(d_own.at[ds(strip, half)], wd.at[core, ds(deep * f + strip, half)], device) for device in me.z
+    ]
+    lax.fori_loop(2, 4, head, 0)
+    post.got(grads_y[1])
+    grads_x.append(relay(quarter(grads_all, t, 1), me.xp))
+    relay(quarter(grads_all, t, 1), me.core)
+    for copy, source in zip(a2_y, me.back):
+        post.got(copy)
+        relay(a_dst(core, deep * source + other_strip, hi), me.core)
+    lax.fori_loop(4, 6, head, 0)
+    attended[...] = att_t[...].T.astype(bf16)
+    mine, far = HALF * x, HALF * (1 - x)
+    here_rows, far_rows = ds(mine, HALF), ds(far, HALF)
+    att_copy = post.send(attended.at[far_rows], att_x, me.xp)
+    keep(attended, att_out)
+    post.got_from(me.core)
+    assemble(3)
+    keep(wh, wh_out)
+    wo_rows = ds(width // 2 * core, width // 2)
+    wo_copy = post.send(wh.at[3, wo_rows], wo_x.at[wo_rows], me.xp)
+    middle[...] = (
+        x_own[here_rows, :].astype(f32) + out_bias[...] + dot_nt(attended[here_rows, :], wh[3])
+    )
+    d_y = []
+    for copy, source in zip(d_z, me.back):
+        post.got(copy)
+        piece = wd.at[core, ds(deep * source + strip, half)]
+        d_y.append(relay(piece, me.yp))
+        relay(piece, me.core)
+    post.got(wo_copy)
+    relay(wo_x.at[wo_rows], me.core)
+    for i in range(2):
+        post.got(grads_x[i])
+        relay(quarter(grads_all, over, i), me.core)
+    post.got_from(me.core)
+    post.got(att_copy)
+    middle[...] += dot_nt(att_x[...], wo_x[...])
+    n2, s2 = row_norm(middle[...])
+    normed[...] = n2
+    inverse[...] = s2
+    low2[here_rows, :] = (n2 * gain2[...] + shift2[...]).astype(bf16)
+    low_copy = post.send(low2.at[here_rows], low2.at[here_rows], me.xp)
+    own_copies[1].wait()
+    for j, place in enumerate(places):
+        g_own[pl.ds(j * BLOCK, BLOCK), :] = block_of(grads_all, place)
+    for copy, source in zip(u_y, me.back):
+        post.got(copy)
+        relay(wu.at[core, ds(deep * source + other_strip, half)], me.core)
+    for copy, source in zip(d_y, me.back):
+        post.got(copy)
+        relay(wd.at[core, ds(deep * source + other_strip, half)], me.core)
+    post.got_from(me.core)
+    own_copies[2].wait()
+    tile = 256
+
+    def feed(rows):
+        second[rows, :] = jnp.zeros((HALF, width), f32)
+
+        def step(j, carried):
+            shard, lanes = j // 3, pl.ds(pl.multiple_of(j % 3 * tile, 128), tile)
+            out = pl.ds(pl.multiple_of(j * tile, 128), tile)
+            pre = dot_nn(low2[rows, :], wu[shard, :, lanes]) + bias_all[shard, 0:1, lanes]
+            below = 0.5 * (1.0 + lax.erf(pre * (2.0**-0.5)))
+            density = jnp.exp(-0.5 * pre * pre) * (2.0 * jnp.pi) ** -0.5
+            hidden[rows, out] = (pre * below).astype(bf16)
+            back = dot_nn(g_own[rows, :], wd[shard, :, lanes])
+            low_back = (back * (below + pre * density)).astype(bf16)
+            pre_grad[rows, out] = low_back
+            second[rows, :] += dot_nt(low_back, wu[shard, :, lanes])
+            return carried
+
+        lax.fori_loop(0, 6, step, 0)
+
+    def mlp(rows):
+        return dot_nt(hidden[rows, 0:width], wd[0]) + dot_nt(hidden[rows, width:], wd[1])
+
+    feed(here_rows)
+    post.got(low_copy)
+    feed(far_rows)
+    second_send[...] = second[far_rows, :].astype(bf16)
+    second_copy = post.send(second_send, second_x, me.xp)
+
+    def weight_step(j, carried):
+        lanes = pl.ds(pl.multiple_of(j * tile, 128), tile)
+        g_up[:, lanes] = dot_tn(low2[...], pre_grad[:, lanes]).astype(bf16)
+        g_down[:, lanes] = dot_tn(g_own[...], hidden[:, lanes]).astype(bf16)
+        return carried
+
+    lax.fori_loop(0, 6, weight_step, 0)
+    keep(g_up, g_up_out)
+    keep(g_down, g_down_out)
+    up_stats[0:1, :] = jnp.sum(pre_grad[:, 0:width].astype(f32), axis=0, keepdims=True)
+    up_stats[1:2, :] = jnp.sum(pre_grad[:, width:].astype(f32), axis=0, keepdims=True)
+    mlp_send[...] = mlp(far_rows).astype(bf16)
+    mlp_own[...] = middle[...] + mlp(here_rows) + down_bias[...]
+    dy = g_own[here_rows, :].astype(f32)
+    stats[2:3, :] = jnp.sum(dy, axis=0, keepdims=True)
+    post.got(second_copy)
+    second_grad = second[here_rows, :] + second_x[...].astype(f32)
+    n2 = normed[...]
+    stats[0:1, :] = jnp.sum(second_grad * n2, axis=0, keepdims=True)
+    stats[1:2, :] = jnp.sum(second_grad, axis=0, keepdims=True)
+    grad = dy + norm_back(second_grad, n2, inverse[...], gain2[...])
+    middle_grad[...] = grad
+    branch = grad.astype(bf16)
+    da_send[...] = dot_nn(branch, wo_x[...]).astype(bf16)
+    post.send(da_send, da.at[here_rows], me.xp)
+    stats[3:4, :] = jnp.sum(branch.astype(f32), axis=0, keepdims=True)
+    da[here_rows, :] = dot_nn(branch, wh[3]).astype(bf16)
+    g_out_send[...] = dot_tn(branch, att_x[...]).astype(bf16)
+    g_out_own[...] = dot_tn(branch, attended[here_rows, :]).astype(bf16)
+    post.close()
+    for copy in own_copies[3:]:
+        copy.wait()
+
+
+def first_half(fsdp_count, where, patches, grads, attn_proj, out_proj, up, down, bias, *rows):
+    width = patches.shape[1]
+    shape = jax.ShapeDtypeStruct
+    vmem = pltpu.VMEM
+    units = 2 * up.shape[1]
+    all_units = 2 * patches.shape[0] // UNIT
+    deep = up.shape[0]
+    fold = lambda a: a.reshape(-1, UNIT, width)
+    return pl.pallas_call(
+        partial(first_kernel, fsdp_count),
+        out_shape=(
+            shape((OWN, 384), bf16),
+            shape((KEYS, 384), bf16),
+            shape((KEYS, 384), bf16),
+            shape((384, KEYS), bf16),
+            shape((OWN, 384), bf16),
+            shape((OWN, width), bf16),
+            shape((OWN, width), bf16),
+            shape((4, width, 384), bf16),
+            shape((width, units), bf16),
+            shape((width, units), bf16),
+            shape((8, OWN), f32),
+            shape((OWN, 384), bf16),
+            shape((HALF, width), f32),
+            shape((HALF, width), f32),
+            shape((HALF, width), bf16),
+            shape((width, 384), bf16),
+            shape((width, 384), bf16),
+            shape((4, width), f32),
+            shape((2, width), f32),
+        ),
+        in_specs=[SMEM, ANY, ANY, VMEM, VMEM, ANY, VMEM] + [VMEM] * 7,
+        out_specs=(ANY,) * 10 + (VMEM,) * 9,
+        scratch_shapes=[
+            vmem((deep, width), bf16),
+            vmem((deep, down.shape[0]), bf16),
+            vmem((all_units, UNIT, width), bf16),
+            vmem((all_units, UNIT, width), bf16),
+            vmem((2, width, width), bf16),
+            vmem((4, width, 384), bf16),
+            vmem((width, 384), bf16),
+            vmem((2, width, up.shape[1]), bf16),
+            vmem((2, width, up.shape[1]), bf16),
+            vmem((2,) + bias.shape, f32),
+            vmem((KEYS, width), bf16),
+            vmem((OWN, width), bf16),
+            vmem((OWN, width), bf16),
+            vmem((OWN, width), bf16),
+            vmem((OWN, 384), bf16),
+            vmem((KEYS, 384), bf16),
+            vmem((KEYS, 384), bf16),
+            vmem((384, KEYS), bf16),
+            vmem((384, KEYS), bf16),
+            vmem((OWN, 384), bf16),
+            vmem((384, OWN), f32),
+            vmem((HALF, 384), bf16),
+            vmem((TRUNK + 2 * BLOCK, OWN), f32),
+            vmem((TRUNK + 2 * BLOCK, OWN), bf16),
+            vmem((HALF, width), f32),
+            vmem((HALF, width), f32),
+            vmem((HALF, 1), f32),
+            vmem((OWN, width), bf16),
+            vmem((OWN, units), bf16),
+            vmem((OWN, units), bf16),
+            vmem((OWN, width), f32),
+            vmem((HALF, width), bf16),
+            vmem((HALF, width), bf16),
+            vmem((HALF, 384), bf16),
+            vmem((width, units), bf16),
+            vmem((width, units), bf16),
+            pltpu.SemaphoreType.DMA((16,)),
+            pltpu.SemaphoreType.DMA((80,)),
+            pltpu.SemaphoreType.DMA((80,)),
+        ],
+        compiler_params=pltpu.CompilerParams(collective_id=0, has_side_effects=True, vmem_limit_bytes=LIMIT),
+        name="first_half",
+    )(where, fold(patches), fold(grads), attn_proj, out_proj, up, down, bias, *rows)
+
+
+class StripSum:
+    def __init__(self, me, post, fsdp_count, held, from_core, buffers):
+        self.me, self.post, self.count = me, post, fsdp_count
+        self.held, self.from_core = held, from_core
+        self.from_y, self.from_z, self.done = buffers
+        self.half = from_core.shape[0] // fsdp_count // 2
+
+    def from_sibling(self, src):
+        self.core_copy = self.post.send(src, self.from_core, self.me.core)
+
+    def add_sibling(self):
+        self.post.got(self.core_copy)
+        half = self.half
+
+        def step(j, carried):
+            rows = ds(j * half, half)
+            self.held[rows, :] = (self.held[rows, :].astype(f32) + self.from_core[rows, :].astype(f32)).astype(bf16)
+            return carried
+
+        lax.fori_loop(0, 2 * self.count, step, 0)
+
+    def strip(self, g, side):
+        return ds(self.half * (2 * g + side), self.half)
+
+    def over_y(self):
+        me = self.me
+        self.y_copies = [
+            self.post.send(self.held.at[self.strip(g, 1 - me.c)], self.from_y.at[g], me.yp)
+            for g in range(self.count)
+        ]
+
+    def over_z(self):
+        me = self.me
+        for copy in self.y_copies:
+            self.post.got(copy)
+
+        def step(g, carried):
+            rows = self.strip(g, me.c)
+            self.held[rows, :] = (self.held[rows, :].astype(f32) + self.from_y[g].astype(f32)).astype(bf16)
+            return carried
+
+        lax.fori_loop(0, self.count, step, 0)
+        self.z_copies = [
+            self.post.send(self.held.at[self.strip((me.f + i + 1) % self.count, me.c)], self.from_z.at[i], device)
+            for i, device in enumerate(me.z)
+        ]
+
+    def finish(self):
+        me = self.me
+        for copy in self.z_copies:
+            self.post.got(copy)
+        total = self.held[self.strip(me.f, me.c), :].astype(f32)
+        for i in range(self.count - 1):
+            total = total + self.from_z[i].astype(f32)
+        self.done[me.c] = total.astype(bf16)
+        self.last = self.post.send(self.done.at[me.c], self.done.at[me.c], me.yp)
+
+    def value(self):
+        self.post.got(self.last)
+        return self.done[...].reshape(2 * self.half, -1).astype(f32)
+
+
+def second_kernel(
+    fsdp_count, where, q_in, k_in, v_in, kt_in, att_in, low_in, x_in, wh_in, g_up, g_down,
+    lse, da, middle_grad, mlp_own, mlp_send, g_out_own, g_out_send, mid_stats, up_stats, gain1,
+    result, patch_grad, grad_attn, grad_out, grad_up, grad_down, all_total, part_total,
+    q, k, v, kt, attended, low_own, x_own, wh, up_own, down_own,
+    delta, st, dpt, pt, dst, dk_acc, dv_acc, dq_t, dq, trunk, trunk_own, trunk_far, trunk_send, trunk_y, dkv_own,
+    mlp_x, first_send, first_x, rows_out, out_core, out_sum, out_x, packed,
+    from_core, from_y, from_z, done, result_stage, patch_stage, stat_buf, stat_in, stat_z, local, stage_sem, ss, rs,
+):
+    me = Here(fsdp_count)
+    f, c, x, core = me.f, me.c, me.x, me.k
+    s = 2 * c + core
+    pair = 2 * BLOCK
+    units = HALF // UNIT
+    width = x_in.shape[1]
+    shard = width
+    mine, far = HALF * x, HALF * (1 - x)
+    here_rows, far_rows = ds(mine, HALF), ds(far, HALF)
+    loads = []
+    own_lanes, sibling_lanes = pl.ds(pl.multiple_of(shard * core, 128), shard), pl.ds(
+        pl.multiple_of(shard * (1 - core), 128), shard
+    )
+    for src, held in (
+        (k_in, k), (q_in, q), (v_in, v), (att_in, attended), (kt_in, kt),
+        (g_up.at[:, own_lanes], up_own), (g_down.at[:, own_lanes], down_own),
+        (low_in, low_own), (x_in, x_own), (wh_in.at[pl.ds(0, 3)], wh),
+    ):
+        copy = pltpu.make_async_copy(src, held, local.at[len(loads)])
+        copy.start()
+        loads.append(copy)
+    greet([me.core, me.xp, me.yp] + me.z)
+    post = Post(ss, rs)
+    mlp_copy = post.send(mlp_send, mlp_x, me.xp)
+    sums = [
+        StripSum(me, post, fsdp_count, held, from_core.at[i], (from_y.at[i], from_z.at[i], done.at[i]))
+        for i, held in enumerate((up_own, down_own, packed.at[core]))
+    ]
+    sums[0].from_sibling(g_up.at[:, sibling_lanes])
+    sums[1].from_sibling(g_down.at[:, sibling_lanes])
+    slab_own = pl.ds(pl.multiple_of(128 * core, 128), 128)
+    slab_sibling = pl.ds(pl.multiple_of(128 * (1 - core), 128), 128)
+    slab_both = pl.ds(256, 128)
+    out_copies = []
+    for i, src in enumerate((g_out_own, g_out_send)):
+        for j, lanes in enumerate((slab_sibling, slab_both)):
+            out_copies.append(post.send(src.at[:, lanes], out_core.at[i, j], me.core))
+    for copy in loads[:5]:
+        copy.wait()
+    product = (da[...].astype(f32) * attended[...].astype(f32)).T
+    for h in range(6):
+        delta[h : h + 1, :] = jnp.sum(product[h * HEAD_DIM : (h + 1) * HEAD_DIM], axis=0, keepdims=True)
+    lane = lax.broadcasted_iota(jnp.int32, (OWN, 128), 1) // HEAD_DIM
+
+    def head(h, carried):
+        slab, part = h // 2, h % 2
+        lanes = pl.ds(pl.multiple_of(slab * 128, 128), 128)
+        q_slab, da_slab = q[:, lanes], da[:, lanes]
+        q_part = jnp.where(lane == part, q_slab, jnp.zeros_like(q_slab))
+        da_part = jnp.where(lane == part, da_slab, jnp.zeros_like(da_slab))
+        st[0:TRUNK, :] = dot_nt(k[0:TRUNK, lanes], q_part)
+        dpt[0:TRUNK, :] = dot_nt(v[0:TRUNK, lanes], da_part)
+        for q_row, k_row, count in PIECES:
+            cols, rows = slice(q_row, q_row + BLOCK), slice(TRUNK, TRUNK + count)
+            st[rows, cols] = dot_nt(k[k_row : k_row + count, lanes], q_part[q_row : q_row + BLOCK])
+            dpt[rows, cols] = dot_nt(v[k_row : k_row + count, lanes], da_part[q_row : q_row + BLOCK])
+        log_total, row_delta = lse[pl.ds(h, 1), :], delta[pl.ds(h, 1), :]
+        for j in range(OWN // BLOCK):
+            cols = slice(j * BLOCK, (j + 1) * BLOCK)
+            count = TRUNK + (0 if j < 2 else PIECES[j - 2][2])
+            for r in range(0, count, BLOCK):
+                weight = jnp.exp(st[r : r + BLOCK, cols] - log_total[:, cols])
+                pt[r : r + BLOCK, cols] = weight.astype(bf16)
+                dst[r : r + BLOCK, cols] = (
+                    weight * (dpt[r : r + BLOCK, cols] - row_delta[:, cols])
+                ).astype(bf16)
+        dk_acc[0:TRUNK, :] += dot_nn(dst[0:TRUNK, :], q_part)
+        dv_acc[0:TRUNK, :] += dot_nn(pt[0:TRUNK, :], da_part)
+        head_rows = ds(h * HEAD_DIM, HEAD_DIM)
+        dq_t[head_rows, :] = dot_nn(kt[head_rows, 0:TRUNK], dst[0:TRUNK, :])
+        for q_row, k_row, count in PIECES:
+            cols, rows = slice(q_row, q_row + BLOCK), slice(TRUNK, TRUNK + count)
+            own = slice(k_row, k_row + count)
+            dk_acc[own, :] += dot_nn(dst[rows, cols], q_part[q_row : q_row + BLOCK])
+            dv_acc[own, :] += dot_nn(pt[rows, cols], da_part[q_row : q_row + BLOCK])
+            dq_t[head_rows, cols] += dot_nn(kt[head_rows, own], dst[rows, cols])
+        return carried
+
+    chip_rows = lambda chip, side: ds(pair * (2 * chip + side), pair)
+    trunk_copies, y_copies = [], []
+
+    def slab_heads(slab):
+        dk_acc[...] = jnp.zeros_like(dk_acc)
+        dv_acc[...] = jnp.zeros_like(dv_acc)
+        lax.fori_loop(2 * slab, 2 * slab + 2, head, 0)
+
+    def trunk_out(slab):
+        trunk[slab, 0] = dk_acc[0:TRUNK, :].astype(bf16)
+        trunk[slab, 1] = dv_acc[0:TRUNK, :].astype(bf16)
+        for i, total in enumerate((dk_acc, dv_acc)):
+            lanes = slice(384 * i + 128 * slab, 384 * i + 128 * slab + 128)
+            dkv_own[pair:, lanes] = total[TRUNK:, :].astype(bf16)
+        trunk_copies.append(
+            (
+                post.send(trunk.at[slab, :, chip_rows(1 - c, 1 - core), :], trunk_far.at[slab], me.core),
+                post.send(trunk.at[slab, :, chip_rows(c, 1 - core), :], trunk_own.at[slab], me.core),
+            )
+        )
+
+    def trunk_over(slab):
+        post.got(trunk_copies[slab][0])
+        trunk_send[slab] = (
+            trunk[slab, :, chip_rows(1 - c, core), :].astype(f32) + trunk_far[slab].astype(f32)
+        ).astype(bf16)
+        y_copies.append(post.send(trunk_send.at[slab], trunk_y.at[slab], me.yp))
+
+    def trunk_in(slab):
+        post.got(trunk_copies[slab][1])
+        post.got(y_copies[slab])
+        total = (
+            trunk[slab, :, chip_rows(c, core), :].astype(f32)
+            + trunk_own[slab].astype(f32)
+            + trunk_y[slab].astype(f32)
+        ).astype(bf16)
+        for i in range(2):
+            lanes = slice(384 * i + 128 * slab, 384 * i + 128 * slab + 128)
+            dkv_own[0:pair, lanes] = total[i]
+
+    slab_heads(0)
+    trunk_out(0)
+    for copy in loads[5:]:
+        copy.wait()
+    sums[0].add_sibling()
+    sums[0].over_y()
+    trunk_over(0)
+    slab_heads(1)
+    trunk_out(1)
+    for copy in out_copies:
+        post.got(copy)
+    for i, src in enumerate((g_out_own, g_out_send)):
+        for j, lanes in enumerate((slab_own, slab_both)):
+            out_sum[i, j] = (src[:, lanes].astype(f32) + out_core[i, j].astype(f32)).astype(bf16)
+    out_copy = post.send(out_sum.at[1], out_x, me.xp)
+    trunk_over(1)
+    sums[1].add_sibling()
+    slab_heads(2)
+    trunk_out(2)
+    dq[...] = (dq_t[...].T * HEAD_DIM ** (-0.5)).astype(bf16)
+    trunk_over(2)
+    sums[0].over_z()
+    for slab in range(3):
+        trunk_in(slab)
+
+    def first(rows):
+        return (
+            dot_nt(dq[rows, :], wh[0])
+            + dot_nt(dkv_own[rows, 0:384], wh[1])
+            + dot_nt(dkv_own[rows, 384:768], wh[2])
+        )
+
+    first_send[...] = first(far_rows).astype(bf16)
+    first_copy = post.send(first_send, first_x, me.xp)
+    sums[1].over_y()
+    own_first = first(here_rows)
+    post.got(mlp_copy)
+    own_units = pl.ds(units * (2 * s + x), units)
+    rows_out[0, own_units] = (mlp_own[...] + mlp_x[...].astype(f32)).astype(bf16).reshape(units, UNIT, width)
+    post.got(out_copy)
+    g_attn = [
+        dot_tn(low_own[...], dq[...]),
+        dot_tn(low_own[...], dkv_own[:, 0:384]),
+        dot_tn(low_own[...], dkv_own[:, 384:768]),
+    ]
+    tails = []
+    for j in (0, 1):
+        for i in range(3):
+            packed[j, :, 128 * i : 128 * i + 128] = g_attn[i][:, 128 * j : 128 * j + 128].astype(bf16)
+        tail = [g[:, 256 + 64 * j : 320 + 64 * j] for g in g_attn]
+        packed[j, :, 512:640] = jnp.concatenate(tail[0:2], axis=1).astype(bf16)
+        packed[j, :, 640:768] = jnp.concatenate([tail[2], jnp.zeros_like(tail[2])], axis=1).astype(bf16)
+    attn_stats = jnp.concatenate(
+        [
+            jnp.sum(dq[...].astype(f32), axis=0, keepdims=True),
+            jnp.sum(dkv_own[:, 384:768].astype(f32), axis=0, keepdims=True),
+        ],
+        axis=1,
+    )
+    sums[2].from_sibling(packed.at[1 - core])
+    sums[2].add_sibling()
+    packed[core, :, 384:512] = (out_sum[0, 0].astype(f32) + out_x[0].astype(f32)).astype(bf16)
+    last = out_sum[0, 1].astype(f32) + out_x[1].astype(f32)
+    side = lax.broadcasted_iota(jnp.int32, last.shape, 1) // HEAD_DIM
+    turned = jnp.concatenate([last[:, HEAD_DIM:], last[:, :HEAD_DIM]], axis=1)
+    tail = jnp.where(core == 0, turned, last)
+    packed[core, :, 640:768] = jnp.where(side == 0, packed[core, :, 640:768].astype(f32), tail).astype(bf16)
+    post.got(first_copy)
+    first_grad = own_first + first_x[...].astype(f32)
+    n1, s1 = row_norm(x_own[here_rows, :].astype(f32))
+    grad = middle_grad[...] + norm_back(first_grad, n1, s1, gain1[...])
+    rows_out[1, own_units] = grad.astype(bf16).reshape(units, UNIT, width)
+    beside = 2 * s + 1 - x
+    beyond = 2 * (2 * (1 - c) + core) + x
+    corner = 2 * (2 * (1 - c) + core) + 1 - x
+    near, over = {}, {}
+
+    def piece(index, owner, start, count):
+        return rows_out.at[index, pl.ds(units * owner + start, count)]
+
+    def spread(index):
+        own = piece(index, 2 * s + x, 0, units)
+        near[index] = (post.send(own, own, me.xp), post.send(own, own, me.yp))
+        post.send(own, own, me.core)
+
+    def pass_on(index):
+        quarter = units // 2
+        post.got(near[index][0])
+        part = piece(index, beside, 0, quarter)
+        diagonal = [post.send(part, part, me.yp)]
+        whole = piece(index, beside, 0, units)
+        post.send(whole, whole, me.core)
+        post.got(near[index][1])
+        part = piece(index, beyond, quarter, units - quarter)
+        diagonal.append(post.send(part, part, me.xp))
+        whole = piece(index, beyond, 0, units)
+        post.send(whole, whole, me.core)
+        over[index] = diagonal
+
+    def corner_on(index):
+        for copy in over[index]:
+            post.got(copy)
+        whole = piece(index, corner, 0, units)
+        post.send(whole, whole, me.core)
+
+    spread(1)
+    rows_mid, rows_up = mid_stats.shape[0], up_stats.shape[0]
+    stat_buf[0:1, :] = jnp.sum(first_grad * n1, axis=0, keepdims=True)
+    stat_buf[1:2, :] = jnp.sum(first_grad, axis=0, keepdims=True)
+    stat_buf[2 : 2 + rows_mid, :] = mid_stats[...]
+    stat_buf[2 + rows_mid : 8, :] = jnp.zeros((6 - rows_mid, width), f32)
+    stat_buf[8 : 8 + rows_up, :] = up_stats[...]
+    stat_buf[8 + rows_up : 9 + rows_up, :] = attn_stats
+    stat_buf[9 + rows_up : 16, :] = jnp.zeros((7 - rows_up, width), f32)
+    level = lambda i: pl.ds(16 * i, 16)
+    stat_copy = post.send(stat_buf.at[level(0)], stat_in.at[0], me.core)
+    sums[2].over_y()
+    post.got(stat_copy)
+    stat_buf[level(1), :] = stat_buf[level(0), :] + stat_in[0]
+    stat_copy = post.send(stat_buf.at[level(1)], stat_in.at[1], me.yp)
+    sums[1].over_z()
+    sums[0].finish()
+    pass_on(1)
+    spread(0)
+    post.got(stat_copy)
+    stat_buf[level(2), :] = stat_buf[level(1), :] + stat_in[1]
+    stat_copy = post.send(stat_buf.at[level(2)], stat_in.at[2], me.xp)
+    sums[2].over_z()
+    corner_on(1)
+    pass_on(0)
+    post.got(stat_copy)
+    stat_buf[48:56, :] = stat_buf[32:40, :] + stat_in[2, 0:8]
+    stat_buf[56:64, :] = stat_buf[40:48, :]
+    stat_z[f] = stat_buf[level(3), :]
+    stat_copies = [post.send(stat_buf.at[level(3)], stat_z.at[f], device) for device in me.z]
+    sums[1].finish()
+    corner_on(0)
+    sums[2].finish()
+    for copy in stat_copies:
+        post.got(copy)
+    total = stat_z[0]
+    for g in range(1, fsdp_count):
+        total = total + stat_z[g]
+    all_total[...] = total[0 : 2 + rows_mid]
+    part_total[...] = total[8 : 9 + rows_up]
+    grad_up[...] = sums[0].value()
+    grad_down[...] = sums[1].value().T
+    value = sums[2].value()
+    tails = [value[:, 512:576], value[:, 576:640], value[:, 640:704], value[:, 704:768]]
+    for i in range(3):
+        grad_attn[i, :, 0:128] = value[:, 128 * i : 128 * i + 128]
+        grad_attn[i, :, 128:192] = tails[i]
+    grad_out[...] = jnp.concatenate([value[:, 384:512], tails[3]], axis=1).T
+    post.close()
+    out = []
+    for j in range(result.shape[0] // BLOCK):
+        for copy in out[max(0, 2 * j - 4) : max(0, 2 * j - 2)]:
+            copy.wait()
+        rows = pl.ds(where[j], BLOCK // UNIT)
+        result_stage[j % 2] = rows_out[0, rows].reshape(BLOCK, -1)
+        patch_stage[j % 2] = rows_out[1, rows].reshape(BLOCK, -1).astype(f32)
+        to = pl.ds(j * BLOCK, BLOCK)
+        for i, (stage, dest) in enumerate(((result_stage, result), (patch_stage, patch_grad))):
+            copy = pltpu.make_async_copy(stage.at[j % 2], dest.at[to], stage_sem.at[i, j % 2])
+            copy.start()
+            out.append(copy)
+    for copy in out[-4:]:
+        copy.wait()
+
+
+def second_half(fsdp_count, where, *operands):
+    shape = jax.ShapeDtypeStruct
+    vmem = pltpu.VMEM
+    width = operands[5].shape[1]
+    rows = where.shape[0] * BLOCK
+    tall = TRUNK + 2 * BLOCK
+    pair = 2 * BLOCK
+    deep = width // fsdp_count
+    half = deep // 2
+    return pl.pallas_call(
+        partial(second_kernel, fsdp_count),
+        out_shape=(
+            shape((rows, width), bf16),
+            shape((rows, width), f32),
+            shape((3, deep, 192), f32),
+            shape((192, deep), f32),
+            shape((deep, width), f32),
+            shape((width, deep), f32),
+            shape((6, width), f32),
+            shape((3, width), f32),
+        ),
+        in_specs=[SMEM] + [ANY] * 10 + [VMEM] * 10,
+        out_specs=(ANY,) * 2 + (VMEM,) * 6,
+        scratch_shapes=[
+            vmem((OWN, 384), bf16),
+            vmem((KEYS, 384), bf16),
+            vmem((KEYS, 384), bf16),
+            vmem((384, KEYS), bf16),
+            vmem((OWN, 384), bf16),
+            vmem((OWN, width), bf16),
+            vmem((OWN, width), bf16),
+            vmem((3, width, 384), bf16),
+            vmem((width, width), bf16),
+            vmem((width, width), bf16),
+            vmem((8, OWN), f32),
+            vmem((tall, OWN), f32),
+            vmem((tall, OWN), f32),
+            vmem((tall, OWN), bf16),
+            vmem((tall, OWN), bf16),
+            vmem((KEYS, 128), f32),
+            vmem((KEYS, 128), f32),
+            vmem((384, OWN), f32),
+            vmem((OWN, 384), bf16),
+            vmem((3, 2, TRUNK, 128), bf16),
+            vmem((3, 2, pair, 128), bf16),
+            vmem((3, 2, pair, 128), bf16),
+            vmem((3, 2, pair, 128), bf16),
+            vmem((3, 2, pair, 128), bf16),
+            vmem((OWN, 768), bf16),
+            vmem((HALF, width), bf16),
+            vmem((HALF, width), bf16),
+            vmem((HALF, width), bf16),
+            vmem((2, 2 * rows // UNIT, UNIT, width), bf16),
+            vmem((2, 2, width, 128), bf16),
+            vmem((2, 2, width, 128), bf16),
+            vmem((2, width, 128), bf16),
+            vmem((2, width, width), bf16),
+            vmem((3, width, width), bf16),
+            vmem((3, fsdp_count, half, width), bf16),
+            vmem((3, fsdp_count - 1, half, width), bf16),
+            vmem((3, 2, half, width), bf16),
+            vmem((2, BLOCK, width), bf16),
+            vmem((2, BLOCK, width), f32),
+            vmem((64, width), f32),
+            vmem((3, 16, width), f32),
+            vmem((fsdp_count, 16, width), f32),
+            pltpu.SemaphoreType.DMA((10,)),
+            pltpu.SemaphoreType.DMA((2, 2)),
+            pltpu.SemaphoreType.DMA((80,)),
+            pltpu.SemaphoreType.DMA((80,)),
+        ],
+        compiler_params=pltpu.CompilerParams(collective_id=1, has_side_effects=True, vmem_limit_bytes=LIMIT),
+        name="second_half",
+    )(where, *operands)
+
+
+def tree_shards(
+    fsdp_count, patches, out_grad, block_order, first_gain, first_shift, attn_proj, attn_bias, out_proj, out_bias,
+    second_gain, second_shift, up_proj, up_bias, down_proj, down_bias,
+):
+    row = lambda vector: vector.reshape(1, -1)
+    order = block_order[0]
+    slots = jnp.arange(order.shape[0], dtype=jnp.int32)
+    unit_count = BLOCK // UNIT
+    where = unit_count * jnp.sum(
+        jnp.where(order[None, :] == slots[:, None], slots[None, :], 0), axis=1, dtype=jnp.int32
+    )
+    branch, leaf = order - TRUNK_BLK, order - TRUNK_BLK - BRANCHES
+    gathered = unit_count * jnp.where(
+        order < TRUNK_BLK,
+        5 * (order // 2) + order % 2,
+        jnp.where(branch < BRANCHES, 5 * branch + 3, 5 * (leaf // 2) + 2 + 2 * (leaf % 2)),
+    )
+    own = patches.shape[0] // BLOCK
+    gathered = lax.dynamic_slice_in_dim(gathered, lax.axis_index("context") * own, own)
+    head_width = attn_bias.shape[1]
+    bias = jnp.zeros((8, up_bias.shape[0]), f32)
+    bias = bias.at[0].set(up_bias).at[1:3, :head_width].set(attn_bias)
+    middle = first_half(
+        fsdp_count, where, patches, out_grad, attn_proj, out_proj, up_proj, down_proj, bias,
+        row(first_gain), row(first_shift), row(second_gain), row(second_shift), row(out_bias), row(down_bias),
+    )
+    result, patch_grad, grad_attn, grad_out, grad_up, grad_down, all_total, part_total = second_half(
+        fsdp_count, gathered, *middle, row(first_gain)
+    )
+    core = lax.axis_index("tensor") % 2
+    up_total = lax.dynamic_index_in_dim(part_total, core, 0, keepdims=False)
+    attn_total = part_total[2].reshape(2, 384)
+    attn_total = jnp.concatenate(
+        [
+            lax.dynamic_slice_in_dim(attn_total, core * 128, 128, 1),
+            lax.dynamic_slice_in_dim(attn_total, 256 + core * 64, 64, 1),
+        ],
+        axis=1,
+    )
+    return (
+        result,
+        patch_grad,
+        all_total[0],
+        all_total[1],
+        grad_attn,
+        attn_total,
+        grad_out,
+        all_total[5],
+        all_total[2],
+        all_total[3],
+        grad_up,
+        up_total,
+        grad_down,
+        all_total[4],
+    )
+
+
 def solution(mesh):
+    fits = mesh.shape["context"] * 2 == BRANCHES and mesh.shape["tensor"] == 4 and mesh.shape["fsdp"] == 4
+    body = partial(tree_shards, mesh.shape["fsdp"]) if fits else shards
     return jax.shard_map(
-        shards,
+        body,
         mesh=mesh,
         in_specs=(
             P(("fsdp", "context"), None),

time: 960 us -> 238 us (0.25)
  waiting for transfers between devices: 520 us -> 0 us
  Pallas kernels: 0 us -> 211 us
  matrix products: 149 us -> 0 us
  blocking collectives: 120 us -> 0 us
  other arithmetic: 79.7 us -> 1.89 us
  local copies, waits for them, and re-layouts: 63.8 us -> 23.6 us
  between operations: 16.4 us -> 0.73 us
    psum x4 -> x0, waiting for transfers between devices: 274 us -> none  [the longest x1 79.9 us: shards(): middle = inputs + (lax.psum(attn_part, 'tensor') + out_bias)]
    pallas_call x0 -> x2, Pallas kernels: none -> 211 us  [the longest x1 108 us: second_half(): pl.pallas_call(partial(second_kernel, fsdp_count), out_shape=(shape((rows...]
    reduce_scatter x3 -> x0, waiting for transfers between devices: 164 us -> none  [the longest x1 65.3 us: shards(): lax.psum_scatter(grad_down, ('fsdp', 'context'), scatter_dimension=1, til...]
    dot_general x55 -> x0, matrix products: 143 us -> none  [the longest x15 27.9 us: scores_of(): jnp.einsum('qhd,khd->hqk', query_heads, key_heads, preferred_element_type...]
    all_gather x6 -> x0, blocking collectives: 81.9 us -> none  [the longest x1 31.5 us: shards(): lax.all_gather(attn_proj, 'fsdp', axis=1, tiled=True)]
    unnamed x14 -> x0, waiting for transfers between devices: 70.9 us -> none
    psum x1 -> x0, blocking collectives: 38 us -> none  [shards(): lax.psum((grad_first_gain, grad_first_shift, grad_attn_bias, grad_out_bia...]
    reduce_sum x14 -> x1, other arithmetic: 34 us -> 0.77 us  [tree_shards(): jnp.sum(jnp.where(order[None, :] == slots[:, None], slots[None, :], 0), a...]
  transfers between devices with their start and end apart: 12 -> 0, of which waited for: 10 -> 0; matrix products, arithmetic and copies ran while one was open for 7% -> 0% of each run, Pallas kernels for 0% -> 0%
where the time goes in v2:
time: 238 us
  Pallas kernels  211 us (89%)
  local copies, waits for them, and re-layouts  23.6 us (10%)
    pallas_call x1, Pallas kernels, second_half(): pl.pallas_call(partial(second_kernel, fsdp_count), out_shape=(shape((rows...  108 us
    pallas_call x1, Pallas kernels, first_half(): pl.pallas_call(partial(first_kernel, fsdp_count), out_shape=(shape((OWN,...  104 us
    unnamed x19, local copies, waits for them, and re-layouts  11.4 us
    reshape x6, local copies, waits for them, and re-layouts, tree_shards(): row = lambda vector: vector.reshape(1, -1)  7.61 us

profile of v2, /device:TPU:0, one launch (start us, length us, event | category | flops | bytes accessed | tf_op | source)
XLA Modules:
  0.0 237.7 jit_solution(8080378691953760554)
XLA Ops:
  0.6 1.3 reshape.115.gain1
  1.9 1.9 copy.31.down
  3.8 0.7 reshape.114
  4.5 1.6 scatter.9.bias
  6.1 0.0 copy-start.4
  6.1 1.3 reshape.116.shift1
  7.4 1.3 reshape.117.gain2
  8.6 1.3 reshape.118.shift2
  9.9 1.3 reshape.119.out_bias
  11.2 1.3 reshape.120.down_bias
  12.4 0.8 select_reduce_fusion
  13.2 0.5 broadcast_multiply_fusion.where
  13.7 103.9 %first_half.1 = (bf16[640,384]{1,0:T(8,128)(2,1)}, bf16[1408,384]{1,0:T(8,128)(2,1)}, bf16[1408,384]{1,0:T(8,128)(2,1)}, bf16[384,1408]{1,0:T(8,128)(2,1)}, bf16...) custom-call(s32[20]{0:T(128)} %broadcast_multiply_fusion.where, ...), custom_call_target="tpu_custom_call" | custom-call | tf_op jit(solution)/shard_map/first_half/pallas_call | solution.py:740
  117.6 0.6 dynamic_slice.13.where
  118.2 107.6 %second_half.1 = (bf16[1280,768]{1,0:T(8,128)(2,1)}, f32[1280,768]{1,0:T(8,128)}, f32[3,192,192]{2,1,0:T(8,128)}, f32[192,192]{1,0:T(8,128)}, f32[192,768]{1,0:T...) custom-call(s32[10]{0:T(128)} %dynamic_slice.13.where, bf16[640,384]{1,0:T(8,128)(2,1)} %get-tuple-element.65.q_in, ...), custom_call_target="tpu_custom_call" | custom-call | tf_op jit(solution)/shard_map/second_half/pallas_call | solution.py:1179
  225.8 1.6 slice_reduce_fusion
  227.5 0.1 constant_dynamic-slice_fusion
  227.5 0.6 pad_maximum_fusion
  228.1 2.2 copy.32
  230.3 3.1 %copy.39 = bf16[1280,768]{1,0:T(8,128)(2,1)} copy(bf16[1280,768]{1,0:T(8,128)(2,1)} %get-tuple-element.144) | data formatting | bytes 3932160
  233.4 1.9 copy.40
  235.4 0.8 copy.41
  236.2 0.7 copy.42
  236.9 0.8 copy.43
  (15 shorter events, 0.1 us)
Async XLA Ops:
  6.1 7.6 %copy-start.4 = (f32[8,768]{1,0:T(8,128)}, f32[8,768]{1,0:T(8,128)S(1)}, u32[]{:S(2)}) copy-start(f32[8,768]{1,0:T(8,128)S(1)} %scatter.9.bias) | copy-start | bytes 73732
  13.7 103.9 %copy-start.5 = (s32[1,20]{1,0:T(1,128)S(1)}, s32[1,20]{1,0:T(1,128)}, u32[]{:S(2)}) copy-start(s32[1,20]{1,0:T(1,128)} %param.21) | copy-start | bytes 244
  230.3 3.1 %copy-start = (f32[1280,768]{1,0:T(8,128)S(1)}, f32[1280,768]{1,0:T(8,128)}, u32[]{:S(2)}) copy-start(f32[1280,768]{1,0:T(8,128)} %get-tuple-element.145) | copy-start | bytes 11796484
  233.4 1.9 copy-start.2
  233.4 2.7 %copy-start.3 = (f32[192,192]{1,0:T(8,128)S(1)}, f32[192,192]{1,0:T(8,128)}, u32[]{:S(2)}) copy-start(f32[192,192]{1,0:T(8,128)} %get-tuple-element.150) | copy-start | bytes 442372
  235.4 1.5 copy-start.1

commit v3 on v2

--- a/solution.py
+++ b/solution.py
@@ -406,11 +406,15 @@
 UNIT = 32
 
 
+def wide(vector):
+    return vector[...].reshape(1, -1)
+
+
 def first_kernel(
-    fsdp_count, where, patches, grads, attn_proj, out_proj, up, down, bias, gain1, shift1, gain2, shift2, out_bias, down_bias,
+    fsdp_count, order, patches, grads, attn_proj, out_proj, up, d_own, up_bias, attn_bias, gain1, shift1, gain2, shift2, out_bias, down_bias,
     q_out, k_out, v_out, kt_out, att_out, low_out, x_out, wh_out, g_up_out, g_down_out,
     lse, da, middle_grad, mlp_own, mlp_send, g_out_own, g_out_send, stats, up_stats,
-    a_own, d_own, rows_all, grads_all, wa, wh, wo_x, wu, wd, bias_all,
+    where, a_own, bias, rows_all, grads_all, wa, wh, wo_x, wu, wd, bias_all,
     low, low_own, x_own, g_own, q, k, v, kt, vt, attended, att_t, att_x, st, pt,
     middle, normed, inverse, low2, hidden, pre_grad, second, second_send, second_x, da_send, g_up, g_down,
     local, ss, rs,
@@ -435,6 +439,7 @@
     keep(patches, rows_all.at[pl.ds(units * c, units)])
     keep(grads, grads_all.at[pl.ds(units * c, units)])
     keep(up, wu.at[core, ds(deep * f, deep)])
+    keep(d_own, wd.at[core, ds(deep * f, deep)])
     a_own[:, 0:128] = attn_proj[0, :, 0:128]
     a_own[:, 128:256] = attn_proj[1, :, 0:128]
     a_own[:, 256:384] = attn_proj[2, :, 0:128]
@@ -442,6 +447,9 @@
     a_own[:, 384:512] = jnp.concatenate([attn_proj[0, :, 128:head_width], attn_proj[1, :, 128:head_width]], axis=1)
     a_own[:, 512:640] = jnp.concatenate([attn_proj[2, :, 128:head_width], out_t[:, 128:head_width]], axis=1)
     a_own[:, 640:768] = out_t[:, 0:128]
+    bias[...] = jnp.zeros_like(bias)
+    bias[0:1, :] = wide(up_bias)
+    bias[1:3, 0:head_width] = attn_bias[...]
     greet([me.core, me.xp, me.yp] + me.z)
     post = Post(ss, rs)
     there = units * (1 - c)
@@ -471,10 +479,18 @@
     a_core = post.send(a_own, wa.at[core, ds(deep * f, deep)], me.core)
     bias_core = post.send(bias, bias_all.at[core], me.core)
     u_core = post.send(up, wu.at[core, ds(deep * f, deep)], me.core)
+    slots = order.shape[1]
+
+    def find(place, carried):
+        slot = jnp.int32(0)
+        for j in range(slots):
+            slot = jnp.where(order[0, j] == place, j, slot)
+        where[place] = slot * (BLOCK // UNIT)
+        return carried
+
+    lax.fori_loop(0, slots, find, 0)
     wa[core, ds(deep * f, deep), :] = a_own[...]
     bias_all[core] = bias[...]
-    d_own[...] = down[...].T
-    wd[core, ds(deep * f, deep), :] = d_own[...]
     d_core = post.send(d_own, wd.at[core, ds(deep * f, deep)], me.core)
     patches_x = []
     for i in range(2):
@@ -500,7 +516,7 @@
     post.got_from(me.core)
     own_copies[0].wait()
 
-    gain_row, shift_row = gain1[...], shift1[...]
+    gain_row, shift_row = wide(gain1), wide(shift1)
 
     def block_of(array, place):
         return array[pl.ds(where[place], BLOCK // UNIT)].reshape(BLOCK, width)
@@ -634,7 +650,7 @@
     wo_rows = ds(width // 2 * core, width // 2)
     wo_copy = post.send(wh.at[3, wo_rows], wo_x.at[wo_rows], me.xp)
     middle[...] = (
-        x_own[here_rows, :].astype(f32) + out_bias[...] + dot_nt(attended[here_rows, :], wh[3])
+        x_own[here_rows, :].astype(f32) + wide(out_bias) + dot_nt(attended[here_rows, :], wh[3])
     )
     d_y = []
     for copy, source in zip(d_z, me.back):
@@ -653,7 +669,7 @@
     n2, s2 = row_norm(middle[...])
     normed[...] = n2
     inverse[...] = s2
-    low2[here_rows, :] = (n2 * gain2[...] + shift2[...]).astype(bf16)
+    low2[here_rows, :] = (n2 * wide(gain2) + wide(shift2)).astype(bf16)
     low_copy = post.send(low2.at[here_rows], low2.at[here_rows], me.xp)
     own_copies[1].wait()
     for j, place in enumerate(places):
@@ -666,6 +682,7 @@
         relay(wd.at[core, ds(deep * source + other_strip, half)], me.core)
     post.got_from(me.core)
     own_copies[2].wait()
+    own_copies[3].wait()
     tile = 256
 
     def feed(rows):
@@ -707,7 +724,7 @@
     up_stats[0:1, :] = jnp.sum(pre_grad[:, 0:width].astype(f32), axis=0, keepdims=True)
     up_stats[1:2, :] = jnp.sum(pre_grad[:, width:].astype(f32), axis=0, keepdims=True)
     mlp_send[...] = mlp(far_rows).astype(bf16)
-    mlp_own[...] = middle[...] + mlp(here_rows) + down_bias[...]
+    mlp_own[...] = middle[...] + mlp(here_rows) + wide(down_bias)
     dy = g_own[here_rows, :].astype(f32)
     stats[2:3, :] = jnp.sum(dy, axis=0, keepdims=True)
     post.got(second_copy)
@@ -715,7 +732,7 @@
     n2 = normed[...]
     stats[0:1, :] = jnp.sum(second_grad * n2, axis=0, keepdims=True)
     stats[1:2, :] = jnp.sum(second_grad, axis=0, keepdims=True)
-    grad = dy + norm_back(second_grad, n2, inverse[...], gain2[...])
+    grad = dy + norm_back(second_grad, n2, inverse[...], wide(gain2))
     middle_grad[...] = grad
     branch = grad.astype(bf16)
     da_send[...] = dot_nn(branch, wo_x[...]).astype(bf16)
@@ -725,11 +742,11 @@
     g_out_send[...] = dot_tn(branch, att_x[...]).astype(bf16)
     g_out_own[...] = dot_tn(branch, attended[here_rows, :]).astype(bf16)
     post.close()
-    for copy in own_copies[3:]:
+    for copy in own_copies[4:]:
         copy.wait()
 
 
-def first_half(fsdp_count, where, patches, grads, attn_proj, out_proj, up, down, bias, *rows):
+def first_half(fsdp_count, order, patches, grads, attn_proj, out_proj, up, down_t, *vectors):
     width = patches.shape[1]
     shape = jax.ShapeDtypeStruct
     vmem = pltpu.VMEM
@@ -760,11 +777,12 @@
             shape((4, width), f32),
             shape((2, width), f32),
         ),
-        in_specs=[SMEM, ANY, ANY, VMEM, VMEM, ANY, VMEM] + [VMEM] * 7,
+        in_specs=[SMEM, ANY, ANY, VMEM, VMEM, ANY, ANY] + [VMEM] * 8,
         out_specs=(ANY,) * 10 + (VMEM,) * 9,
         scratch_shapes=[
+            pltpu.SMEM(order.shape[1:], jnp.int32),
             vmem((deep, width), bf16),
-            vmem((deep, down.shape[0]), bf16),
+            vmem((8, width), f32),
             vmem((all_units, UNIT, width), bf16),
             vmem((all_units, UNIT, width), bf16),
             vmem((2, width, width), bf16),
@@ -772,7 +790,7 @@
             vmem((width, 384), bf16),
             vmem((2, width, up.shape[1]), bf16),
             vmem((2, width, up.shape[1]), bf16),
-            vmem((2,) + bias.shape, f32),
+            vmem((2, 8, width), f32),
             vmem((KEYS, width), bf16),
             vmem((OWN, width), bf16),
             vmem((OWN, width), bf16),
@@ -805,7 +823,7 @@
         ],
         compiler_params=pltpu.CompilerParams(collective_id=0, has_side_effects=True, vmem_limit_bytes=LIMIT),
         name="first_half",
-    )(where, fold(patches), fold(grads), attn_proj, out_proj, up, down, bias, *rows)
+    )(order, fold(patches), fold(grads), attn_proj, out_proj, up, down_t, *vectors)
 
 
 class StripSum:
@@ -865,19 +883,15 @@
         self.done[me.c] = total.astype(bf16)
         self.last = self.post.send(self.done.at[me.c], self.done.at[me.c], me.yp)
 
-    def value(self):
-        self.post.got(self.last)
-        return self.done[...].reshape(2 * self.half, -1).astype(f32)
-
 
 def second_kernel(
-    fsdp_count, where, q_in, k_in, v_in, kt_in, att_in, low_in, x_in, wh_in, g_up, g_down,
+    fsdp_count, q_in, k_in, v_in, kt_in, att_in, low_in, x_in, wh_in, g_up, g_down,
     lse, da, middle_grad, mlp_own, mlp_send, g_out_own, g_out_send, mid_stats, up_stats, gain1,
-    result, patch_grad, grad_attn, grad_out, grad_up, grad_down, all_total, part_total,
+    rows_out, grads_out, all_total, part_total,
     q, k, v, kt, attended, low_own, x_own, wh, up_own, down_own,
     delta, st, dpt, pt, dst, dk_acc, dv_acc, dq_t, dq, trunk, trunk_own, trunk_far, trunk_send, trunk_y, dkv_own,
-    mlp_x, first_send, first_x, rows_out, out_core, out_sum, out_x, packed,
-    from_core, from_y, from_z, done, result_stage, patch_stage, stat_buf, stat_in, stat_z, local, stage_sem, ss, rs,
+    mlp_x, first_send, first_x, rows_own, out_core, out_sum, out_x, packed,
+    from_core, from_y, from_z, done, stat_buf, stat_in, stat_z, local, ss, rs,
 ):
     me = Here(fsdp_count)
     f, c, x, core = me.f, me.c, me.x, me.k
@@ -1034,8 +1048,7 @@
     sums[1].over_y()
     own_first = first(here_rows)
     post.got(mlp_copy)
-    own_units = pl.ds(units * (2 * s + x), units)
-    rows_out[0, own_units] = (mlp_own[...] + mlp_x[...].astype(f32)).astype(bf16).reshape(units, UNIT, width)
+    rows_own[0] = (mlp_own[...] + mlp_x[...].astype(f32)).astype(bf16).reshape(units, UNIT, width)
     post.got(out_copy)
     g_attn = [
         dot_tn(low_own[...], dq[...]),
@@ -1067,8 +1080,8 @@
     post.got(first_copy)
     first_grad = own_first + first_x[...].astype(f32)
     n1, s1 = row_norm(x_own[here_rows, :].astype(f32))
-    grad = middle_grad[...] + norm_back(first_grad, n1, s1, gain1[...])
-    rows_out[1, own_units] = grad.astype(bf16).reshape(units, UNIT, width)
+    grad = middle_grad[...] + norm_back(first_grad, n1, s1, wide(gain1))
+    rows_own[1] = grad.astype(bf16).reshape(units, UNIT, width)
     beside = 2 * s + 1 - x
     beyond = 2 * (2 * (1 - c) + core) + x
     corner = 2 * (2 * (1 - c) + core) + 1 - x
@@ -1078,9 +1091,12 @@
         return rows_out.at[index, pl.ds(units * owner + start, count)]
 
     def spread(index):
-        own = piece(index, 2 * s + x, 0, units)
-        near[index] = (post.send(own, own, me.xp), post.send(own, own, me.yp))
-        post.send(own, own, me.core)
+        own, there = rows_own.at[index], piece(index, 2 * s + x, 0, units)
+        near[index] = (post.send(own, there, me.xp), post.send(own, there, me.yp))
+        post.send(own, there, me.core)
+        copy = pltpu.make_async_copy(own, there, local.at[len(loads)])
+        copy.start()
+        loads.append(copy)
 
     def pass_on(index):
         quarter = units // 2
@@ -1142,36 +1158,19 @@
         total = total + stat_z[g]
     all_total[...] = total[0 : 2 + rows_mid]
     part_total[...] = total[8 : 9 + rows_up]
-    grad_up[...] = sums[0].value()
-    grad_down[...] = sums[1].value().T
-    value = sums[2].value()
-    tails = [value[:, 512:576], value[:, 576:640], value[:, 640:704], value[:, 704:768]]
-    for i in range(3):
-        grad_attn[i, :, 0:128] = value[:, 128 * i : 128 * i + 128]
-        grad_attn[i, :, 128:192] = tails[i]
-    grad_out[...] = jnp.concatenate([value[:, 384:512], tails[3]], axis=1).T
+    for total in sums:
+        post.got(total.last)
+    grads_out[...] = done[...]
     post.close()
-    out = []
-    for j in range(result.shape[0] // BLOCK):
-        for copy in out[max(0, 2 * j - 4) : max(0, 2 * j - 2)]:
-            copy.wait()
-        rows = pl.ds(where[j], BLOCK // UNIT)
-        result_stage[j % 2] = rows_out[0, rows].reshape(BLOCK, -1)
-        patch_stage[j % 2] = rows_out[1, rows].reshape(BLOCK, -1).astype(f32)
-        to = pl.ds(j * BLOCK, BLOCK)
-        for i, (stage, dest) in enumerate(((result_stage, result), (patch_stage, patch_grad))):
-            copy = pltpu.make_async_copy(stage.at[j % 2], dest.at[to], stage_sem.at[i, j % 2])
-            copy.start()
-            out.append(copy)
-    for copy in out[-4:]:
+    for copy in loads[10:]:
         copy.wait()
 
 
-def second_half(fsdp_count, where, *operands):
+def second_half(fsdp_count, row_count, *operands):
     shape = jax.ShapeDtypeStruct
     vmem = pltpu.VMEM
     width = operands[5].shape[1]
-    rows = where.shape[0] * BLOCK
+    rows = row_count
     tall = TRUNK + 2 * BLOCK
     pair = 2 * BLOCK
     deep = width // fsdp_count
@@ -1179,17 +1178,13 @@
     return pl.pallas_call(
         partial(second_kernel, fsdp_count),
         out_shape=(
-            shape((rows, width), bf16),
-            shape((rows, width), f32),
-            shape((3, deep, 192), f32),
-            shape((192, deep), f32),
-            shape((deep, width), f32),
-            shape((width, deep), f32),
+            shape((2, 2 * rows // UNIT, UNIT, width), bf16),
+            shape((3, 2, half, width), bf16),
             shape((6, width), f32),
             shape((3, width), f32),
         ),
-        in_specs=[SMEM] + [ANY] * 10 + [VMEM] * 10,
-        out_specs=(ANY,) * 2 + (VMEM,) * 6,
+        in_specs=[ANY] * 10 + [VMEM] * 10,
+        out_specs=(ANY,) + (VMEM,) * 3,
         scratch_shapes=[
             vmem((OWN, 384), bf16),
             vmem((KEYS, 384), bf16),
@@ -1219,7 +1214,7 @@
             vmem((HALF, width), bf16),
             vmem((HALF, width), bf16),
             vmem((HALF, width), bf16),
-            vmem((2, 2 * rows // UNIT, UNIT, width), bf16),
+            vmem((2, HALF // UNIT, UNIT, width), bf16),
             vmem((2, 2, width, 128), bf16),
             vmem((2, 2, width, 128), bf16),
             vmem((2, width, 128), bf16),
@@ -1228,76 +1223,104 @@
             vmem((3, fsdp_count, half, width), bf16),
             vmem((3, fsdp_count - 1, half, width), bf16),
             vmem((3, 2, half, width), bf16),
-            vmem((2, BLOCK, width), bf16),
-            vmem((2, BLOCK, width), f32),
             vmem((64, width), f32),
             vmem((3, 16, width), f32),
             vmem((fsdp_count, 16, width), f32),
-            pltpu.SemaphoreType.DMA((10,)),
-            pltpu.SemaphoreType.DMA((2, 2)),
+            pltpu.SemaphoreType.DMA((12,)),
             pltpu.SemaphoreType.DMA((80,)),
             pltpu.SemaphoreType.DMA((80,)),
         ],
         compiler_params=pltpu.CompilerParams(collective_id=1, has_side_effects=True, vmem_limit_bytes=LIMIT),
         name="second_half",
-    )(where, *operands)
+    )(*operands)
+
+
+def place_kernel(
+    order, rows_all, grads, all_total, part_total,
+    result, patch_grad, gain1, shift1, grad_attn, attn_bias, grad_out, out_bias, gain2, shift2, grad_up, up_bias,
+    grad_down_t, down_bias, patch_low, sems,
+):
+    own = result.shape[0] // BLOCK
+    units = BLOCK // UNIT
+    core = lax.axis_index("tensor") % 2
+    copies = []
+    for j in range(own):
+        block = order[0, own * lax.axis_index("context") + j]
+        branch, leaf = block - TRUNK_BLK, block - TRUNK_BLK - BRANCHES
+        index = jnp.where(
+            branch < 0,
+            5 * (block // 2) + block % 2,
+            jnp.where(leaf < 0, 5 * branch + 3, 5 * (leaf // 2) + 2 + 2 * (leaf % 2)),
+        )
+        to = pl.ds(j * units, units)
+        for i, dest in enumerate((result, patch_low)):
+            if i == 0:
+                dest = result.reshape(own * units, UNIT, result.shape[1])
+            copy = pltpu.make_async_copy(
+                rows_all.at[i, pl.ds(index * units, units)], dest.at[to], sems.at[i, j]
+            )
+            copy.start()
+            copies.append(copy)
+    total = lambda i: all_total[i, :]
+    gain1[...], shift1[...], gain2[...], shift2[...] = total(0), total(1), total(2), total(3)
+    down_bias[...], out_bias[...] = total(4), total(5)
+    up_bias[...] = part_total[core, :]
+    for i in range(2):
+        lanes = slice(384 * i, 384 * i + 384)
+        row = part_total[2:3, lanes]
+        first = jnp.where(core == 0, row[:, 0:128], row[:, 128:256])
+        second = jnp.where(core == 0, row[:, 256:320], row[:, 320:384])
+        attn_bias[i : i + 1, :] = jnp.concatenate([first, second], axis=1)
+    side, half, width = grads.shape[1:]
+    value = lambda i: grads[i].reshape(side * half, width).astype(f32)
+    grad_up[...] = value(0)
+    grad_down_t[...] = value(1)
+    attn = value(2)
+    tails = [attn[:, 512:576], attn[:, 576:640], attn[:, 640:704], attn[:, 704:768]]
+    for i in range(3):
+        grad_attn[i, :, 0:128] = attn[:, 128 * i : 128 * i + 128]
+        grad_attn[i, :, 128:192] = tails[i]
+    grad_out[...] = jnp.concatenate([attn[:, 384:512], tails[3]], axis=1).T
+    for copy in copies:
+        copy.wait()
+    patch_grad[...] = patch_low[...].reshape(patch_grad.shape).astype(f32)
+
+
+def place(order, row_count, rows_all, grads, all_total, part_total):
+    shape = jax.ShapeDtypeStruct
+    width = rows_all.shape[3]
+    deep = grads.shape[1] * grads.shape[2]
+    vector = shape((width,), f32)
+    return pl.pallas_call(
+        place_kernel,
+        out_shape=(
+            shape((row_count, width), bf16), shape((row_count, width), f32), vector, vector,
+            shape((3, deep, 192), f32), shape((2, 192), f32), shape((192, deep), f32), vector, vector, vector,
+            shape((deep, width), f32), vector, shape((deep, width), f32), vector,
+        ),
+        in_specs=[SMEM, ANY] + [VMEM] * 3,
+        out_specs=(VMEM,) * 14,
+        scratch_shapes=[
+            pltpu.VMEM((row_count // UNIT, UNIT, width), bf16),
+            pltpu.SemaphoreType.DMA((2, row_count // BLOCK)),
+        ],
+        compiler_params=pltpu.CompilerParams(vmem_limit_bytes=LIMIT),
+        name="place",
+    )(order, rows_all, grads, all_total, part_total)
 
 
 def tree_shards(
     fsdp_count, patches, out_grad, block_order, first_gain, first_shift, attn_proj, attn_bias, out_proj, out_bias,
     second_gain, second_shift, up_proj, up_bias, down_proj, down_bias,
 ):
-    row = lambda vector: vector.reshape(1, -1)
-    order = block_order[0]
-    slots = jnp.arange(order.shape[0], dtype=jnp.int32)
-    unit_count = BLOCK // UNIT
-    where = unit_count * jnp.sum(
-        jnp.where(order[None, :] == slots[:, None], slots[None, :], 0), axis=1, dtype=jnp.int32
-    )
-    branch, leaf = order - TRUNK_BLK, order - TRUNK_BLK - BRANCHES
-    gathered = unit_count * jnp.where(
-        order < TRUNK_BLK,
-        5 * (order // 2) + order % 2,
-        jnp.where(branch < BRANCHES, 5 * branch + 3, 5 * (leaf // 2) + 2 + 2 * (leaf % 2)),
-    )
-    own = patches.shape[0] // BLOCK
-    gathered = lax.dynamic_slice_in_dim(gathered, lax.axis_index("context") * own, own)
-    head_width = attn_bias.shape[1]
-    bias = jnp.zeros((8, up_bias.shape[0]), f32)
-    bias = bias.at[0].set(up_bias).at[1:3, :head_width].set(attn_bias)
     middle = first_half(
-        fsdp_count, where, patches, out_grad, attn_proj, out_proj, up_proj, down_proj, bias,
-        row(first_gain), row(first_shift), row(second_gain), row(second_shift), row(out_bias), row(down_bias),
-    )
-    result, patch_grad, grad_attn, grad_out, grad_up, grad_down, all_total, part_total = second_half(
-        fsdp_count, gathered, *middle, row(first_gain)
-    )
-    core = lax.axis_index("tensor") % 2
-    up_total = lax.dynamic_index_in_dim(part_total, core, 0, keepdims=False)
-    attn_total = part_total[2].reshape(2, 384)
-    attn_total = jnp.concatenate(
-        [
-            lax.dynamic_slice_in_dim(attn_total, core * 128, 128, 1),
-            lax.dynamic_slice_in_dim(attn_total, 256 + core * 64, 64, 1),
-        ],
-        axis=1,
-    )
-    return (
-        result,
-        patch_grad,
-        all_total[0],
-        all_total[1],
-        grad_attn,
-        attn_total,
-        grad_out,
-        all_total[5],
-        all_total[2],
-        all_total[3],
-        grad_up,
-        up_total,
-        grad_down,
-        all_total[4],
-    )
+        fsdp_count, block_order, patches, out_grad, attn_proj, out_proj, up_proj, down_proj.T, up_bias, attn_bias,
+        first_gain, first_shift, second_gain, second_shift, out_bias, down_bias,
+    )
+    sums = second_half(fsdp_count, patches.shape[0], *middle, first_gain)
+    outputs = list(place(block_order, patches.shape[0], *sums))
+    outputs[12] = outputs[12].T
+    return tuple(outputs)
 
 
 def solution(mesh):

time: 238 us -> 214 us (0.90)
  local copies, waits for them, and re-layouts: 23.6 us -> 0 us
    unnamed x19 -> x0, local copies, waits for them, and re-layouts: 11.4 us -> none
    reshape x6 -> x0, local copies, waits for them, and re-layouts: 7.61 us -> none  [tree_shards(): row = lambda vector: vector.reshape(1, -1)]
    pallas_call x1 -> x2, Pallas kernels: 108 us -> 109 us  [the longest x1 102 us: second_half(): pl.pallas_call(partial(second_kernel, fsdp_count), out_shape=(shape((2, 2...]
where the time goes in v3:
time: 214 us
  Pallas kernels  213 us (100%)
    pallas_call x1, Pallas kernels, first_half(): pl.pallas_call(partial(first_kernel, fsdp_count), out_shape=(shape((OWN,...  104 us
    pallas_call x1, Pallas kernels, second_half(): pl.pallas_call(partial(second_kernel, fsdp_count), out_shape=(shape((2, 2...  102 us
    pallas_call x1, Pallas kernels, place(): pl.pallas_call(place_kernel, out_shape=(shape((row_count, width), bf16),...  6.91 us

profile of v3, /device:TPU:0, one launch (start us, length us, event | category | flops | bytes accessed | tf_op | source)
XLA Modules:
  0.0 214.3 jit_solution(9444364514625637689)
XLA Ops:
  0.7 104.1 %first_half.1 = (bf16[640,384]{1,0:T(8,128)(2,1)}, bf16[1408,384]{1,0:T(8,128)(2,1)}, bf16[1408,384]{1,0:T(8,128)(2,1)}, bf16[384,1408]{1,0:T(8,128)(2,1)}, bf16...) custom-call(s32[1,20]{1,0:T(1,128)} %order.3, ...), custom_call_target="tpu_custom_call" | custom-call | tf_op jit(solution)/shard_map/first_half/pallas_call | solution.py:757
  104.7 102.4 %second_half.1 = (bf16[2,80,32,768]{3,2,1,0:T(8,128)(2,1)}, bf16[3,2,96,768]{3,2,1,0:T(8,128)(2,1)}, f32[6,768]{1,0:T(8,128)}, f32[3,768]{1,0:T(4,128)}) custom-call(bf16[640,384]{1,0:T(8,128)(2,1)} %get-tuple-element.51.q_in, bf16[1408,384]{1,0:T(8,128)(2,1)} %get-tuple-element.52.k_in, bf16[1408,384]{1,0:T(8,128)(2,1)} %get-tuple-element.53.v_in, ...), custom_call_target="tpu_custom_call" | custom-call | tf_op jit(solution)/shard_map/second_half/pallas_call | solution.py:1178
  207.2 6.9 %place.1 = (bf16[1280,768]{1,0:T(8,128)(2,1)}, f32[1280,768]{1,0:T(8,128)}, f32[768]{0:T(1024)}, f32[768]{0:T(1024)}, f32[3,192,192]{2,1,0:T(8,128)}, /*index=5*...) custom-call(s32[1,20]{1,0:T(1,128)} %order.3, ...), custom_call_target="tpu_custom_call" | custom-call | tf_op jit(solution)/shard_map/place/pallas_call | solution.py:1294

commit v4 on v3

--- a/solution.py
+++ b/solution.py
@@ -306,7 +306,7 @@
 SMEM = pl.BlockSpec(memory_space=pltpu.SMEM)
 ANY = pl.BlockSpec(memory_space=pl.ANY)
 MESH = pl.DeviceIdType.MESH
-LIMIT = 60 * 1024 * 1024
+LIMIT = 61 * 1024 * 1024
 
 
 def dot_nn(a, b):
@@ -403,7 +403,7 @@
     return center * inverse, inverse
 
 HALF = OWN // 2
-UNIT = 32
+UNIT = 16
 
 
 def wide(vector):
@@ -412,11 +412,11 @@
 
 def first_kernel(
     fsdp_count, order, patches, grads, attn_proj, out_proj, up, d_own, up_bias, attn_bias, gain1, shift1, gain2, shift2, out_bias, down_bias,
-    q_out, k_out, v_out, kt_out, att_out, low_out, x_out, wh_out, g_up_out, g_down_out,
+    q_out, k_out, v_out, att_out, low_out, x_out, wh_out, g_up_out, g_down_out,
     lse, da, middle_grad, mlp_own, mlp_send, g_out_own, g_out_send, stats, up_stats,
     where, a_own, bias, rows_all, grads_all, wa, wh, wo_x, wu, wd, bias_all,
-    low, low_own, x_own, g_own, q, k, v, kt, vt, attended, att_t, att_x, st, pt,
-    middle, normed, inverse, low2, hidden, pre_grad, second, second_send, second_x, da_send, g_up, g_down,
+    low_all, low, low_own, x_own, g_own, q, k, v, vt, attended, att_t, att_x, st, pt,
+    middle, normed, inverse, low2, hidden, pre_grad, second, second_send, second_x, branch, da_send, g_up, g_down, g_sum,
     local, ss, rs,
 ):
     me = Here(fsdp_count)
@@ -426,9 +426,7 @@
     part = units // 4
     width = patches.shape[2]
     deep = up.shape[0]
-    half = deep // 2
     head_width = attn_proj.shape[2]
-    early = 640
     own_copies = []
 
     def keep(src, dst):
@@ -453,13 +451,14 @@
     greet([me.core, me.xp, me.yp] + me.z)
     post = Post(ss, rs)
     there = units * (1 - c)
+    half = deep // 2
     strip, other_strip = half * c, half * (1 - c)
 
-    def quarter(array, index, piece, count=2):
+    def quarter(array, index, piece, count):
         size = part // count
         return array.at[pl.ds(there + part * index + size * piece, size)]
 
-    def to_y(src, dst, piece, count=2):
+    def to_y(src, dst, piece, count):
         size = part // count
         return post.send(
             src.at[pl.ds(part * t + size * piece, size)],
@@ -470,77 +469,104 @@
     def relay(piece, device):
         return post.send(piece, piece, device)
 
-    a_dst = lambda shard, row, lanes: wa.at[shard, ds(row, half), lanes]
-    lo, hi = pl.ds(0, early), pl.ds(early, width - early)
-    patches_y = [to_y(patches, rows_all, i) for i in range(2)]
-    a1_z = [
-        post.send(a_own.at[ds(strip, half), lo], a_dst(core, deep * f + strip, lo), device) for device in me.z
+    part_rows = half // 2
+    a_part = lambda source, row, count: wa.at[core, ds(deep * source + row, count)]
+    pieces = 4
+    patches_y = [to_y(patches, rows_all, i, pieces) for i in range(pieces)]
+    a_z = [
+        [
+            post.send(
+                a_own.at[ds(strip + part_rows * i, part_rows)], a_part(f, strip + part_rows * i, part_rows), device
+            )
+            for device in me.z
+        ]
+        for i in range(2)
     ]
-    a_core = post.send(a_own, wa.at[core, ds(deep * f, deep)], me.core)
-    bias_core = post.send(bias, bias_all.at[core], me.core)
-    u_core = post.send(up, wu.at[core, ds(deep * f, deep)], me.core)
+    post.send(a_own, wa.at[core, ds(deep * f, deep)], me.core)
+    post.send(bias, bias_all.at[core], me.core)
+    gain_row, shift_row = wide(gain1), wide(shift1)
+
+    def norm_units(start, count):
+        values = rows_all[pl.ds(start, count)].reshape(count * UNIT, width).astype(f32)
+        normed_rows, _ = row_norm(values)
+        low_rows = (normed_rows * gain_row + shift_row).astype(bf16)
+        low_all[pl.ds(start, count)] = low_rows.reshape(count, UNIT, width)
+
+    block_units = BLOCK // UNIT
+    own_blocks = units // block_units
+
+    def norm_own(j, carried):
+        norm_units(units * c + block_units * j, block_units)
+        return carried
+
     slots = order.shape[1]
 
     def find(place, carried):
         slot = jnp.int32(0)
         for j in range(slots):
             slot = jnp.where(order[0, j] == place, j, slot)
-        where[place] = slot * (BLOCK // UNIT)
+        where[place] = slot * block_units
         return carried
 
     lax.fori_loop(0, slots, find, 0)
     wa[core, ds(deep * f, deep), :] = a_own[...]
     bias_all[core] = bias[...]
-    d_core = post.send(d_own, wd.at[core, ds(deep * f, deep)], me.core)
-    patches_x = []
+    own_copies[0].wait()
+    lax.fori_loop(0, own_blocks - pieces, norm_own, 0)
+    size = part // pieces
+    over = (t + 2) % 4
+    beside, across = t + 1 - 2 * core, over + 1 - 2 * core
+    patches_x, patches_core = [], []
+    for i in range(pieces):
+        post.got(patches_y[i])
+        patches_x.append(relay(quarter(rows_all, t, i, pieces), me.xp))
+        patches_core.append(relay(quarter(rows_all, t, i, pieces), me.core))
+        norm_units(there + part * t + size * i, size)
+        norm_own(own_blocks - pieces + i, 0)
+    a_y = []
     for i in range(2):
-        post.got(patches_y[i])
-        patches_x.append(relay(quarter(rows_all, t, i), me.xp))
-        relay(quarter(rows_all, t, i), me.core)
-    a1_y = []
-    for copy, source in zip(a1_z, me.back):
-        post.got(copy)
-        piece = a_dst(core, deep * source + strip, lo)
-        a1_y.append(relay(piece, me.yp))
-        relay(piece, me.core)
-    a2_z = [
-        post.send(a_own.at[ds(strip, half), hi], a_dst(core, deep * f + strip, hi), device) for device in me.z
-    ]
+        for copy, source in zip(a_z[i], me.back):
+            post.got(copy)
+            piece = a_part(source, strip + part_rows * i, part_rows)
+            a_y.append(relay(piece, me.yp))
+            relay(piece, me.core)
+    grads_y = [to_y(grads, grads_all, i, 2) for i in range(2)]
     u_z = [
         post.send(up.at[ds(strip, half)], wu.at[core, ds(deep * f + strip, half)], device) for device in me.z
     ]
-    over = (t + 2) % 4
-    for i in range(2):
+    post.send(up, wu.at[core, ds(deep * f, deep)], me.core)
+    post.send(d_own, wd.at[core, ds(deep * f, deep)], me.core)
+    for i in range(pieces):
+        post.got(patches_core[i])
+        norm_units(there + part * beside + size * i, size)
+    patches_core = []
+    for i in range(pieces):
         post.got(patches_x[i])
-        relay(quarter(rows_all, over, i), me.core)
-    post.got_from(me.core)
-    own_copies[0].wait()
-
-    gain_row, shift_row = wide(gain1), wide(shift1)
+        patches_core.append(relay(quarter(rows_all, over, i, pieces), me.core))
+        norm_units(there + part * over + size * i, size)
+    for index, copy in enumerate(a_y):
+        post.got(copy)
+        source, i = me.back[index % len(me.back)], index // len(me.back)
+        relay(a_part(source, other_strip + part_rows * i, part_rows), me.core)
+    for i in range(pieces):
+        post.got(patches_core[i])
+        norm_units(there + part * across + size * i, size)
 
     def block_of(array, place):
-        return array[pl.ds(where[place], BLOCK // UNIT)].reshape(BLOCK, width)
-
-    def norm_block(place, row):
-        normed_rows, _ = row_norm(block_of(rows_all, place).astype(f32))
-        low[ds(row, BLOCK), :] = (normed_rows * gain_row + shift_row).astype(bf16)
+        return array[pl.ds(where[place], block_units)].reshape(BLOCK, width)
 
     def trunk_step(j, carried):
-        norm_block(j, j * BLOCK)
+        low[ds(j * BLOCK, BLOCK), :] = block_of(low_all, j)
         return carried
 
     lax.fori_loop(0, TRUNK_BLK, trunk_step, 0)
     places = own_places(s)
     for j in range(2, 5):
-        norm_block(places[j], TRUNK + (j - 2) * BLOCK)
+        low[TRUNK + (j - 2) * BLOCK : TRUNK + (j - 1) * BLOCK, :] = block_of(low_all, places[j])
     for j, place in enumerate(places):
         x_own[pl.ds(j * BLOCK, BLOCK), :] = block_of(rows_all, place)
     low_own[0 : 2 * BLOCK, :] = low[ds(2 * BLOCK * s, 2 * BLOCK), :]
     low_own[2 * BLOCK :, :] = low[TRUNK:, :]
-    for copy, source in zip(a1_y, me.back):
-        post.got(copy)
-        relay(a_dst(core, deep * source + other_strip, lo), me.core)
-    grads_y = [to_y(grads, grads_all, i) for i in range(2)]
     post.got_from(me.core)
 
     def assemble(i):
@@ -552,8 +578,11 @@
             [wa[0, :, start : start + 64], wa[1, :, start : start + 64]], axis=1
         )
 
-    for i in range(3):
+    for i in range(4):
         assemble(i)
+    wo_rows = ds(width // 2 * core, width // 2)
+    wo_copy = post.send(wh.at[3, wo_rows], wo_x.at[wo_rows], me.xp)
+    keep(wh, wh_out)
 
     def heads_row(row):
         a, b = bias_all[0, row : row + 1, :], bias_all[1, row : row + 1, :]
@@ -569,9 +598,8 @@
         return carried
 
     lax.fori_loop(0, 2, project, 0)
-    kt[...] = k[...].T
     vt[...] = v[...].T
-    for src, dst in ((q, q_out), (k, k_out), (v, v_out), (kt, kt_out), (low_own, low_out), (x_own, x_out)):
+    for src, dst in ((q, q_out), (k, k_out), (v, v_out), (low_own, low_out), (x_own, x_out)):
         keep(src, dst)
     lane = lax.broadcasted_iota(jnp.int32, (OWN, 128), 1) // HEAD_DIM
 
@@ -602,91 +630,89 @@
             tops.append(top)
             sums.append(jnp.sum(total, axis=0, keepdims=True))
         total = jnp.concatenate(sums, axis=1)
-        head_rows = ds(h * HEAD_DIM, HEAD_DIM)
-        att_t[head_rows, :] = dot_nn(vt[head_rows, 0:TRUNK], pt[0:TRUNK, :])
+        head_rows, side_rows = ds(h * HEAD_DIM, HEAD_DIM), ds(side * HEAD_DIM, HEAD_DIM)
+        att_t[side_rows, :] = dot_nn(vt[head_rows, 0:TRUNK], pt[0:TRUNK, :])
         for q_row, k_row, count in PIECES:
             cols = slice(q_row, q_row + BLOCK)
-            att_t[head_rows, cols] += dot_nn(
+            att_t[side_rows, cols] += dot_nn(
                 vt[head_rows, k_row : k_row + count], pt[TRUNK : TRUNK + count, cols]
             )
-        att_t[head_rows, :] = att_t[head_rows, :] / total
+        att_t[side_rows, :] = att_t[side_rows, :] / total
         lse[pl.ds(h, 1), :] = jnp.concatenate(tops, axis=1) + jnp.log(total)
         return carried
 
-    lax.fori_loop(0, 2, head, 0)
-    a2_y, u_y, grads_x = [], [], []
-    for copy, source in zip(a2_z, me.back):
-        post.got(copy)
-        piece = a_dst(core, deep * source + strip, hi)
-        a2_y.append(relay(piece, me.yp))
-        relay(piece, me.core)
-    post.got(grads_y[0])
-    grads_x.append(relay(quarter(grads_all, t, 0), me.xp))
-    relay(quarter(grads_all, t, 0), me.core)
-    for copy, source in zip(u_z, me.back):
-        post.got(copy)
-        piece = wu.at[core, ds(deep * source + strip, half)]
-        u_y.append(relay(piece, me.yp))
-        relay(piece, me.core)
+    mine, far = HALF * x, HALF * (1 - x)
+    here_rows, far_rows = ds(mine, HALF), ds(far, HALF)
+    att_copies = []
+
+    def slab_heads(slab):
+        lax.fori_loop(2 * slab, 2 * slab + 2, head, 0)
+        lanes = pl.ds(128 * slab, 128)
+        attended[:, lanes] = att_t[...].T.astype(bf16)
+        att_copies.append(post.send(attended.at[far_rows, lanes], att_x.at[:, lanes], me.xp))
+
+    def grads_on(i):
+        post.got(grads_y[i])
+        relay(quarter(grads_all, t, i, 2), me.core)
+        return relay(quarter(grads_all, t, i, 2), me.xp)
+
+    def strips_on(copies, array):
+        passed = []
+        for copy, source in zip(copies, me.back):
+            post.got(copy)
+            piece = array.at[core, ds(deep * source + strip, half)]
+            passed.append(relay(piece, me.yp))
+            relay(piece, me.core)
+        return passed
+
+    def strips_in(copies, array):
+        for copy, source in zip(copies, me.back):
+            post.got(copy)
+            relay(array.at[core, ds(deep * source + other_strip, half)], me.core)
+
+    grads_x = [grads_on(0)]
+    u_y = strips_on(u_z, wu)
     d_z = [
         post.send(d_own.at[ds(strip, half)], wd.at[core, ds(deep * f + strip, half)], device) for device in me.z
     ]
-    lax.fori_loop(2, 4, head, 0)
-    post.got(grads_y[1])
-    grads_x.append(relay(quarter(grads_all, t, 1), me.xp))
-    relay(quarter(grads_all, t, 1), me.core)
-    for copy, source in zip(a2_y, me.back):
-        post.got(copy)
-        relay(a_dst(core, deep * source + other_strip, hi), me.core)
-    lax.fori_loop(4, 6, head, 0)
-    attended[...] = att_t[...].T.astype(bf16)
-    mine, far = HALF * x, HALF * (1 - x)
-    here_rows, far_rows = ds(mine, HALF), ds(far, HALF)
-    att_copy = post.send(attended.at[far_rows], att_x, me.xp)
+    slab_heads(0)
+    grads_x.append(grads_on(1))
+    slab_heads(1)
+    post.got(wo_copy)
+    relay(wo_x.at[wo_rows], me.core)
+    slab_heads(2)
     keep(attended, att_out)
-    post.got_from(me.core)
-    assemble(3)
-    keep(wh, wh_out)
-    wo_rows = ds(width // 2 * core, width // 2)
-    wo_copy = post.send(wh.at[3, wo_rows], wo_x.at[wo_rows], me.xp)
     middle[...] = (
         x_own[here_rows, :].astype(f32) + wide(out_bias) + dot_nt(attended[here_rows, :], wh[3])
     )
-    d_y = []
-    for copy, source in zip(d_z, me.back):
-        post.got(copy)
-        piece = wd.at[core, ds(deep * source + strip, half)]
-        d_y.append(relay(piece, me.yp))
-        relay(piece, me.core)
-    post.got(wo_copy)
-    relay(wo_x.at[wo_rows], me.core)
     for i in range(2):
         post.got(grads_x[i])
-        relay(quarter(grads_all, over, i), me.core)
+        relay(quarter(grads_all, over, i, 2), me.core)
+    strips_in(u_y, wu)
     post.got_from(me.core)
-    post.got(att_copy)
+    for copy in att_copies:
+        post.got(copy)
     middle[...] += dot_nt(att_x[...], wo_x[...])
     n2, s2 = row_norm(middle[...])
     normed[...] = n2
     inverse[...] = s2
     low2[here_rows, :] = (n2 * wide(gain2) + wide(shift2)).astype(bf16)
-    low_copy = post.send(low2.at[here_rows], low2.at[here_rows], me.xp)
+    chunk = HALF // 2
+    here_chunks = [ds(mine + chunk * i, chunk) for i in range(2)]
+    far_chunks = [ds(far + chunk * i, chunk) for i in range(2)]
+    low_copies = [post.send(low2.at[rows], low2.at[rows], me.xp) for rows in here_chunks]
     own_copies[1].wait()
     for j, place in enumerate(places):
         g_own[pl.ds(j * BLOCK, BLOCK), :] = block_of(grads_all, place)
-    for copy, source in zip(u_y, me.back):
-        post.got(copy)
-        relay(wu.at[core, ds(deep * source + other_strip, half)], me.core)
-    for copy, source in zip(d_y, me.back):
-        post.got(copy)
-        relay(wd.at[core, ds(deep * source + other_strip, half)], me.core)
-    post.got_from(me.core)
+    d_y = strips_on(d_z, wd)
     own_copies[2].wait()
     own_copies[3].wait()
+    strips_in(d_y, wd)
+    post.got_from(me.core)
     tile = 256
 
-    def feed(rows):
-        second[rows, :] = jnp.zeros((HALF, width), f32)
+    def feed(rows, count):
+        second[rows, :] = jnp.zeros((count, width), f32)
 
         def step(j, carried):
             shard, lanes = j // 3, pl.ds(pl.multiple_of(j % 3 * tile, 128), tile)
@@ -706,41 +732,64 @@
     def mlp(rows):
         return dot_nt(hidden[rows, 0:width], wd[0]) + dot_nt(hidden[rows, width:], wd[1])
 
-    feed(here_rows)
-    post.got(low_copy)
-    feed(far_rows)
-    second_send[...] = second[far_rows, :].astype(bf16)
-    second_copy = post.send(second_send, second_x, me.xp)
-
-    def weight_step(j, carried):
-        lanes = pl.ds(pl.multiple_of(j * tile, 128), tile)
-        g_up[:, lanes] = dot_tn(low2[...], pre_grad[:, lanes]).astype(bf16)
-        g_down[:, lanes] = dot_tn(g_own[...], hidden[:, lanes]).astype(bf16)
-        return carried
-
-    lax.fori_loop(0, 6, weight_step, 0)
-    keep(g_up, g_up_out)
-    keep(g_down, g_down_out)
+    second_copies = []
+    for i in range(2):
+        post.got(low_copies[i])
+        feed(far_chunks[i], chunk)
+        second_send[i] = second[far_chunks[i], :].astype(bf16)
+        second_copies.append(post.send(second_send.at[i], second_x.at[i], me.xp))
+    feed(here_rows, HALF)
+
+    own_lanes, sibling_lanes = (
+        pl.ds(pl.multiple_of(width * side, 128), width) for side in (core, 1 - core)
+    )
+    sibling_copies = []
+    for index, (left, right, grad) in enumerate(((low2, pre_grad, g_up), (g_own, hidden, g_down))):
+
+        def weight_step(j, carried):
+            lanes = pl.ds(pl.multiple_of(j * tile, 128), tile)
+            grad[:, lanes] = dot_tn(left[...], right[:, lanes]).astype(bf16)
+            return carried
+
+        lax.fori_loop(0, 6, weight_step, 0)
+        sibling_copies.append(post.send(grad.at[:, sibling_lanes], g_sum.at[index], me.core))
     up_stats[0:1, :] = jnp.sum(pre_grad[:, 0:width].astype(f32), axis=0, keepdims=True)
     up_stats[1:2, :] = jnp.sum(pre_grad[:, width:].astype(f32), axis=0, keepdims=True)
     mlp_send[...] = mlp(far_rows).astype(bf16)
     mlp_own[...] = middle[...] + mlp(here_rows) + wide(down_bias)
-    dy = g_own[here_rows, :].astype(f32)
-    stats[2:3, :] = jnp.sum(dy, axis=0, keepdims=True)
-    post.got(second_copy)
-    second_grad = second[here_rows, :] + second_x[...].astype(f32)
-    n2 = normed[...]
-    stats[0:1, :] = jnp.sum(second_grad * n2, axis=0, keepdims=True)
-    stats[1:2, :] = jnp.sum(second_grad, axis=0, keepdims=True)
-    grad = dy + norm_back(second_grad, n2, inverse[...], wide(gain2))
-    middle_grad[...] = grad
-    branch = grad.astype(bf16)
-    da_send[...] = dot_nn(branch, wo_x[...]).astype(bf16)
-    post.send(da_send, da.at[here_rows], me.xp)
-    stats[3:4, :] = jnp.sum(branch.astype(f32), axis=0, keepdims=True)
-    da[here_rows, :] = dot_nn(branch, wh[3]).astype(bf16)
-    g_out_send[...] = dot_tn(branch, att_x[...]).astype(bf16)
-    g_out_own[...] = dot_tn(branch, attended[here_rows, :]).astype(bf16)
+    total = [jnp.zeros((1, width), f32)] * 4
+    for i in range(2):
+        rows = here_chunks[i]
+        part_rows = slice(chunk * i, chunk * i + chunk)
+        post.got(second_copies[i])
+        second_grad = second[rows, :] + second_x[i].astype(f32)
+        n2 = normed[part_rows, :]
+        dy = g_own[rows, :].astype(f32)
+        grad = dy + norm_back(second_grad, n2, inverse[part_rows, :], wide(gain2))
+        middle_grad[part_rows, :] = grad
+        low_grad = grad.astype(bf16)
+        branch[part_rows, :] = low_grad
+        da_send[part_rows, :] = dot_nn(low_grad, wo_x[...]).astype(bf16)
+        post.send(da_send.at[pl.ds(chunk * i, chunk)], da.at[rows], me.xp)
+        terms = (second_grad * n2, second_grad, dy, low_grad.astype(f32))
+        total = [a + jnp.sum(b, axis=0, keepdims=True) for a, b in zip(total, terms)]
+    for i in range(4):
+        stats[i : i + 1, :] = total[i]
+    da[here_rows, :] = dot_nn(branch[...], wh[3]).astype(bf16)
+    g_out_send[...] = dot_tn(branch[...], att_x[...]).astype(bf16)
+    g_out_own[...] = dot_tn(branch[...], attended[here_rows, :]).astype(bf16)
+    for index, (grad, out) in enumerate(((g_up, g_up_out), (g_down, g_down_out))):
+        post.got(sibling_copies[index])
+
+        def add_sibling(j, carried):
+            rows = ds(j * BLOCK, BLOCK)
+            g_sum[index, rows, :] = (
+                g_sum[index, rows, :].astype(f32) + grad[rows, own_lanes].astype(f32)
+            ).astype(bf16)
+            return carried
+
+        lax.fori_loop(0, width // BLOCK, add_sibling, 0)
+        keep(g_sum.at[index], out)
     post.close()
     for copy in own_copies[4:]:
         copy.wait()
@@ -760,13 +809,12 @@
             shape((OWN, 384), bf16),
             shape((KEYS, 384), bf16),
             shape((KEYS, 384), bf16),
-            shape((384, KEYS), bf16),
             shape((OWN, 384), bf16),
             shape((OWN, width), bf16),
             shape((OWN, width), bf16),
             shape((4, width, 384), bf16),
-            shape((width, units), bf16),
-            shape((width, units), bf16),
+            shape((width, width), bf16),
+            shape((width, width), bf16),
             shape((8, OWN), f32),
             shape((OWN, 384), bf16),
             shape((HALF, width), f32),
@@ -778,7 +826,7 @@
             shape((2, width), f32),
         ),
         in_specs=[SMEM, ANY, ANY, VMEM, VMEM, ANY, ANY] + [VMEM] * 8,
-        out_specs=(ANY,) * 10 + (VMEM,) * 9,
+        out_specs=(ANY,) * 9 + (VMEM,) * 9,
         scratch_shapes=[
             pltpu.SMEM(order.shape[1:], jnp.int32),
             vmem((deep, width), bf16),
@@ -791,6 +839,7 @@
             vmem((2, width, up.shape[1]), bf16),
             vmem((2, width, up.shape[1]), bf16),
             vmem((2, 8, width), f32),
+            vmem((all_units, UNIT, width), bf16),
             vmem((KEYS, width), bf16),
             vmem((OWN, width), bf16),
             vmem((OWN, width), bf16),
@@ -799,9 +848,8 @@
             vmem((KEYS, 384), bf16),
             vmem((KEYS, 384), bf16),
             vmem((384, KEYS), bf16),
-            vmem((384, KEYS), bf16),
             vmem((OWN, 384), bf16),
-            vmem((384, OWN), f32),
+            vmem((128, OWN), f32),
             vmem((HALF, 384), bf16),
             vmem((TRUNK + 2 * BLOCK, OWN), f32),
             vmem((TRUNK + 2 * BLOCK, OWN), bf16),
@@ -812,14 +860,16 @@
             vmem((OWN, units), bf16),
             vmem((OWN, units), bf16),
             vmem((OWN, width), f32),
-            vmem((HALF, width), bf16),
+            vmem((2, HALF // 2, width), bf16),
+            vmem((2, HALF // 2, width), bf16),
             vmem((HALF, width), bf16),
             vmem((HALF, 384), bf16),
             vmem((width, units), bf16),
             vmem((width, units), bf16),
+            vmem((2, width, width), bf16),
             pltpu.SemaphoreType.DMA((16,)),
-            pltpu.SemaphoreType.DMA((80,)),
-            pltpu.SemaphoreType.DMA((80,)),
+            pltpu.SemaphoreType.DMA((112,)),
+            pltpu.SemaphoreType.DMA((112,)),
         ],
         compiler_params=pltpu.CompilerParams(collective_id=0, has_side_effects=True, vmem_limit_bytes=LIMIT),
         name="first_half",
@@ -831,7 +881,7 @@
         self.me, self.post, self.count = me, post, fsdp_count
         self.held, self.from_core = held, from_core
         self.from_y, self.from_z, self.done = buffers
-        self.half = from_core.shape[0] // fsdp_count // 2
+        self.half = held.shape[0] // fsdp_count // 2
 
     def from_sibling(self, src):
         self.core_copy = self.post.send(src, self.from_core, self.me.core)
@@ -872,6 +922,23 @@
             self.post.send(self.held.at[self.strip((me.f + i + 1) % self.count, me.c)], self.from_z.at[i], device)
             for i, device in enumerate(me.z)
         ]
+
+    def over_z_first(self):
+        me, deep = self.me, 2 * self.half
+        self.z_copies = [
+            self.post.send(self.held.at[ds(deep * ((me.f + i + 1) % self.count), deep)], self.from_z.at[i], device)
+            for i, device in enumerate(me.z)
+        ]
+
+    def finish_z_first(self):
+        me, deep = self.me, 2 * self.half
+        for copy in self.z_copies:
+            self.post.got(copy)
+        total = self.held[ds(deep * me.f, deep), :].astype(f32)
+        for i in range(self.count - 1):
+            total = total + self.from_z[i].astype(f32)
+        self.done[0] = total.astype(bf16)
+        self.last = self.post.send(self.done.at[0], self.done.at[1], me.yp)
 
     def finish(self):
         me = self.me
@@ -885,13 +952,13 @@
 
 
 def second_kernel(
-    fsdp_count, q_in, k_in, v_in, kt_in, att_in, low_in, x_in, wh_in, g_up, g_down,
+    fsdp_count, q_in, k_in, v_in, att_in, low_in, x_in, wh_in, g_up, g_down,
     lse, da, middle_grad, mlp_own, mlp_send, g_out_own, g_out_send, mid_stats, up_stats, gain1,
-    rows_out, grads_out, all_total, part_total,
+    rows_out, up_out, rest_out, all_total, part_total,
     q, k, v, kt, attended, low_own, x_own, wh, up_own, down_own,
-    delta, st, dpt, pt, dst, dk_acc, dv_acc, dq_t, dq, trunk, trunk_own, trunk_far, trunk_send, trunk_y, dkv_own,
+    delta, st, dpt, pt, dst, dk_acc, dv_acc, dq_t, dq, own_first, trunk, trunk_own, trunk_far, trunk_send, trunk_y, dkv_own,
     mlp_x, first_send, first_x, rows_own, out_core, out_sum, out_x, packed,
-    from_core, from_y, from_z, done, stat_buf, stat_in, stat_z, local, ss, rs,
+    from_core, from_y, from_z, done, deep_z, deep_done, stat_buf, stat_in, stat_z, local, ss, rs,
 ):
     me = Here(fsdp_count)
     f, c, x, core = me.f, me.c, me.x, me.k
@@ -899,16 +966,11 @@
     pair = 2 * BLOCK
     units = HALF // UNIT
     width = x_in.shape[1]
-    shard = width
     mine, far = HALF * x, HALF * (1 - x)
     here_rows, far_rows = ds(mine, HALF), ds(far, HALF)
     loads = []
-    own_lanes, sibling_lanes = pl.ds(pl.multiple_of(shard * core, 128), shard), pl.ds(
-        pl.multiple_of(shard * (1 - core), 128), shard
-    )
     for src, held in (
-        (k_in, k), (q_in, q), (v_in, v), (att_in, attended), (kt_in, kt),
-        (g_up.at[:, own_lanes], up_own), (g_down.at[:, own_lanes], down_own),
+        (g_up, up_own), (g_down, down_own), (k_in, k), (q_in, q), (v_in, v), (att_in, attended),
         (low_in, low_own), (x_in, x_own), (wh_in.at[pl.ds(0, 3)], wh),
     ):
         copy = pltpu.make_async_copy(src, held, local.at[len(loads)])
@@ -917,12 +979,11 @@
     greet([me.core, me.xp, me.yp] + me.z)
     post = Post(ss, rs)
     mlp_copy = post.send(mlp_send, mlp_x, me.xp)
+    buffers = [(from_y, from_z, done)] + [(None, deep_z.at[i], deep_done.at[i]) for i in range(2)]
     sums = [
-        StripSum(me, post, fsdp_count, held, from_core.at[i], (from_y.at[i], from_z.at[i], done.at[i]))
-        for i, held in enumerate((up_own, down_own, packed.at[core]))
+        StripSum(me, post, fsdp_count, held, from_core, buffer)
+        for held, buffer in zip((up_own, down_own, packed.at[core]), buffers)
     ]
-    sums[0].from_sibling(g_up.at[:, sibling_lanes])
-    sums[1].from_sibling(g_down.at[:, sibling_lanes])
     slab_own = pl.ds(pl.multiple_of(128 * core, 128), 128)
     slab_sibling = pl.ds(pl.multiple_of(128 * (1 - core), 128), 128)
     slab_both = pl.ds(256, 128)
@@ -930,8 +991,13 @@
     for i, src in enumerate((g_out_own, g_out_send)):
         for j, lanes in enumerate((slab_sibling, slab_both)):
             out_copies.append(post.send(src.at[:, lanes], out_core.at[i, j], me.core))
-    for copy in loads[:5]:
+    for copy in loads[:2]:
         copy.wait()
+    sums[0].over_y()
+    sums[1].over_z_first()
+    for copy in loads[2:6]:
+        copy.wait()
+    kt[...] = k[...].T
     product = (da[...].astype(f32) * attended[...].astype(f32)).T
     for h in range(6):
         delta[h : h + 1, :] = jnp.sum(product[h * HEAD_DIM : (h + 1) * HEAD_DIM], axis=0, keepdims=True)
@@ -1013,26 +1079,67 @@
 
     slab_heads(0)
     trunk_out(0)
-    for copy in loads[5:]:
-        copy.wait()
-    sums[0].add_sibling()
-    sums[0].over_y()
-    trunk_over(0)
-    slab_heads(1)
-    trunk_out(1)
     for copy in out_copies:
         post.got(copy)
     for i, src in enumerate((g_out_own, g_out_send)):
         for j, lanes in enumerate((slab_own, slab_both)):
             out_sum[i, j] = (src[:, lanes].astype(f32) + out_core[i, j].astype(f32)).astype(bf16)
     out_copy = post.send(out_sum.at[1], out_x, me.xp)
+    for copy in loads[6:]:
+        copy.wait()
+    trunk_over(0)
+    slab_heads(1)
+    trunk_out(1)
+    post.got(mlp_copy)
+    rows_own[0] = (mlp_own[...] + mlp_x[...].astype(f32)).astype(bf16).reshape(units, UNIT, width)
+    beside = 2 * s + 1 - x
+    beyond = 2 * (2 * (1 - c) + core) + x
+    corner = 2 * (2 * (1 - c) + core) + 1 - x
+    part = units // 2
+    over_x, over_y, diagonal = {}, {}, {}
+
+    def piece(index, owner, half):
+        return rows_out.at[index, pl.ds(units * owner + part * half, part)]
+
+    def own_piece(index, half):
+        return rows_own.at[index, pl.ds(part * half, part)], piece(index, 2 * s + x, half)
+
+    def spread_x(index, half):
+        own, there = own_piece(index, half)
+        over_x[index, half] = post.send(own, there, me.xp)
+        post.send(own, there, me.core)
+        copy = pltpu.make_async_copy(own, there, local.at[len(loads)])
+        copy.start()
+        loads.append(copy)
+
+    def spread_y(index, half):
+        own, there = own_piece(index, half)
+        over_y[index, half] = post.send(own, there, me.yp)
+
+    def pass_on(index, half):
+        for copies, owner, onward in ((over_x, beside, me.yp), (over_y, beyond, me.xp)):
+            post.got(copies[index, half])
+            got = piece(index, owner, half)
+            if (half == 0) == (onward is me.yp):
+                diagonal[index, half] = post.send(got, got, onward)
+            post.send(got, got, me.core)
+
+    def corner_on(index):
+        for half in range(2):
+            post.got(diagonal[index, half])
+            got = piece(index, corner, half)
+            post.send(got, got, me.core)
+
+    for half in range(2):
+        spread_x(0, half)
     trunk_over(1)
-    sums[1].add_sibling()
+    sums[0].over_z()
     slab_heads(2)
     trunk_out(2)
     dq[...] = (dq_t[...].T * HEAD_DIM ** (-0.5)).astype(bf16)
     trunk_over(2)
-    sums[0].over_z()
+    for half in range(2):
+        spread_y(0, half)
     for slab in range(3):
         trunk_in(slab)
 
@@ -1043,12 +1150,12 @@
             + dot_nt(dkv_own[rows, 384:768], wh[2])
         )
 
-    first_send[...] = first(far_rows).astype(bf16)
-    first_copy = post.send(first_send, first_x, me.xp)
-    sums[1].over_y()
-    own_first = first(here_rows)
-    post.got(mlp_copy)
-    rows_own[0] = (mlp_own[...] + mlp_x[...].astype(f32)).astype(bf16).reshape(units, UNIT, width)
+    chunk = HALF // 2
+    first_copies = []
+    for i in range(2):
+        first_send[i] = first(ds(far + chunk * i, chunk)).astype(bf16)
+        first_copies.append(post.send(first_send.at[i], first_x.at[i], me.xp))
+    own_first[...] = first(here_rows)
     post.got(out_copy)
     g_attn = [
         dot_tn(low_own[...], dq[...]),
@@ -1070,58 +1177,35 @@
         axis=1,
     )
     sums[2].from_sibling(packed.at[1 - core])
+    def put_out():
+        packed[core, :, 384:512] = (out_sum[0, 0].astype(f32) + out_x[0].astype(f32)).astype(bf16)
+        last = out_sum[0, 1].astype(f32) + out_x[1].astype(f32)
+        side = lax.broadcasted_iota(jnp.int32, last.shape, 1) // HEAD_DIM
+        turned = jnp.concatenate([last[:, HEAD_DIM:], last[:, :HEAD_DIM]], axis=1)
+        tail = jnp.where(core == 0, turned, last)
+        packed[core, :, 640:768] = jnp.where(side == 0, packed[core, :, 640:768].astype(f32), tail).astype(bf16)
+
+    for half in range(2):
+        pass_on(0, half)
+    n1_all, s1_all = row_norm(x_own[here_rows, :].astype(f32))
+    first_total = [jnp.zeros((1, width), f32)] * 2
+    for i in range(2):
+        post.got(first_copies[i])
+        rows = slice(chunk * i, chunk * i + chunk)
+        first_grad = own_first[rows, :] + first_x[i].astype(f32)
+        n1, s1 = n1_all[rows], s1_all[rows]
+        grad = middle_grad[rows, :] + norm_back(first_grad, n1, s1, wide(gain1))
+        rows_own[1, part * i : part * i + part] = grad.astype(bf16).reshape(part, UNIT, width)
+        spread_x(1, i)
+        spread_y(1, i)
+        first_total = [
+            a + jnp.sum(b, axis=0, keepdims=True) for a, b in zip(first_total, (first_grad * n1, first_grad))
+        ]
     sums[2].add_sibling()
-    packed[core, :, 384:512] = (out_sum[0, 0].astype(f32) + out_x[0].astype(f32)).astype(bf16)
-    last = out_sum[0, 1].astype(f32) + out_x[1].astype(f32)
-    side = lax.broadcasted_iota(jnp.int32, last.shape, 1) // HEAD_DIM
-    turned = jnp.concatenate([last[:, HEAD_DIM:], last[:, :HEAD_DIM]], axis=1)
-    tail = jnp.where(core == 0, turned, last)
-    packed[core, :, 640:768] = jnp.where(side == 0, packed[core, :, 640:768].astype(f32), tail).astype(bf16)
-    post.got(first_copy)
-    first_grad = own_first + first_x[...].astype(f32)
-    n1, s1 = row_norm(x_own[here_rows, :].astype(f32))
-    grad = middle_grad[...] + norm_back(first_grad, n1, s1, wide(gain1))
-    rows_own[1] = grad.astype(bf16).reshape(units, UNIT, width)
-    beside = 2 * s + 1 - x
-    beyond = 2 * (2 * (1 - c) + core) + x
-    corner = 2 * (2 * (1 - c) + core) + 1 - x
-    near, over = {}, {}
-
-    def piece(index, owner, start, count):
-        return rows_out.at[index, pl.ds(units * owner + start, count)]
-
-    def spread(index):
-        own, there = rows_own.at[index], piece(index, 2 * s + x, 0, units)
-        near[index] = (post.send(own, there, me.xp), post.send(own, there, me.yp))
-        post.send(own, there, me.core)
-        copy = pltpu.make_async_copy(own, there, local.at[len(loads)])
-        copy.start()
-        loads.append(copy)
-
-    def pass_on(index):
-        quarter = units // 2
-        post.got(near[index][0])
-        part = piece(index, beside, 0, quarter)
-        diagonal = [post.send(part, part, me.yp)]
-        whole = piece(index, beside, 0, units)
-        post.send(whole, whole, me.core)
-        post.got(near[index][1])
-        part = piece(index, beyond, quarter, units - quarter)
-        diagonal.append(post.send(part, part, me.xp))
-        whole = piece(index, beyond, 0, units)
-        post.send(whole, whole, me.core)
-        over[index] = diagonal
-
-    def corner_on(index):
-        for copy in over[index]:
-            post.got(copy)
-        whole = piece(index, corner, 0, units)
-        post.send(whole, whole, me.core)
-
-    spread(1)
+    put_out()
+    sums[2].over_z_first()
     rows_mid, rows_up = mid_stats.shape[0], up_stats.shape[0]
-    stat_buf[0:1, :] = jnp.sum(first_grad * n1, axis=0, keepdims=True)
-    stat_buf[1:2, :] = jnp.sum(first_grad, axis=0, keepdims=True)
+    stat_buf[0:1, :], stat_buf[1:2, :] = first_total
     stat_buf[2 : 2 + rows_mid, :] = mid_stats[...]
     stat_buf[2 + rows_mid : 8, :] = jnp.zeros((6 - rows_mid, width), f32)
     stat_buf[8 : 8 + rows_up, :] = up_stats[...]
@@ -1129,28 +1213,24 @@
     stat_buf[9 + rows_up : 16, :] = jnp.zeros((7 - rows_up, width), f32)
     level = lambda i: pl.ds(16 * i, 16)
     stat_copy = post.send(stat_buf.at[level(0)], stat_in.at[0], me.core)
-    sums[2].over_y()
+    sums[0].finish()
     post.got(stat_copy)
     stat_buf[level(1), :] = stat_buf[level(0), :] + stat_in[0]
     stat_copy = post.send(stat_buf.at[level(1)], stat_in.at[1], me.yp)
-    sums[1].over_z()
-    sums[0].finish()
-    pass_on(1)
-    spread(0)
+    sums[1].finish_z_first()
+    corner_on(0)
     post.got(stat_copy)
     stat_buf[level(2), :] = stat_buf[level(1), :] + stat_in[1]
     stat_copy = post.send(stat_buf.at[level(2)], stat_in.at[2], me.xp)
-    sums[2].over_z()
-    corner_on(1)
-    pass_on(0)
+    pass_on(1, 0)
     post.got(stat_copy)
     stat_buf[48:56, :] = stat_buf[32:40, :] + stat_in[2, 0:8]
     stat_buf[56:64, :] = stat_buf[40:48, :]
     stat_z[f] = stat_buf[level(3), :]
     stat_copies = [post.send(stat_buf.at[level(3)], stat_z.at[f], device) for device in me.z]
-    sums[1].finish()
-    corner_on(0)
-    sums[2].finish()
+    pass_on(1, 1)
+    sums[2].finish_z_first()
+    corner_on(1)
     for copy in stat_copies:
         post.got(copy)
     total = stat_z[0]
@@ -1160,16 +1240,17 @@
     part_total[...] = total[8 : 9 + rows_up]
     for total in sums:
         post.got(total.last)
-    grads_out[...] = done[...]
+    up_out[...] = done[...]
+    rest_out[...] = deep_done[...]
     post.close()
-    for copy in loads[10:]:
+    for copy in loads[9:]:
         copy.wait()
 
 
 def second_half(fsdp_count, row_count, *operands):
     shape = jax.ShapeDtypeStruct
     vmem = pltpu.VMEM
-    width = operands[5].shape[1]
+    width = operands[4].shape[1]
     rows = row_count
     tall = TRUNK + 2 * BLOCK
     pair = 2 * BLOCK
@@ -1179,12 +1260,13 @@
         partial(second_kernel, fsdp_count),
         out_shape=(
             shape((2, 2 * rows // UNIT, UNIT, width), bf16),
-            shape((3, 2, half, width), bf16),
+            shape((2, half, width), bf16),
+            shape((2, 2, deep, width), bf16),
             shape((6, width), f32),
             shape((3, width), f32),
         ),
-        in_specs=[ANY] * 10 + [VMEM] * 10,
-        out_specs=(ANY,) + (VMEM,) * 3,
+        in_specs=[ANY] * 9 + [VMEM] * 10,
+        out_specs=(ANY,) + (VMEM,) * 4,
         scratch_shapes=[
             vmem((OWN, 384), bf16),
             vmem((KEYS, 384), bf16),
@@ -1205,6 +1287,7 @@
             vmem((KEYS, 128), f32),
             vmem((384, OWN), f32),
             vmem((OWN, 384), bf16),
+            vmem((HALF, width), f32),
             vmem((3, 2, TRUNK, 128), bf16),
             vmem((3, 2, pair, 128), bf16),
             vmem((3, 2, pair, 128), bf16),
@@ -1212,21 +1295,23 @@
             vmem((3, 2, pair, 128), bf16),
             vmem((OWN, 768), bf16),
             vmem((HALF, width), bf16),
-            vmem((HALF, width), bf16),
-            vmem((HALF, width), bf16),
+            vmem((2, HALF // 2, width), bf16),
+            vmem((2, HALF // 2, width), bf16),
             vmem((2, HALF // UNIT, UNIT, width), bf16),
             vmem((2, 2, width, 128), bf16),
             vmem((2, 2, width, 128), bf16),
             vmem((2, width, 128), bf16),
             vmem((2, width, width), bf16),
-            vmem((3, width, width), bf16),
-            vmem((3, fsdp_count, half, width), bf16),
-            vmem((3, fsdp_count - 1, half, width), bf16),
-            vmem((3, 2, half, width), bf16),
+            vmem((width, width), bf16),
+            vmem((fsdp_count, half, width), bf16),
+            vmem((fsdp_count - 1, half, width), bf16),
+            vmem((2, half, width), bf16),
+            vmem((2, fsdp_count - 1, deep, width), bf16),
+            vmem((2, 2, deep, width), bf16),
             vmem((64, width), f32),
             vmem((3, 16, width), f32),
             vmem((fsdp_count, 16, width), f32),
-            pltpu.SemaphoreType.DMA((12,)),
+            pltpu.SemaphoreType.DMA((16,)),
             pltpu.SemaphoreType.DMA((80,)),
             pltpu.SemaphoreType.DMA((80,)),
         ],
@@ -1236,7 +1321,7 @@
 
 
 def place_kernel(
-    order, rows_all, grads, all_total, part_total,
+    order, rows_all, up_sum, rest, all_total, part_total,
     result, patch_grad, gain1, shift1, grad_attn, attn_bias, grad_out, out_bias, gain2, shift2, grad_up, up_bias,
     grad_down_t, down_bias, patch_low, sems,
 ):
@@ -1271,11 +1356,9 @@
         first = jnp.where(core == 0, row[:, 0:128], row[:, 128:256])
         second = jnp.where(core == 0, row[:, 256:320], row[:, 320:384])
         attn_bias[i : i + 1, :] = jnp.concatenate([first, second], axis=1)
-    side, half, width = grads.shape[1:]
-    value = lambda i: grads[i].reshape(side * half, width).astype(f32)
-    grad_up[...] = value(0)
-    grad_down_t[...] = value(1)
-    attn = value(2)
+    grad_up[...] = up_sum[...].reshape(grad_up.shape).astype(f32)
+    grad_down_t[...] = rest[0, 0].astype(f32) + rest[0, 1].astype(f32)
+    attn = rest[1, 0].astype(f32) + rest[1, 1].astype(f32)
     tails = [attn[:, 512:576], attn[:, 576:640], attn[:, 640:704], attn[:, 704:768]]
     for i in range(3):
         grad_attn[i, :, 0:128] = attn[:, 128 * i : 128 * i + 128]
@@ -1286,10 +1369,10 @@
     patch_grad[...] = patch_low[...].reshape(patch_grad.shape).astype(f32)
 
 
-def place(order, row_count, rows_all, grads, all_total, part_total):
+def place(order, row_count, rows_all, up_sum, rest, all_total, part_total):
     shape = jax.ShapeDtypeStruct
     width = rows_all.shape[3]
-    deep = grads.shape[1] * grads.shape[2]
+    deep = rest.shape[2]
     vector = shape((width,), f32)
     return pl.pallas_call(
         place_kernel,
@@ -1298,7 +1381,7 @@
             shape((3, deep, 192), f32), shape((2, 192), f32), shape((192, deep), f32), vector, vector, vector,
             shape((deep, width), f32), vector, shape((deep, width), f32), vector,
         ),
-        in_specs=[SMEM, ANY] + [VMEM] * 3,
+        in_specs=[SMEM, ANY] + [VMEM] * 4,
         out_specs=(VMEM,) * 14,
         scratch_shapes=[
             pltpu.VMEM((row_count // UNIT, UNIT, width), bf16),
@@ -1306,7 +1389,7 @@
         ],
         compiler_params=pltpu.CompilerParams(vmem_limit_bytes=LIMIT),
         name="place",
-    )(order, rows_all, grads, all_total, part_total)
+    )(order, rows_all, up_sum, rest, all_total, part_total)
 
 
 def tree_shards(

time: 214 us -> 192 us (0.90); the launches traced: 214 us -> 189 us
  Pallas kernels: 213 us -> 188 us
    pallas_call x1, Pallas kernels: 102 us -> 81.1 us  [second_half(): pl.pallas_call(partial(second_kernel, fsdp_count), out_shape=(shape((2, 2...]
    pallas_call x1, Pallas kernels: 104 us -> 100 us  [first_half(): pl.pallas_call(partial(first_kernel, fsdp_count), out_shape=(shape((OWN,...]
where the time goes in v4:
time: 192 us; the launch traced here: 189 us
  Pallas kernels  188 us (98%)
    pallas_call x1, Pallas kernels, first_half(): pl.pallas_call(partial(first_kernel, fsdp_count), out_shape=(shape((OWN,...  100 us
    pallas_call x1, Pallas kernels, second_half(): pl.pallas_call(partial(second_kernel, fsdp_count), out_shape=(shape((2, 2...  81.1 us
    pallas_call x1, Pallas kernels, place(): pl.pallas_call(place_kernel, out_shape=(shape((row_count, width), bf16),...  7.08 us

profile of v4, /device:TPU:0, one launch (start us, length us, event | category | flops | bytes accessed | tf_op | source)
XLA Modules:
  0.0 189.3 jit_solution(1915435425597316180)
XLA Ops:
  0.7 100.3 %first_half.1 = (bf16[640,384]{1,0:T(8,128)(2,1)}, bf16[1408,384]{1,0:T(8,128)(2,1)}, bf16[1408,384]{1,0:T(8,128)(2,1)}, bf16[640,384]{1,0:T(8,128)(2,1)}, bf16[...) custom-call(s32[1,20]{1,0:T(1,128)} %order.3, ...), custom_call_target="tpu_custom_call" | custom-call | tf_op jit(solution)/shard_map/first_half/pallas_call | solution.py:806
  101.0 81.1 %second_half.1 = (bf16[2,160,16,768]{3,2,1,0:T(8,128)(2,1)}, bf16[2,96,768]{2,1,0:T(8,128)(2,1)}, bf16[2,2,192,768]{3,2,1,0:T(8,128)(2,1)}, f32[6,768]{1,0:T(8,128)}, f32[3,768]{1,0:T(4,128)}) custom-call(bf16[640,384]{1,0:T(8,128)(2,1)} %get-tuple-element.51.q_in, bf16[1408,384]{1,0:T(8,128)(2,1)} %get-tuple-element.52.k_in, ...), custom_call_target="tpu_custom_call" | custom-call | tf_op jit(solution)/shard_map/second_half/pallas_call | solution.py:1259
  182.1 7.1 %place.1 = (bf16[1280,768]{1,0:T(8,128)(2,1)}, f32[1280,768]{1,0:T(8,128)}, f32[768]{0:T(1024)}, f32[768]{0:T(1024)}, f32[3,192,192]{2,1,0:T(8,128)}, /*index=5*...) custom-call(s32[1,20]{1,0:T(1,128)} %order.3, ...), custom_call_target="tpu_custom_call" | custom-call | tf_op jit(solution)/shard_map/place/pallas_call | solution.py:1377

commit v5 on v4

--- a/solution.py
+++ b/solution.py
@@ -363,8 +363,10 @@
         return copy
 
     def got(self, copy):
-        copy.wait_recv()
-        self.open = [entry for entry in self.open if entry[0] is not copy]
+        left = [entry for entry in self.open if entry[0] is not copy]
+        if len(left) < len(self.open):
+            copy.wait_recv()
+        self.open = left
 
     def got_from(self, device):
         for copy, to in self.open:
@@ -413,7 +415,9 @@
 def first_kernel(
     fsdp_count, order, patches, grads, attn_proj, out_proj, up, d_own, up_bias, attn_bias, gain1, shift1, gain2, shift2, out_bias, down_bias,
     q_out, k_out, v_out, att_out, low_out, x_out, wh_out, g_up_out, g_down_out,
-    lse, da, middle_grad, mlp_own, mlp_send, g_out_own, g_out_send, stats, up_stats,
+    middle_grad_out, mlp_own_out, mlp_send_out, g_out_own_out, g_out_send_out,
+    lse, da, stats, up_stats,
+    middle_grad, mlp_own, mlp_send, g_out_own, g_out_send,
     where, a_own, bias, rows_all, grads_all, wa, wh, wo_x, wu, wd, bias_all,
     low_all, low, low_own, x_own, g_own, q, k, v, vt, attended, att_t, att_x, st, pt,
     middle, normed, inverse, low2, hidden, pre_grad, second, second_send, second_x, branch, da_send, g_up, g_down, g_sum,
@@ -438,6 +442,32 @@
     keep(grads, grads_all.at[pl.ds(units * c, units)])
     keep(up, wu.at[core, ds(deep * f, deep)])
     keep(d_own, wd.at[core, ds(deep * f, deep)])
+    greet([me.core, me.xp, me.yp] + me.z)
+    post = Post(ss, rs)
+    there = units * (1 - c)
+    half = deep // 2
+    strip, other_strip = half * c, half * (1 - c)
+
+    def quarter(array, index, piece, count):
+        size = part // count
+        return array.at[pl.ds(there + part * index + size * piece, size)]
+
+    def to_y(src, dst, piece, count):
+        size = part // count
+        return post.send(
+            src.at[pl.ds(part * t + size * piece, size)],
+            dst.at[pl.ds(units * c + part * t + size * piece, size)],
+            me.yp,
+        )
+
+    def relay(piece, device):
+        return post.send(piece, piece, device)
+
+    third = deep // 3
+    lone, other_lone = 2 * third * c, 2 * third * (1 - c)
+    a_part = lambda source, row, count: wa.at[core, ds(deep * source + row, count)]
+    pieces = 4
+    patches_y = [to_y(patches, rows_all, i, pieces) for i in range(pieces)]
     a_own[:, 0:128] = attn_proj[0, :, 0:128]
     a_own[:, 128:256] = attn_proj[1, :, 0:128]
     a_own[:, 256:384] = attn_proj[2, :, 0:128]
@@ -448,40 +478,7 @@
     bias[...] = jnp.zeros_like(bias)
     bias[0:1, :] = wide(up_bias)
     bias[1:3, 0:head_width] = attn_bias[...]
-    greet([me.core, me.xp, me.yp] + me.z)
-    post = Post(ss, rs)
-    there = units * (1 - c)
-    half = deep // 2
-    strip, other_strip = half * c, half * (1 - c)
-
-    def quarter(array, index, piece, count):
-        size = part // count
-        return array.at[pl.ds(there + part * index + size * piece, size)]
-
-    def to_y(src, dst, piece, count):
-        size = part // count
-        return post.send(
-            src.at[pl.ds(part * t + size * piece, size)],
-            dst.at[pl.ds(units * c + part * t + size * piece, size)],
-            me.yp,
-        )
-
-    def relay(piece, device):
-        return post.send(piece, piece, device)
-
-    part_rows = half // 2
-    a_part = lambda source, row, count: wa.at[core, ds(deep * source + row, count)]
-    pieces = 4
-    patches_y = [to_y(patches, rows_all, i, pieces) for i in range(pieces)]
-    a_z = [
-        [
-            post.send(
-                a_own.at[ds(strip + part_rows * i, part_rows)], a_part(f, strip + part_rows * i, part_rows), device
-            )
-            for device in me.z
-        ]
-        for i in range(2)
-    ]
+    a_z = [post.send(a_own.at[ds(lone, third)], a_part(f, lone, third), device) for device in me.z]
     post.send(a_own, wa.at[core, ds(deep * f, deep)], me.core)
     post.send(bias, bias_all.at[core], me.core)
     gain_row, shift_row = wide(gain1), wide(shift1)
@@ -522,18 +519,16 @@
         patches_x.append(relay(quarter(rows_all, t, i, pieces), me.xp))
         patches_core.append(relay(quarter(rows_all, t, i, pieces), me.core))
         norm_units(there + part * t + size * i, size)
+        if i == 2:
+            a_y = []
+            for copy, source in zip(a_z, me.back):
+                post.got(copy)
+                a_y.append(relay(a_part(source, lone, third), me.yp))
+                relay(a_part(source, lone, third), me.core)
+            a_shared = [
+                post.send(a_own.at[ds(third, third)], a_part(f, third, third), device) for device in me.z
+            ]
         norm_own(own_blocks - pieces + i, 0)
-    a_y = []
-    for i in range(2):
-        for copy, source in zip(a_z[i], me.back):
-            post.got(copy)
-            piece = a_part(source, strip + part_rows * i, part_rows)
-            a_y.append(relay(piece, me.yp))
-            relay(piece, me.core)
-    grads_y = [to_y(grads, grads_all, i, 2) for i in range(2)]
-    u_z = [
-        post.send(up.at[ds(strip, half)], wu.at[core, ds(deep * f + strip, half)], device) for device in me.z
-    ]
     post.send(up, wu.at[core, ds(deep * f, deep)], me.core)
     post.send(d_own, wd.at[core, ds(deep * f, deep)], me.core)
     for i in range(pieces):
@@ -544,10 +539,16 @@
         post.got(patches_x[i])
         patches_core.append(relay(quarter(rows_all, over, i, pieces), me.core))
         norm_units(there + part * over + size * i, size)
-    for index, copy in enumerate(a_y):
+    for copy, source in zip(a_shared, me.back):
         post.got(copy)
-        source, i = me.back[index % len(me.back)], index // len(me.back)
-        relay(a_part(source, other_strip + part_rows * i, part_rows), me.core)
+        relay(a_part(source, third, third), me.core)
+    u_z = [
+        post.send(up.at[ds(strip, half)], wu.at[core, ds(deep * f + strip, half)], device) for device in me.z
+    ]
+    for copy, source in zip(a_y, me.back):
+        post.got(copy)
+        relay(a_part(source, other_lone, third), me.core)
+    grads_y = [to_y(grads, grads_all, i, 2) for i in range(2)]
     for i in range(pieces):
         post.got(patches_core[i])
         norm_units(there + part * across + size * i, size)
@@ -580,7 +581,8 @@
 
     for i in range(4):
         assemble(i)
-    wo_rows = ds(width // 2 * core, width // 2)
+    wo_quarter = width // 4
+    wo_rows = ds(wo_quarter * (2 * c + core), wo_quarter)
     wo_copy = post.send(wh.at[3, wo_rows], wo_x.at[wo_rows], me.xp)
     keep(wh, wh_out)
 
@@ -670,27 +672,30 @@
             post.got(copy)
             relay(array.at[core, ds(deep * source + other_strip, half)], me.core)
 
+    d_part = lambda source, row: wd.at[core, ds(deep * source + row, third)]
+    post.got(wo_copy)
+    wo_y = relay(wo_x.at[wo_rows], me.yp)
+    wo_core = [relay(wo_x.at[wo_rows], me.core)]
     grads_x = [grads_on(0)]
-    u_y = strips_on(u_z, wu)
-    d_z = [
-        post.send(d_own.at[ds(strip, half)], wd.at[core, ds(deep * f + strip, half)], device) for device in me.z
-    ]
     slab_heads(0)
     grads_x.append(grads_on(1))
     slab_heads(1)
-    post.got(wo_copy)
-    relay(wo_x.at[wo_rows], me.core)
+    u_y = strips_on(u_z, wu)
+    d_lone = [post.send(d_own.at[ds(lone, third)], d_part(f, lone), device) for device in me.z]
+    post.got(wo_y)
+    wo_core.append(relay(wo_x.at[ds(wo_quarter * (2 * (1 - c) + core), wo_quarter)], me.core))
     slab_heads(2)
     keep(attended, att_out)
     middle[...] = (
         x_own[here_rows, :].astype(f32) + wide(out_bias) + dot_nt(attended[here_rows, :], wh[3])
     )
-    for i in range(2):
-        post.got(grads_x[i])
-        relay(quarter(grads_all, over, i, 2), me.core)
-    strips_in(u_y, wu)
-    post.got_from(me.core)
-    for copy in att_copies:
+    d_y = []
+    for copy, source in zip(d_lone, me.back):
+        post.got(copy)
+        d_y.append(relay(d_part(source, lone), me.yp))
+        relay(d_part(source, lone), me.core)
+    d_shared = [post.send(d_own.at[ds(third, third)], d_part(f, third), device) for device in me.z]
+    for copy in wo_core + att_copies:
         post.got(copy)
     middle[...] += dot_nt(att_x[...], wo_x[...])
     n2, s2 = row_norm(middle[...])
@@ -701,62 +706,79 @@
     here_chunks = [ds(mine + chunk * i, chunk) for i in range(2)]
     far_chunks = [ds(far + chunk * i, chunk) for i in range(2)]
     low_copies = [post.send(low2.at[rows], low2.at[rows], me.xp) for rows in here_chunks]
-    own_copies[1].wait()
+    for i in range(2):
+        post.got(grads_x[i])
+        relay(quarter(grads_all, over, i, 2), me.core)
+    strips_in(u_y, wu)
+    for copy in own_copies[1:4]:
+        copy.wait()
+    post.got_from(me.core)
     for j, place in enumerate(places):
         g_own[pl.ds(j * BLOCK, BLOCK), :] = block_of(grads_all, place)
-    d_y = strips_on(d_z, wd)
-    own_copies[2].wait()
-    own_copies[3].wait()
-    strips_in(d_y, wd)
-    post.got_from(me.core)
     tile = 256
 
-    def feed(rows, count):
-        second[rows, :] = jnp.zeros((count, width), f32)
-
-        def step(j, carried):
+    def tiles(step):
+        def tile_step(j, carried):
             shard, lanes = j // 3, pl.ds(pl.multiple_of(j % 3 * tile, 128), tile)
-            out = pl.ds(pl.multiple_of(j * tile, 128), tile)
+            step(shard, lanes, pl.ds(pl.multiple_of(j * tile, 128), tile))
+            return carried
+
+        lax.fori_loop(0, 6, tile_step, 0)
+
+    def forward(rows):
+        def step(shard, lanes, out):
             pre = dot_nn(low2[rows, :], wu[shard, :, lanes]) + bias_all[shard, 0:1, lanes]
             below = 0.5 * (1.0 + lax.erf(pre * (2.0**-0.5)))
             density = jnp.exp(-0.5 * pre * pre) * (2.0 * jnp.pi) ** -0.5
             hidden[rows, out] = (pre * below).astype(bf16)
+            pre_grad[rows, out] = (below + pre * density).astype(bf16)
+
+        tiles(step)
+
+    def backward(rows, count):
+        second[rows, :] = jnp.zeros((count, width), f32)
+
+        def step(shard, lanes, out):
             back = dot_nn(g_own[rows, :], wd[shard, :, lanes])
-            low_back = (back * (below + pre * density)).astype(bf16)
+            low_back = (back * pre_grad[rows, out].astype(f32)).astype(bf16)
             pre_grad[rows, out] = low_back
             second[rows, :] += dot_nt(low_back, wu[shard, :, lanes])
-            return carried
-
-        lax.fori_loop(0, 6, step, 0)
+
+        tiles(step)
 
     def mlp(rows):
         return dot_nt(hidden[rows, 0:width], wd[0]) + dot_nt(hidden[rows, width:], wd[1])
 
+    own_lanes, sibling_lanes = (
+        pl.ds(pl.multiple_of(width * side, 128), width) for side in (core, 1 - core)
+    )
+    sibling_copies = {}
+
+    def weight_grad(index, left, right, grad):
+        def step(shard, lanes, out):
+            grad[:, out] = dot_tn(left[...], right[:, out]).astype(bf16)
+
+        tiles(step)
+        sibling_copies[index] = post.send(grad.at[:, sibling_lanes], g_sum.at[index], me.core)
+
+    forward(here_rows)
+    for i in range(2):
+        post.got(low_copies[i])
+        forward(far_chunks[i])
+    weight_grad(1, g_own, hidden, g_down)
+    for copies, row in ((d_shared, third), (d_y, other_lone)):
+        for copy, source in zip(copies, me.back):
+            post.got(copy)
+            relay(d_part(source, row), me.core)
+    post.got_from(me.core)
     second_copies = []
     for i in range(2):
-        post.got(low_copies[i])
-        feed(far_chunks[i], chunk)
+        backward(far_chunks[i], chunk)
         second_send[i] = second[far_chunks[i], :].astype(bf16)
         second_copies.append(post.send(second_send.at[i], second_x.at[i], me.xp))
-    feed(here_rows, HALF)
-
-    own_lanes, sibling_lanes = (
-        pl.ds(pl.multiple_of(width * side, 128), width) for side in (core, 1 - core)
-    )
-    sibling_copies = []
-    for index, (left, right, grad) in enumerate(((low2, pre_grad, g_up), (g_own, hidden, g_down))):
-
-        def weight_step(j, carried):
-            lanes = pl.ds(pl.multiple_of(j * tile, 128), tile)
-            grad[:, lanes] = dot_tn(left[...], right[:, lanes]).astype(bf16)
-            return carried
-
-        lax.fori_loop(0, 6, weight_step, 0)
-        sibling_copies.append(post.send(grad.at[:, sibling_lanes], g_sum.at[index], me.core))
-    up_stats[0:1, :] = jnp.sum(pre_grad[:, 0:width].astype(f32), axis=0, keepdims=True)
-    up_stats[1:2, :] = jnp.sum(pre_grad[:, width:].astype(f32), axis=0, keepdims=True)
-    mlp_send[...] = mlp(far_rows).astype(bf16)
-    mlp_own[...] = middle[...] + mlp(here_rows) + wide(down_bias)
+    backward(here_rows, HALF)
+
+    weight_grad(0, low2, pre_grad, g_up)
     total = [jnp.zeros((1, width), f32)] * 4
     for i in range(2):
         rows = here_chunks[i]
@@ -775,9 +797,17 @@
         total = [a + jnp.sum(b, axis=0, keepdims=True) for a, b in zip(total, terms)]
     for i in range(4):
         stats[i : i + 1, :] = total[i]
+    up_stats[0:1, :] = jnp.sum(pre_grad[:, 0:width].astype(f32), axis=0, keepdims=True)
+    up_stats[1:2, :] = jnp.sum(pre_grad[:, width:].astype(f32), axis=0, keepdims=True)
+    mlp_send[...] = mlp(far_rows).astype(bf16)
+    mlp_own[...] = middle[...] + mlp(here_rows) + wide(down_bias)
+    for src, out in ((middle_grad, middle_grad_out), (mlp_own, mlp_own_out), (mlp_send, mlp_send_out)):
+        keep(src, out)
     da[here_rows, :] = dot_nn(branch[...], wh[3]).astype(bf16)
     g_out_send[...] = dot_tn(branch[...], att_x[...]).astype(bf16)
     g_out_own[...] = dot_tn(branch[...], attended[here_rows, :]).astype(bf16)
+    keep(g_out_send, g_out_send_out)
+    keep(g_out_own, g_out_own_out)
     for index, (grad, out) in enumerate(((g_up, g_up_out), (g_down, g_down_out))):
         post.got(sibling_copies[index])
 
@@ -815,19 +845,24 @@
             shape((4, width, 384), bf16),
             shape((width, width), bf16),
             shape((width, width), bf16),
-            shape((8, OWN), f32),
-            shape((OWN, 384), bf16),
             shape((HALF, width), f32),
             shape((HALF, width), f32),
             shape((HALF, width), bf16),
             shape((width, 384), bf16),
             shape((width, 384), bf16),
+            shape((8, OWN), f32),
+            shape((OWN, 384), bf16),
             shape((4, width), f32),
             shape((2, width), f32),
         ),
         in_specs=[SMEM, ANY, ANY, VMEM, VMEM, ANY, ANY] + [VMEM] * 8,
-        out_specs=(ANY,) * 9 + (VMEM,) * 9,
+        out_specs=(ANY,) * 14 + (VMEM,) * 4,
         scratch_shapes=[
+            vmem((HALF, width), f32),
+            vmem((HALF, width), f32),
+            vmem((HALF, width), bf16),
+            vmem((width, 384), bf16),
+            vmem((width, 384), bf16),
             pltpu.SMEM(order.shape[1:], jnp.int32),
             vmem((deep, width), bf16),
             vmem((8, width), f32),
@@ -867,7 +902,7 @@
             vmem((width, units), bf16),
             vmem((width, units), bf16),
             vmem((2, width, width), bf16),
-            pltpu.SemaphoreType.DMA((16,)),
+            pltpu.SemaphoreType.DMA((24,)),
             pltpu.SemaphoreType.DMA((112,)),
             pltpu.SemaphoreType.DMA((112,)),
         ],
@@ -953,9 +988,9 @@
 
 def second_kernel(
     fsdp_count, q_in, k_in, v_in, att_in, low_in, x_in, wh_in, g_up, g_down,
-    lse, da, middle_grad, mlp_own, mlp_send, g_out_own, g_out_send, mid_stats, up_stats, gain1,
+    middle_grad_in, mlp_own_in, mlp_send, g_out_own_in, g_out_send_in, lse, da, mid_stats, up_stats, gain1,
     rows_out, up_out, rest_out, all_total, part_total,
-    q, k, v, kt, attended, low_own, x_own, wh, up_own, down_own,
+    middle_grad, mlp_own, g_out_own, g_out_send, q, k, v, kt, attended, low_own, x_own, wh, up_own, down_own,
     delta, st, dpt, pt, dst, dk_acc, dv_acc, dq_t, dq, own_first, trunk, trunk_own, trunk_far, trunk_send, trunk_y, dkv_own,
     mlp_x, first_send, first_x, rows_own, out_core, out_sum, out_x, packed,
     from_core, from_y, from_z, done, deep_z, deep_done, stat_buf, stat_in, stat_z, local, ss, rs,
@@ -971,7 +1006,8 @@
     loads = []
     for src, held in (
         (g_up, up_own), (g_down, down_own), (k_in, k), (q_in, q), (v_in, v), (att_in, attended),
-        (low_in, low_own), (x_in, x_own), (wh_in.at[pl.ds(0, 3)], wh),
+        (g_out_own_in, g_out_own), (g_out_send_in, g_out_send), (mlp_own_in, mlp_own),
+        (low_in, low_own), (x_in, x_own), (middle_grad_in, middle_grad), (wh_in.at[pl.ds(0, 3)], wh),
     ):
         copy = pltpu.make_async_copy(src, held, local.at[len(loads)])
         copy.start()
@@ -988,7 +1024,7 @@
     slab_sibling = pl.ds(pl.multiple_of(128 * (1 - core), 128), 128)
     slab_both = pl.ds(256, 128)
     out_copies = []
-    for i, src in enumerate((g_out_own, g_out_send)):
+    for i, src in enumerate((g_out_own_in, g_out_send_in)):
         for j, lanes in enumerate((slab_sibling, slab_both)):
             out_copies.append(post.send(src.at[:, lanes], out_core.at[i, j], me.core))
     for copy in loads[:2]:
@@ -1079,14 +1115,14 @@
 
     slab_heads(0)
     trunk_out(0)
+    for copy in loads[6:13]:
+        copy.wait()
     for copy in out_copies:
         post.got(copy)
     for i, src in enumerate((g_out_own, g_out_send)):
         for j, lanes in enumerate((slab_own, slab_both)):
             out_sum[i, j] = (src[:, lanes].astype(f32) + out_core[i, j].astype(f32)).astype(bf16)
     out_copy = post.send(out_sum.at[1], out_x, me.xp)
-    for copy in loads[6:]:
-        copy.wait()
     trunk_over(0)
     slab_heads(1)
     trunk_out(1)
@@ -1155,8 +1191,6 @@
     for i in range(2):
         first_send[i] = first(ds(far + chunk * i, chunk)).astype(bf16)
         first_copies.append(post.send(first_send.at[i], first_x.at[i], me.xp))
-    own_first[...] = first(here_rows)
-    post.got(out_copy)
     g_attn = [
         dot_tn(low_own[...], dq[...]),
         dot_tn(low_own[...], dkv_own[:, 0:384]),
@@ -1178,6 +1212,7 @@
     )
     sums[2].from_sibling(packed.at[1 - core])
     def put_out():
+        post.got(out_copy)
         packed[core, :, 384:512] = (out_sum[0, 0].astype(f32) + out_x[0].astype(f32)).astype(bf16)
         last = out_sum[0, 1].astype(f32) + out_x[1].astype(f32)
         side = lax.broadcasted_iota(jnp.int32, last.shape, 1) // HEAD_DIM
@@ -1185,6 +1220,10 @@
         tail = jnp.where(core == 0, turned, last)
         packed[core, :, 640:768] = jnp.where(side == 0, packed[core, :, 640:768].astype(f32), tail).astype(bf16)
 
+    sums[2].add_sibling()
+    put_out()
+    sums[2].over_z_first()
+    own_first[...] = first(here_rows)
     for half in range(2):
         pass_on(0, half)
     n1_all, s1_all = row_norm(x_own[here_rows, :].astype(f32))
@@ -1201,9 +1240,6 @@
         first_total = [
             a + jnp.sum(b, axis=0, keepdims=True) for a, b in zip(first_total, (first_grad * n1, first_grad))
         ]
-    sums[2].add_sibling()
-    put_out()
-    sums[2].over_z_first()
     rows_mid, rows_up = mid_stats.shape[0], up_stats.shape[0]
     stat_buf[0:1, :], stat_buf[1:2, :] = first_total
     stat_buf[2 : 2 + rows_mid, :] = mid_stats[...]
@@ -1243,7 +1279,7 @@
     up_out[...] = done[...]
     rest_out[...] = deep_done[...]
     post.close()
-    for copy in loads[9:]:
+    for copy in loads[13:]:
         copy.wait()
 
 
@@ -1265,9 +1301,13 @@
             shape((6, width), f32),
             shape((3, width), f32),
         ),
-        in_specs=[ANY] * 9 + [VMEM] * 10,
+        in_specs=[ANY] * 14 + [VMEM] * 5,
         out_specs=(ANY,) + (VMEM,) * 4,
         scratch_shapes=[
+            vmem((HALF, width), f32),
+            vmem((HALF, width), f32),
+            vmem((width, 384), bf16),
+            vmem((width, 384), bf16),
             vmem((OWN, 384), bf16),
             vmem((KEYS, 384), bf16),
             vmem((KEYS, 384), bf16),
@@ -1311,7 +1351,7 @@
             vmem((64, width), f32),
             vmem((3, 16, width), f32),
             vmem((fsdp_count, 16, width), f32),
-            pltpu.SemaphoreType.DMA((16,)),
+            pltpu.SemaphoreType.DMA((20,)),
             pltpu.SemaphoreType.DMA((80,)),
             pltpu.SemaphoreType.DMA((80,)),
         ],
@@ -1323,10 +1363,10 @@
 def place_kernel(
     order, rows_all, up_sum, rest, all_total, part_total,
     result, patch_grad, gain1, shift1, grad_attn, attn_bias, grad_out, out_bias, gain2, shift2, grad_up, up_bias,
-    grad_down_t, down_bias, patch_low, sems,
+    grad_down_t, down_bias, result_low, patch_low, patch_wide, sems, out_sems,
 ):
-    own = result.shape[0] // BLOCK
     units = BLOCK // UNIT
+    own = result.shape[0] // units
     core = lax.axis_index("tensor") % 2
     copies = []
     for j in range(own):
@@ -1338,9 +1378,7 @@
             jnp.where(leaf < 0, 5 * branch + 3, 5 * (leaf // 2) + 2 + 2 * (leaf % 2)),
         )
         to = pl.ds(j * units, units)
-        for i, dest in enumerate((result, patch_low)):
-            if i == 0:
-                dest = result.reshape(own * units, UNIT, result.shape[1])
+        for i, dest in enumerate((result_low, patch_low)):
             copy = pltpu.make_async_copy(
                 rows_all.at[i, pl.ds(index * units, units)], dest.at[to], sems.at[i, j]
             )
@@ -1364,9 +1402,18 @@
         grad_attn[i, :, 0:128] = attn[:, 128 * i : 128 * i + 128]
         grad_attn[i, :, 128:192] = tails[i]
     grad_out[...] = jnp.concatenate([attn[:, 384:512], tails[3]], axis=1).T
-    for copy in copies:
+    out = []
+    for j in range(own):
+        block = pl.ds(j * units, units)
+        copies[2 * j].wait()
+        copies[2 * j + 1].wait()
+        patch_wide[block] = patch_low[block].astype(f32)
+        for i, (src, dest) in enumerate(((result_low, result), (patch_wide, patch_grad))):
+            copy = pltpu.make_async_copy(src.at[block], dest.at[block], out_sems.at[i, j])
+            copy.start()
+            out.append(copy)
+    for copy in out:
         copy.wait()
-    patch_grad[...] = patch_low[...].reshape(patch_grad.shape).astype(f32)
 
 
 def place(order, row_count, rows_all, up_sum, rest, all_total, part_total):
@@ -1377,14 +1424,17 @@
     return pl.pallas_call(
         place_kernel,
         out_shape=(
-            shape((row_count, width), bf16), shape((row_count, width), f32), vector, vector,
+            shape((row_count // UNIT, UNIT, width), bf16), shape((row_count // UNIT, UNIT, width), f32), vector, vector,
             shape((3, deep, 192), f32), shape((2, 192), f32), shape((192, deep), f32), vector, vector, vector,
             shape((deep, width), f32), vector, shape((deep, width), f32), vector,
         ),
         in_specs=[SMEM, ANY] + [VMEM] * 4,
-        out_specs=(VMEM,) * 14,
+        out_specs=(ANY,) * 2 + (VMEM,) * 12,
         scratch_shapes=[
             pltpu.VMEM((row_count // UNIT, UNIT, width), bf16),
+            pltpu.VMEM((row_count // UNIT, UNIT, width), bf16),
+            pltpu.VMEM((row_count // UNIT, UNIT, width), f32),
+            pltpu.SemaphoreType.DMA((2, row_count // BLOCK)),
             pltpu.SemaphoreType.DMA((2, row_count // BLOCK)),
         ],
         compiler_params=pltpu.CompilerParams(vmem_limit_bytes=LIMIT),
@@ -1402,6 +1452,7 @@
     )
     sums = second_half(fsdp_count, patches.shape[0], *middle, first_gain)
     outputs = list(place(block_order, patches.shape[0], *sums))
+    outputs[0], outputs[1] = (rows.reshape(patches.shape) for rows in outputs[:2])
     outputs[12] = outputs[12].T
     return tuple(outputs)
 

time: 192 us -> 187 us (0.974); the launches traced: 189 us -> 187 us
  Pallas kernels: 188 us -> 186 us
    pallas_call x1, Pallas kernels: 100 us -> 91.6 us  [first_half(): pl.pallas_call(partial(first_kernel, fsdp_count), out_shape=(shape((OWN,...]
    pallas_call x1, Pallas kernels: 81.1 us -> 87.8 us  [second_half(): pl.pallas_call(partial(second_kernel, fsdp_count), out_shape=(shape((2, 2...]
where the time goes in v5:
time: 187 us
  Pallas kernels  186 us (99%)
    pallas_call x1, Pallas kernels, first_half(): pl.pallas_call(partial(first_kernel, fsdp_count), out_shape=(shape((OWN,...  91.6 us
    pallas_call x1, Pallas kernels, second_half(): pl.pallas_call(partial(second_kernel, fsdp_count), out_shape=(shape((2, 2...  87.8 us
    pallas_call x1, Pallas kernels, place(): pl.pallas_call(place_kernel, out_shape=(shape((row_count // UNIT, UNIT, w...  6.72 us

profile of v5, /device:TPU:0, one launch (start us, length us, event | category | flops | bytes accessed | tf_op | source)
XLA Modules:
  0.0 186.9 jit_solution(6335475400451629423)
XLA Ops:
  0.7 91.6 %first_half.1 = (bf16[640,384]{1,0:T(8,128)(2,1)}, bf16[1408,384]{1,0:T(8,128)(2,1)}, bf16[1408,384]{1,0:T(8,128)(2,1)}, bf16[640,384]{1,0:T(8,128)(2,1)}, bf16[...) custom-call(s32[1,20]{1,0:T(1,128)} %order.3, ...), custom_call_target="tpu_custom_call" | custom-call | tf_op jit(solution)/shard_map/first_half/pallas_call | solution.py:836
  92.2 87.8 %second_half.1 = (bf16[2,160,16,768]{3,2,1,0:T(8,128)(2,1)}, bf16[2,96,768]{2,1,0:T(8,128)(2,1)}, bf16[2,2,192,768]{3,2,1,0:T(8,128)(2,1)}, f32[6,768]{1,0:T(8,128)}, f32[3,768]{1,0:T(4,128)}) custom-call(bf16[640,384]{1,0:T(8,128)(2,1)} %get-tuple-element.51.q_in, bf16[1408,384]{1,0:T(8,128)(2,1)} %get-tuple-element.52.k_in, ...), custom_call_target="tpu_custom_call" | custom-call | tf_op jit(solution)/shard_map/second_half/pallas_call | solution.py:1295
  180.0 6.7 %place.1 = (bf16[80,16,768]{2,1,0:T(8,128)(2,1)}, f32[80,16,768]{2,1,0:T(8,128)}, f32[768]{0:T(1024)}, f32[768]{0:T(1024)}, f32[3,192,192]{2,1,0:T(8,128)}, /*in...) custom-call(s32[1,20]{1,0:T(1,128)} %order.3, ...), custom_call_target="tpu_custom_call" | custom-call | tf_op jit(solution)/shard_map/place/pallas_call | solution.py:1424

commit v6 on v5

--- a/solution.py
+++ b/solution.py
@@ -986,12 +986,15 @@
         self.last = self.post.send(self.done.at[me.c], self.done.at[me.c], me.yp)
 
 
+TALL, WIDE = 256, 256
+
+
 def second_kernel(
     fsdp_count, q_in, k_in, v_in, att_in, low_in, x_in, wh_in, g_up, g_down,
     middle_grad_in, mlp_own_in, mlp_send, g_out_own_in, g_out_send_in, lse, da, mid_stats, up_stats, gain1,
     rows_out, up_out, rest_out, all_total, part_total,
     middle_grad, mlp_own, g_out_own, g_out_send, q, k, v, kt, attended, low_own, x_own, wh, up_own, down_own,
-    delta, st, dpt, pt, dst, dk_acc, dv_acc, dq_t, dq, own_first, trunk, trunk_own, trunk_far, trunk_send, trunk_y, dkv_own,
+    delta, pt, dst, dk_acc, dv_acc, dq_t, dq, own_first, trunk, trunk_own, trunk_far, trunk_send, trunk_y, dkv_own,
     mlp_x, first_send, first_x, rows_own, out_core, out_sum, out_x, packed,
     from_core, from_y, from_z, done, deep_z, deep_done, stat_buf, stat_in, stat_z, local, ss, rs,
 ):
@@ -1045,22 +1048,21 @@
         q_slab, da_slab = q[:, lanes], da[:, lanes]
         q_part = jnp.where(lane == part, q_slab, jnp.zeros_like(q_slab))
         da_part = jnp.where(lane == part, da_slab, jnp.zeros_like(da_slab))
-        st[0:TRUNK, :] = dot_nt(k[0:TRUNK, lanes], q_part)
-        dpt[0:TRUNK, :] = dot_nt(v[0:TRUNK, lanes], da_part)
+        log_total, row_delta = lse[pl.ds(h, 1), :], delta[pl.ds(h, 1), :]
+
+        def tile(keys, rows, cols):
+            scores = dot_nt(k[keys, lanes], q_part[cols])
+            prob_grad = dot_nt(v[keys, lanes], da_part[cols])
+            weight = jnp.exp(scores - log_total[:, cols])
+            pt[rows, cols] = weight.astype(bf16)
+            dst[rows, cols] = (weight * (prob_grad - row_delta[:, cols])).astype(bf16)
+
+        for col in range(0, OWN, WIDE):
+            cols = slice(col, min(col + WIDE, OWN))
+            for row in range(0, TRUNK, TALL):
+                tile(slice(row, row + TALL), slice(row, row + TALL), cols)
         for q_row, k_row, count in PIECES:
-            cols, rows = slice(q_row, q_row + BLOCK), slice(TRUNK, TRUNK + count)
-            st[rows, cols] = dot_nt(k[k_row : k_row + count, lanes], q_part[q_row : q_row + BLOCK])
-            dpt[rows, cols] = dot_nt(v[k_row : k_row + count, lanes], da_part[q_row : q_row + BLOCK])
-        log_total, row_delta = lse[pl.ds(h, 1), :], delta[pl.ds(h, 1), :]
-        for j in range(OWN // BLOCK):
-            cols = slice(j * BLOCK, (j + 1) * BLOCK)
-            count = TRUNK + (0 if j < 2 else PIECES[j - 2][2])
-            for r in range(0, count, BLOCK):
-                weight = jnp.exp(st[r : r + BLOCK, cols] - log_total[:, cols])
-                pt[r : r + BLOCK, cols] = weight.astype(bf16)
-                dst[r : r + BLOCK, cols] = (
-                    weight * (dpt[r : r + BLOCK, cols] - row_delta[:, cols])
-                ).astype(bf16)
+            tile(slice(k_row, k_row + count), slice(TRUNK, TRUNK + count), slice(q_row, q_row + BLOCK))
         dk_acc[0:TRUNK, :] += dot_nn(dst[0:TRUNK, :], q_part)
         dv_acc[0:TRUNK, :] += dot_nn(pt[0:TRUNK, :], da_part)
         head_rows = ds(h * HEAD_DIM, HEAD_DIM)
@@ -1319,8 +1321,6 @@
             vmem((width, width), bf16),
             vmem((width, width), bf16),
             vmem((8, OWN), f32),
-            vmem((tall, OWN), f32),
-            vmem((tall, OWN), f32),
             vmem((tall, OWN), bf16),
             vmem((tall, OWN), bf16),
             vmem((KEYS, 128), f32),

time: 187 us -> 187 us (level)
  no operation moved by 1% of the time
where the time goes in v6:
time: 187 us
  Pallas kernels  186 us (99%)
    pallas_call x1, Pallas kernels, first_half(): pl.pallas_call(partial(first_kernel, fsdp_count), out_shape=(shape((OWN,...  91.6 us
    pallas_call x1, Pallas kernels, second_half(): pl.pallas_call(partial(second_kernel, fsdp_count), out_shape=(shape((2, 2...  87.6 us
    pallas_call x1, Pallas kernels, place(): pl.pallas_call(place_kernel, out_shape=(shape((row_count // UNIT, UNIT, w...  6.72 us

profile of v6, /device:TPU:0, one launch (start us, length us, event | category | flops | bytes accessed | tf_op | source)
XLA Modules:
  0.0 186.7 jit_solution(6461510345390207847)
XLA Ops:
  0.7 91.6 %first_half.1 = (bf16[640,384]{1,0:T(8,128)(2,1)}, bf16[1408,384]{1,0:T(8,128)(2,1)}, bf16[1408,384]{1,0:T(8,128)(2,1)}, bf16[640,384]{1,0:T(8,128)(2,1)}, bf16[...) custom-call(s32[1,20]{1,0:T(1,128)} %order.3, ...), custom_call_target="tpu_custom_call" | custom-call | tf_op jit(solution)/shard_map/first_half/pallas_call | solution.py:836
  92.2 87.6 %second_half.1 = (bf16[2,160,16,768]{3,2,1,0:T(8,128)(2,1)}, bf16[2,96,768]{2,1,0:T(8,128)(2,1)}, bf16[2,2,192,768]{3,2,1,0:T(8,128)(2,1)}, f32[6,768]{1,0:T(8,128)}, f32[3,768]{1,0:T(4,128)}) custom-call(bf16[640,384]{1,0:T(8,128)(2,1)} %get-tuple-element.51.q_in, bf16[1408,384]{1,0:T(8,128)(2,1)} %get-tuple-element.52.k_in, ...), custom_call_target="tpu_custom_call" | custom-call | tf_op jit(solution)/shard_map/second_half/pallas_call | solution.py:1297
  179.8 6.7 %place.1 = (bf16[80,16,768]{2,1,0:T(8,128)(2,1)}, f32[80,16,768]{2,1,0:T(8,128)}, f32[768]{0:T(1024)}, f32[768]{0:T(1024)}, f32[3,192,192]{2,1,0:T(8,128)}, /*in...) custom-call(s32[1,20]{1,0:T(1,128)} %order.3, ...), custom_call_target="tpu_custom_call" | custom-call | tf_op jit(solution)/shard_map/place/pallas_call | solution.py:1424

commit v7 on v6

--- a/solution.py
+++ b/solution.py
@@ -1158,7 +1158,7 @@
         for copies, owner, onward in ((over_x, beside, me.yp), (over_y, beyond, me.xp)):
             post.got(copies[index, half])
             got = piece(index, owner, half)
-            if (half == 0) == (onward is me.yp):
+            if (index == 1 and half == 0) == (onward is me.yp):
                 diagonal[index, half] = post.send(got, got, onward)
             post.send(got, got, me.core)
 

time: 187 us -> 186 us (level)
  Pallas kernels: 186 us -> 184 us
where the time goes in v7:
time: 186 us; the launch traced here: 185 us
  Pallas kernels  184 us (99%)
    pallas_call x1, Pallas kernels, first_half(): pl.pallas_call(partial(first_kernel, fsdp_count), out_shape=(shape((OWN,...  91.6 us
    pallas_call x1, Pallas kernels, second_half(): pl.pallas_call(partial(second_kernel, fsdp_count), out_shape=(shape((2, 2...  86 us
    pallas_call x1, Pallas kernels, place(): pl.pallas_call(place_kernel, out_shape=(shape((row_count // UNIT, UNIT, w...  6.72 us

profile of v7, /device:TPU:0, one launch (start us, length us, event | category | flops | bytes accessed | tf_op | source)
XLA Modules:
  0.0 185.1 jit_solution(9518798554687134595)
XLA Ops:
  0.7 91.6 %first_half.1 = (bf16[640,384]{1,0:T(8,128)(2,1)}, bf16[1408,384]{1,0:T(8,128)(2,1)}, bf16[1408,384]{1,0:T(8,128)(2,1)}, bf16[640,384]{1,0:T(8,128)(2,1)}, bf16[...) custom-call(s32[1,20]{1,0:T(1,128)} %order.3, ...), custom_call_target="tpu_custom_call" | custom-call | tf_op jit(solution)/shard_map/first_half/pallas_call | solution.py:836
  92.2 86.0 %second_half.1 = (bf16[2,160,16,768]{3,2,1,0:T(8,128)(2,1)}, bf16[2,96,768]{2,1,0:T(8,128)(2,1)}, bf16[2,2,192,768]{3,2,1,0:T(8,128)(2,1)}, f32[6,768]{1,0:T(8,128)}, f32[3,768]{1,0:T(4,128)}) custom-call(bf16[640,384]{1,0:T(8,128)(2,1)} %get-tuple-element.51.q_in, bf16[1408,384]{1,0:T(8,128)(2,1)} %get-tuple-element.52.k_in, ...), custom_call_target="tpu_custom_call" | custom-call | tf_op jit(solution)/shard_map/second_half/pallas_call | solution.py:1297
  178.2 6.7 %place.1 = (bf16[80,16,768]{2,1,0:T(8,128)(2,1)}, f32[80,16,768]{2,1,0:T(8,128)}, f32[768]{0:T(1024)}, f32[768]{0:T(1024)}, f32[3,192,192]{2,1,0:T(8,128)}, /*in...) custom-call(s32[1,20]{1,0:T(1,128)} %order.3, ...), custom_call_target="tpu_custom_call" | custom-call | tf_op jit(solution)/shard_map/place/pallas_call | solution.py:1424

commit v8 on v7

--- a/solution.py
+++ b/solution.py
@@ -1176,10 +1176,10 @@
     trunk_out(2)
     dq[...] = (dq_t[...].T * HEAD_DIM ** (-0.5)).astype(bf16)
     trunk_over(2)
+    for slab in range(3):
+        trunk_in(slab)
     for half in range(2):
         spread_y(0, half)
-    for slab in range(3):
-        trunk_in(slab)
 
     def first(rows):
         return (

time: 186 us -> 186 us (level)
  no operation moved by 1% of the time
where the time goes in v8:
time: 186 us; the launch traced here: 185 us
  Pallas kernels  184 us (99%)
    pallas_call x1, Pallas kernels, first_half(): pl.pallas_call(partial(first_kernel, fsdp_count), out_shape=(shape((OWN,...  91.6 us
    pallas_call x1, Pallas kernels, second_half(): pl.pallas_call(partial(second_kernel, fsdp_count), out_shape=(shape((2, 2...  86.1 us
    pallas_call x1, Pallas kernels, place(): pl.pallas_call(place_kernel, out_shape=(shape((row_count // UNIT, UNIT, w...  6.72 us

profile of v8, /device:TPU:0, one launch (start us, length us, event | category | flops | bytes accessed | tf_op | source)
XLA Modules:
  0.0 185.2 jit_solution(12156546847534260744)
XLA Ops:
  0.7 91.6 %first_half.1 = (bf16[640,384]{1,0:T(8,128)(2,1)}, bf16[1408,384]{1,0:T(8,128)(2,1)}, bf16[1408,384]{1,0:T(8,128)(2,1)}, bf16[640,384]{1,0:T(8,128)(2,1)}, bf16[...) custom-call(s32[1,20]{1,0:T(1,128)} %order.3, ...), custom_call_target="tpu_custom_call" | custom-call | tf_op jit(solution)/shard_map/first_half/pallas_call | solution.py:836
  92.2 86.1 %second_half.1 = (bf16[2,160,16,768]{3,2,1,0:T(8,128)(2,1)}, bf16[2,96,768]{2,1,0:T(8,128)(2,1)}, bf16[2,2,192,768]{3,2,1,0:T(8,128)(2,1)}, f32[6,768]{1,0:T(8,128)}, f32[3,768]{1,0:T(4,128)}) custom-call(bf16[640,384]{1,0:T(8,128)(2,1)} %get-tuple-element.51.q_in, bf16[1408,384]{1,0:T(8,128)(2,1)} %get-tuple-element.52.k_in, ...), custom_call_target="tpu_custom_call" | custom-call | tf_op jit(solution)/shard_map/second_half/pallas_call | solution.py:1297
  178.3 6.7 %place.1 = (bf16[80,16,768]{2,1,0:T(8,128)(2,1)}, f32[80,16,768]{2,1,0:T(8,128)}, f32[768]{0:T(1024)}, f32[768]{0:T(1024)}, f32[3,192,192]{2,1,0:T(8,128)}, /*in...) custom-call(s32[1,20]{1,0:T(1,128)} %order.3, ...), custom_call_target="tpu_custom_call" | custom-call | tf_op jit(solution)/shard_map/place/pallas_call | solution.py:1424
